TPU v7x, 32 devices: a whole 2x2x4 slice. The times are simulated.
32 devices in a mesh: gx: 4 (over z), gy: 2 (over y), gz: 4 (over x, core).
Axes of the slice: x: 2, y: 2, z: 4, core: 2. Of those that a mesh axis runs over, the one named last changes fastest.
Arguments:
- right_side: float32 [3, 16, 16, 512], P(None, 'gz', 'gy', 'gx'), may hold values from -5 to 5
- stiff_scale: float32 [16, 16, 512], P('gz', 'gy', 'gx'), may hold values from 0.5 to 2
- nodal_mass: float32 [16, 16, 512], P('gz', 'gy', 'gx'), may hold values from 0.01 to 0.1
- stencil_blocks: float32 [27, 3, 3], replicated, may hold values from -0.5 to 6, as said below
Outputs:
- correction: float32 [3, 16, 16, 512], P(None, 'gz', 'gy', 'gx')
Inputs may be any that keep to these rules, and one draw needn't show every extreme that they name: `stencil_blocks`: every block is symmetric and the block of the opposite offset equals it; the centre block is S plus 0.01 times the diagonal of S, where S is minus the sum of the other 26 blocks.
All inputs are finite; a program needn't handle non-finite values.
Results may differ from a plain program's by a relative error of at most 0.0003.
Values sent between devices are 32-bit elements; how exact they have to be, the bound alone decides.
No kernel may reach another device: no remote copies, remote signals or barrier semaphores. Data moves between devices by JAX's collectives and lax.ppermute only.
A program may use at most 128 MiB of HBM per device.

v0:
```python
import jax
import jax.numpy as jnp
from jax import lax
from jax.sharding import PartitionSpec as P

SMOOTH_DEGREE = 2
COARSE_ITERS = 8


smooth_ratio = 20.0
coarse_ratio = 200.0


def padded_2(cells, sides, width):
    for axis, dim in sides:
        count = lax.axis_size(axis)
        ends = count - 1
        head = lax.slice_in_dim(cells, 0, width, axis=dim)
        tail = lax.slice_in_dim(cells, cells.shape[dim] - width, cells.shape[dim], axis=dim)
        cells = jnp.concatenate(
            [
                lax.ppermute(tail, axis, [(i, (i + 1) % count) for i in range(ends)]),
                cells,
                lax.ppermute(head, axis, [((i + 1) % count, i) for i in range(ends)]),
            ],
            axis=dim,
        )
    return cells


def offset_list():
    return [
        (step_z, step_y, step_x)
        for step_z in (-1, 0, 1)
        for step_y in (-1, 0, 1)
        for step_x in (-1, 0, 1)
    ]


def stencil(padded, kernel):
    extent_z = padded.shape[1] - 2
    extent_y = padded.shape[2] - 2
    extent_x = padded.shape[3] - 2
    summed = None
    for offset_id, (step_z, step_y, step_x) in enumerate(offset_list()):
        portion = padded[
            :,
            1 + step_z : 1 + step_z + extent_z,
            1 + step_y : 1 + step_y + extent_y,
            1 + step_x : 1 + step_x + extent_x,
        ]
        addend = jnp.einsum(
            "ab,bzyx->azyx", kernel[offset_id], portion, precision=lax.Precision.HIGHEST
        )
        summed = addend if summed is None else summed + addend
    return summed


def make_operator(scale, mass, kernel, padder):

    def operate(values):
        weighted = scale[None] * values
        return scale[None] * stencil(padder(weighted), kernel) + mass[None] * values

    return operate


def diagonal_of(scale, mass, kernel):
    centre = jnp.diagonal(kernel[13])
    return centre[:, None, None, None] * (scale * scale)[None] + mass[None]


def ratio_max(scale, mass, kernel, padder):
    spread_scale = jnp.broadcast_to(scale[None], (3,) + scale.shape)
    row_sum = scale[None] * stencil(padder(spread_scale), jnp.abs(kernel)) + mass[None]
    return jnp.max(row_sum / diagonal_of(scale, mass, kernel))


def coarsen(values):
    extent = values.shape
    return values.reshape(extent[0], extent[1] // 2, 2, extent[2] // 2, 2, extent[3] // 2, 2).sum(
        axis=(2, 4, 6)
    )


def refine(values):
    return jnp.repeat(jnp.repeat(jnp.repeat(values, 2, axis=1), 2, axis=2), 2, axis=3)


def chebyshev(
    iterate, residue, degree, inverse_diag, upper_end, range_ratio, operate, keep_residue
):
    lower_end = upper_end / range_ratio
    centre = 0.5 * (upper_end + lower_end)
    spread = 0.5 * (upper_end - lower_end)
    sigma_val = centre / spread
    rho_now = 1.0 / sigma_val
    direction = inverse_diag * residue / centre
    for sweep_id in range(degree):
        iterate = iterate + direction
        if sweep_id < degree - 1 or keep_residue:
            residue = residue - operate(direction)
        if sweep_id < degree - 1:
            rho_next = 1.0 / (2.0 * sigma_val - rho_now)
            direction = (
                rho_next * rho_now * direction + 2.0 * rho_next / spread * inverse_diag * residue
            )
            rho_now = rho_next
    return (iterate, residue)


def cycle(tier_id, source, operators, inverses, bounds, coarse_solve):
    if tier_id == 2:
        return coarse_solve(source)
    operate = operators[tier_id]
    inverse_diag = inverses[tier_id]
    start_zero = jnp.zeros_like(source)
    iterate, residue = chebyshev(
        start_zero,
        source,
        SMOOTH_DEGREE,
        inverse_diag,
        bounds[tier_id],
        smooth_ratio,
        operate,
        True,
    )
    omega_val = 4.0 / 3.0 / bounds[tier_id]
    smoothed = residue - omega_val * operate(inverse_diag * residue)
    coarse = cycle(tier_id + 1, coarsen(smoothed), operators, inverses, bounds, coarse_solve)
    lifted = refine(coarse)
    iterate = iterate + lifted - omega_val * inverse_diag * operate(lifted)
    residue = source - operate(iterate)
    iterate, residue = chebyshev(
        iterate, residue, SMOOTH_DEGREE, inverse_diag, bounds[tier_id], smooth_ratio, operate, False
    )
    return iterate


def fine_pad(values):
    return padded_2(values, (("gx", 3), ("gy", 2), ("gz", 1)), 1)


def mid_pad(values):
    return padded_2(values, (("gx", 3), ("gy", 2), ("gz", 1)), 1)


def coarse_pad(values):
    return padded_2(values, (("gx", 3), ("gy", 2), ("gz", 1)), 1)


def on_device(right_side, stiff_scale, nodal_mass, stencil_blocks):
    scales = [stiff_scale]
    masses = [nodal_mass]
    for tier_id in range(2):
        scales.append(coarsen(scales[-1][None])[0] / 8.0)
        masses.append(coarsen(masses[-1][None])[0])
    kernels = [stencil_blocks, 2.0 * stencil_blocks, 4.0 * stencil_blocks]
    padders = [fine_pad, mid_pad, coarse_pad]
    operators = [
        make_operator(scales[tier_id], masses[tier_id], kernels[tier_id], padders[tier_id])
        for tier_id in range(3)
    ]
    inverses = [
        1.0 / diagonal_of(scales[tier_id], masses[tier_id], kernels[tier_id])
        for tier_id in range(3)
    ]
    ratio_fine = ratio_max(scales[0], masses[0], kernels[0], fine_pad)
    ratio_mid = ratio_max(scales[1], masses[1], kernels[1], mid_pad)
    ratio_coarse = ratio_max(scales[2], masses[2], kernels[2], coarse_pad)
    bounds = lax.pmax((ratio_fine, ratio_mid, ratio_coarse), ("gx", "gy", "gz"))

    def coarse_solve(source):
        iterate, residue = chebyshev(
            jnp.zeros_like(source),
            source,
            COARSE_ITERS,
            inverses[2],
            bounds[2],
            coarse_ratio,
            operators[2],
            False,
        )
        return iterate

    result = cycle(0, right_side, operators, inverses, bounds, coarse_solve)
    return result


def solution(mesh):
    placed = (P(None, "gz", "gy", "gx"), P("gz", "gy", "gx"), P("gz", "gy", "gx"), P())
    return jax.shard_map(
        on_device, mesh=mesh, in_specs=placed, out_specs=P(None, "gz", "gy", "gx"), check_vma=False
    )
```

profile of v0, /device:TPU:26, one launch (start us, length us, event | category | flops | bytes accessed | tf_op | source)
XLA Modules:
  0.0 705.5 jit_solution(9060346961243448020)
XLA Ops:
  8.4 5.2 collective-permute-start.1
  30.7 4.2 collective-permute-done.48
  36.3 4.5 collective-permute-start.50
  42.5 4.5 collective-permute-start.26
  48.8 4.5 collective-permute-start.2
  91.4 38.8 %all-reduce = (f32[]{:T(128)}, f32[]{:T(128)}, f32[]{:T(128)}) all-reduce(f32[]{:T(128)} %fusion.568, f32[]{:T(128)} %fusion.567, f32[]{:T(128)} %fusion.569), channel_id=1, replica_groups=mesh['gx'=4,'gy'=2,'gz'=4] {'gx','gy','gz'}, use_global_device_ids=true, to_apply=%region_6.7 | all-reduce | flops 3 | bytes 24 | tf_op jit(solution)/shard_map/pmax | solution.py:171
  143.7 4.3 collective-permute-done.6
  209.2 4.3 collective-permute-done.18
  245.2 4.2 collective-permute-done.30
  250.8 4.5 collective-permute-start.32
  281.8 4.2 collective-permute-done.36
  287.3 4.5 collective-permute-start.38
  316.0 4.2 collective-permute-done.42
  321.6 4.5 collective-permute-start.44
  344.5 4.2 collective-permute-done.54
  350.1 4.5 collective-permute-start.56
  370.9 4.2 collective-permute-done.60
  376.4 4.5 collective-permute-start.62
  397.2 4.2 collective-permute-done.66
  402.7 4.5 collective-permute-start.68
  429.0 4.5 collective-permute-start.74
  455.3 4.5 collective-permute-start.80
  481.7 4.5 collective-permute-start.86
  508.0 4.5 collective-permute-start.92
  529.2 4.2 collective-permute-done.96
  534.7 4.5 collective-permute-start.98
  556.7 4.2 collective-permute-done.102
  562.3 4.5 collective-permute-start.104
  584.2 4.2 collective-permute-done.108
  589.8 4.5 collective-permute-start.110
  646.8 4.3 collective-permute-done.120
  677.7 4.3 collective-permute-done.126
  (1271 shorter events, 515.6 us)
Async XLA Ops:
  2.2 34.1 %collective-permute-start.25 = (f32[3,2,4,1]{3,0,2,1:T(4,128)S(1)}, f32[3,2,4,1]{3,0,2,1:T(4,128)S(1)}, u32[]{:S(2)}, u32[]{:S(2)}) collective-permute-start(f32[3,2,4,1]{3,0,2,1:T(4,128)S(1)} %mul.925), channel_id=1, source_target_pairs={{8,0},{16,8},{24,16},{9,1},{17,9},{25,17},{10,2},{18,10},{26,18},{... | collective-permute-start | bytes 296 | tf_op jit(solution)/shard_map/ppermute | solution.py:24
  4.6 36.2 %collective-permute-start.24 = (f32[3,2,4,1]{3,0,2,1:T(4,128)S(1)}, f32[3,2,4,1]{3,0,2,1:T(4,128)S(1)}, u32[]{:S(2)}, u32[]{:S(2)}) collective-permute-start(f32[3,2,4,1]{3,0,2,1:T(4,128)S(1)} %mul.924), channel_id=1, source_target_pairs={{0,8},{8,16},{16,24},{1,9},{9,17},{17,25},{2,10},{10,18},{18,26},{... | collective-permute-start | bytes 296 | tf_op jit(solution)/shard_map/ppermute | solution.py:22
  7.0 35.5 %collective-permute-start = (f32[3,4,8,1]{3,0,2,1:T(4,128)S(1)}, f32[3,4,8,1]{3,0,2,1:T(4,128)S(1)}, u32[]{:S(2)}, u32[]{:S(2)}) collective-permute-start(f32[3,4,8,1]{3,0,2,1:T(4,128)S(1)} %mul.891), channel_id=1, source_target_pairs={{0,8},{8,16},{16,24},{1,9},{9,17},{17,25},{2,10},{10,18},{18,26},{... | collective-permute-start | bytes 1160 | tf_op jit(solution)/shard_map/ppermute | solution.py:22
  8.4 38.7 %collective-permute-start.1 = (f32[3,4,8,1]{3,0,2,1:T(4,128)S(1)}, f32[3,4,8,1]{3,0,2,1:T(4,128)S(1)}, u32[]{:S(2)}, u32[]{:S(2)}) collective-permute-start(f32[3,4,8,1]{3,0,2,1:T(4,128)S(1)} %mul.892), channel_id=1, source_target_pairs={{8,0},{16,8},{24,16},{9,1},{17,9},{25,17},{10,2},{18,10},{26,18},{... | collective-permute-start | bytes 1160 | tf_op jit(solution)/shard_map/ppermute | solution.py:24
  14.0 15.3 %collective-permute-start.49 = (f32[3,1,2,1]{3,0,2,1:T(4,128)S(1)}, f32[3,1,2,1]{3,0,2,1:T(4,128)S(1)}, u32[]{:S(2)}, u32[]{:S(2)}) collective-permute-start(f32[3,1,2,1]{3,0,2,1:T(4,128)S(1)} %mul.959), channel_id=1, source_target_pairs={{8,0},{16,8},{24,16},{9,1},{17,9},{25,17},{10,2},{18,10},{26,18},{... | collective-permute-start | bytes 80 | tf_op jit(solution)/shard_map/ppermute | solution.py:24
  35.0 13.8 %collective-permute-start.51 = (f32[3,1,1,34]{3,0,2,1:T(4,128)S(1)}, f32[3,1,1,34]{3,0,2,1:T(4,128)S(1)}, u32[]{:S(2)}, u32[]{:S(2)}) collective-permute-start(f32[3,1,1,34]{3,0,2,1:T(4,128)S(1)} %get-tuple-element.372), channel_id=1, source_target_pairs={{4,0},{5,1},{6,2},{7,3},{12,8},{13,9},{14,10},{15,11},{20,16},{21,... | collective-permute-start | bytes 1232 | tf_op jit(solution)/shard_map/ppermute | solution.py:24
  36.3 17.1 %collective-permute-start.50 = (f32[3,1,1,34]{3,0,2,1:T(4,128)S(1)}, f32[3,1,1,34]{3,0,2,1:T(4,128)S(1)}, u32[]{:S(2)}, u32[]{:S(2)}) collective-permute-start(f32[3,1,1,34]{3,0,2,1:T(4,128)S(1)} %get-tuple-element.371), channel_id=1, source_target_pairs={{0,4},{1,5},{2,6},{3,7},{8,12},{9,13},{10,14},{11,15},{16,20},{17,... | collective-permute-start | bytes 1232 | tf_op jit(solution)/shard_map/ppermute | solution.py:22
  41.0 14.8 %collective-permute-start.27 = (f32[3,2,1,66]{3,0,2,1:T(4,128)S(1)}, f32[3,2,1,66]{3,0,2,1:T(4,128)S(1)}, u32[]{:S(2)}, u32[]{:S(2)}) collective-permute-start(f32[3,2,1,66]{3,0,2,1:T(4,128)S(1)} %get-tuple-element.295), channel_id=1, source_target_pairs={{4,0},{5,1},{6,2},{7,3},{12,8},{13,9},{14,10},{15,11},{20,16},{21,... | collective-permute-start | bytes 4760 | tf_op jit(solution)/shard_map/ppermute | solution.py:24
  42.5 15.6 %collective-permute-start.26 = (f32[3,2,1,66]{3,0,2,1:T(4,128)S(1)}, f32[3,2,1,66]{3,0,2,1:T(4,128)S(1)}, u32[]{:S(2)}, u32[]{:S(2)}) collective-permute-start(f32[3,2,1,66]{3,0,2,1:T(4,128)S(1)} %get-tuple-element.294), channel_id=1, source_target_pairs={{0,4},{1,5},{2,6},{3,7},{8,12},{9,13},{10,14},{11,15},{16,20},{17,... | collective-permute-start | bytes 4760 | tf_op jit(solution)/shard_map/ppermute | solution.py:22
  47.2 28.0 %collective-permute-start.3 = (f32[3,4,1,130]{3,0,2,1:T(4,128)S(1)}, f32[3,4,1,130]{3,0,2,1:T(4,128)S(1)}, u32[]{:S(2)}, u32[]{:S(2)}) collective-permute-start(f32[3,4,1,130]{3,0,2,1:T(4,128)S(1)} %get-tuple-element.240), channel_id=1, source_target_pairs={{4,0},{5,1},{6,2},{7,3},{12,8},{13,9},{14,10},{15,11},{20,16},{21,... | collective-permute-start | bytes 18728 | tf_op jit(solution)/shard_map/ppermute | solution.py:24
  48.8 26.4 %collective-permute-start.2 = (f32[3,4,1,130]{3,0,2,1:T(4,128)S(1)}, f32[3,4,1,130]{3,0,2,1:T(4,128)S(1)}, u32[]{:S(2)}, u32[]{:S(2)}) collective-permute-start(f32[3,4,1,130]{3,0,2,1:T(4,128)S(1)} %get-tuple-element.241), channel_id=1, source_target_pairs={{0,4},{1,5},{2,6},{3,7},{8,12},{9,13},{10,14},{11,15},{16,20},{17,... | collective-permute-start | bytes 18728 | tf_op jit(solution)/shard_map/ppermute | solution.py:22
  53.5 14.6 %collective-permute-start.53 = (f32[3,1,4,34]{3,0,2,1:T(4,128)S(1)}, f32[3,1,4,34]{3,0,2,1:T(4,128)S(1)}, u32[]{:S(2)}, u32[]{:S(2)}) collective-permute-start(f32[3,1,4,34]{3,0,2,1:T(4,128)S(1)} %pad_maximum_fusion.147), channel_id=1, source_target_pairs={{1,0},{2,1},{3,2},{5,4},{6,5},{7,6},{9,8},{10,9},{11,10},{13,12},{... | collective-permute-start | bytes 4904 | tf_op jit(solution)/shard_map/ppermute | solution.py:24
  58.3 12.2 %collective-permute-start.28 = (f32[3,1,6,66]{3,0,2,1:T(4,128)S(1)}, f32[3,1,6,66]{3,0,2,1:T(4,128)S(1)}, u32[]{:S(2)}, u32[]{:S(2)}) collective-permute-start(f32[3,1,6,66]{3,0,2,1:T(4,128)S(1)} %get-tuple-element.308), channel_id=1, source_target_pairs={{0,1},{1,2},{2,3},{4,5},{5,6},{6,7},{8,9},{9,10},{10,11},{12,13},{... | collective-permute-start | bytes 14264 | tf_op jit(solution)/shard_map/ppermute | solution.py:22
  61.6 8.9 %collective-permute-start.29 = (f32[3,1,6,66]{3,0,2,1:T(4,128)S(1)}, f32[3,1,6,66]{3,0,2,1:T(4,128)S(1)}, u32[]{:S(2)}, u32[]{:S(2)}) collective-permute-start(f32[3,1,6,66]{3,0,2,1:T(4,128)S(1)} %get-tuple-element.309), channel_id=1, source_target_pairs={{1,0},{2,1},{3,2},{5,4},{6,5},{7,6},{9,8},{10,9},{11,10},{13,12},{... | collective-permute-start | bytes 14264 | tf_op jit(solution)/shard_map/ppermute | solution.py:24
  141.8 6.2 collective-permute-start.6
  175.9 6.2 collective-permute-start.12
  207.3 6.2 collective-permute-start.18
  256.7 7.1 %collective-permute-start.34 = (f32[3,1,6,66]{3,0,2,1:T(4,128)S(1)}, f32[3,1,6,66]{3,0,2,1:T(4,128)S(1)}, u32[]{:S(2)}, u32[]{:S(2)}) collective-permute-start(f32[3,1,6,66]{3,0,2,1:T(4,128)S(1)} %get-tuple-element.306), channel_id=1, source_target_pairs={{0,1},{1,2},{2,3},{4,5},{5,6},{6,7},{8,9},{9,10},{10,11},{12,13},{... | collective-permute-start | bytes 14264 | tf_op jit(solution)/shard_map/ppermute | solution.py:22
  286.1 6.7 collective-permute-start.39
  297.8 6.4 collective-permute-start.40
  320.3 6.1 collective-permute-start.45
  356.0 9.8 %collective-permute-start.59 = (f32[3,1,4,34]{3,0,2,1:T(4,128)S(1)}, f32[3,1,4,34]{3,0,2,1:T(4,128)S(1)}, u32[]{:S(2)}, u32[]{:S(2)}) collective-permute-start(f32[3,1,4,34]{3,0,2,1:T(4,128)S(1)} %pad_maximum_fusion.148), channel_id=1, source_target_pairs={{1,0},{2,1},{3,2},{5,4},{6,5},{7,6},{9,8},{10,9},{11,10},{13,12},{... | collective-permute-start | bytes 4904 | tf_op jit(solution)/shard_map/ppermute | solution.py:24
  382.3 9.8 %collective-permute-start.65 = (f32[3,1,4,34]{3,0,2,1:T(4,128)S(1)}, f32[3,1,4,34]{3,0,2,1:T(4,128)S(1)}, u32[]{:S(2)}, u32[]{:S(2)}) collective-permute-start(f32[3,1,4,34]{3,0,2,1:T(4,128)S(1)} %pad_maximum_fusion.149), channel_id=1, source_target_pairs={{1,0},{2,1},{3,2},{5,4},{6,5},{7,6},{9,8},{10,9},{11,10},{13,12},{... | collective-permute-start | bytes 4904 | tf_op jit(solution)/shard_map/ppermute | solution.py:24
  408.7 9.8 %collective-permute-start.71 = (f32[3,1,4,34]{3,0,2,1:T(4,128)S(1)}, f32[3,1,4,34]{3,0,2,1:T(4,128)S(1)}, u32[]{:S(2)}, u32[]{:S(2)}) collective-permute-start(f32[3,1,4,34]{3,0,2,1:T(4,128)S(1)} %pad_maximum_fusion.150), channel_id=1, source_target_pairs={{1,0},{2,1},{3,2},{5,4},{6,5},{7,6},{9,8},{10,9},{11,10},{13,12},{... | collective-permute-start | bytes 4904 | tf_op jit(solution)/shard_map/ppermute | solution.py:24
  435.0 9.8 %collective-permute-start.77 = (f32[3,1,4,34]{3,0,2,1:T(4,128)S(1)}, f32[3,1,4,34]{3,0,2,1:T(4,128)S(1)}, u32[]{:S(2)}, u32[]{:S(2)}) collective-permute-start(f32[3,1,4,34]{3,0,2,1:T(4,128)S(1)} %pad_maximum_fusion.151), channel_id=1, source_target_pairs={{1,0},{2,1},{3,2},{5,4},{6,5},{7,6},{9,8},{10,9},{11,10},{13,12},{... | collective-permute-start | bytes 4904 | tf_op jit(solution)/shard_map/ppermute | solution.py:24
  461.3 9.8 %collective-permute-start.83 = (f32[3,1,4,34]{3,0,2,1:T(4,128)S(1)}, f32[3,1,4,34]{3,0,2,1:T(4,128)S(1)}, u32[]{:S(2)}, u32[]{:S(2)}) collective-permute-start(f32[3,1,4,34]{3,0,2,1:T(4,128)S(1)} %pad_maximum_fusion.152), channel_id=1, source_target_pairs={{1,0},{2,1},{3,2},{5,4},{6,5},{7,6},{9,8},{10,9},{11,10},{13,12},{... | collective-permute-start | bytes 4904 | tf_op jit(solution)/shard_map/ppermute | solution.py:24
  487.6 9.8 %collective-permute-start.89 = (f32[3,1,4,34]{3,0,2,1:T(4,128)S(1)}, f32[3,1,4,34]{3,0,2,1:T(4,128)S(1)}, u32[]{:S(2)}, u32[]{:S(2)}) collective-permute-start(f32[3,1,4,34]{3,0,2,1:T(4,128)S(1)} %pad_maximum_fusion.153), channel_id=1, source_target_pairs={{1,0},{2,1},{3,2},{5,4},{6,5},{7,6},{9,8},{10,9},{11,10},{13,12},{... | collective-permute-start | bytes 4904 | tf_op jit(solution)/shard_map/ppermute | solution.py:24
  513.9 9.8 %collective-permute-start.95 = (f32[3,1,4,34]{3,0,2,1:T(4,128)S(1)}, f32[3,1,4,34]{3,0,2,1:T(4,128)S(1)}, u32[]{:S(2)}, u32[]{:S(2)}) collective-permute-start(f32[3,1,4,34]{3,0,2,1:T(4,128)S(1)} %pad_maximum_fusion.154), channel_id=1, source_target_pairs={{1,0},{2,1},{3,2},{5,4},{6,5},{7,6},{9,8},{10,9},{11,10},{13,12},{... | collective-permute-start | bytes 4904 | tf_op jit(solution)/shard_map/ppermute | solution.py:24
  541.9 6.1 collective-permute-start.100
  611.1 6.2 collective-permute-start.114
  644.9 6.2 collective-permute-start.120
  675.8 6.2 collective-permute-start.126
  (228 other events, 12895.7 us)
where the time goes:
time: 716 us; the launch traced here: 706 us
  starting transfers between devices  301 us (42%)
  waiting for transfers between devices  162 us (23%)
  matrix products  156 us (22%)
  blocking collectives  38.8 us (5%)
  local copies, waits for them, and re-layouts  19.9 us (3%)
  other arithmetic  14.6 us (2%)
  between operations  14.1 us (2%)
    ppermute x66, starting transfers between devices, padded_2(): lax.ppermute(tail, axis, [(i, (i + 1) % count) for i in range(ends)])  167 us
    dot_general x594, matrix products, stencil(): jnp.einsum('ab,bzyx->azyx', kernel[offset_id], portion, precision=lax.Pre...  156 us
    ppermute x66, starting transfers between devices, padded_2(): lax.ppermute(head, axis, [((i + 1) % count, i) for i in range(ends)])  134 us
    ppermute x66, waiting for transfers between devices, padded_2(): lax.ppermute(tail, axis, [(i, (i + 1) % count) for i in range(ends)])  131 us
    pmax x1, blocking collectives, on_device(): bounds = lax.pmax((ratio_fine, ratio_mid, ratio_coarse), ('gx', 'gy', 'gz'))  38.8 us
    ppermute x66, waiting for transfers between devices, padded_2(): lax.ppermute(head, axis, [((i + 1) % count, i) for i in range(ends)])  30.8 us
  transfers between devices with their start and end apart: 132, of which 68 were waited for; matrix products, arithmetic and copies ran while one was open for 8% of the time, Pallas kernels for 0%

commit v1 on v0

v1 whole, which is shorter than its diff:
```python
import functools

import jax
import jax.numpy as jnp
from jax import lax
from jax.experimental import pallas as pl
from jax.experimental.pallas import tpu as pltpu
from jax.sharding import PartitionSpec as P

AXES = ("gx", "gy", "gz")
COARSE_ITERS = 8
SMOOTH_RATIO = 20.0
COARSE_RATIO = 200.0
F32, BF16 = jnp.float32, jnp.bfloat16
PARAMS = pltpu.CompilerParams(vmem_limit_bytes=40 * 1024 * 1024)
VM = pl.BlockSpec(memory_space=pltpu.VMEM)
SM = pl.BlockSpec(memory_space=pltpu.SMEM)
ROWS, LANES = 16, 256
SLAB = 3 * ROWS
GROUP = 3


def call(kernel, outs, specs=None, scratch=(), flops=1000000, size=100000):
    outs = [jax.ShapeDtypeStruct(shape, dtype) for shape, dtype in outs]

    def run(*args):
        return pl.pallas_call(
            kernel,
            out_shape=outs,
            in_specs=specs or [VM] * len(args),
            out_specs=[VM] * len(outs),
            scratch_shapes=scratch,
            compiler_params=PARAMS,
            cost_estimate=pl.CostEstimate(flops=flops, bytes_accessed=size, transcendentals=0),
        )(*args)

    return run


def iota(shape, dim):
    return lax.broadcasted_iota(jnp.int32, shape, dim)


def ones_where(mask):
    return jnp.where(mask, 1.0, 0.0).astype(F32)


def split(values):
    high = values.astype(BF16)
    return high, (values - high.astype(F32)).astype(BF16)


def dot(left, right):
    return jnp.dot(left, right, preferred_element_type=F32)


def dot_select(left, right):
    return jnp.dot(left, right, preferred_element_type=F32, precision=lax.Precision.HIGHEST)


def banded(matrix_high, matrix_low, values):
    high, low = split(values)
    return dot(matrix_high, high) + dot(matrix_low, high) + dot(matrix_high, low)


def shifted_sum(product, slabs, rows, lanes):
    parts = product.reshape(slabs, 3, rows, lanes)
    below = parts[:, 0].reshape(slabs * rows, lanes)
    above = parts[:, 2].reshape(slabs * rows, lanes)
    here = parts[:, 1].reshape(slabs * rows, lanes)
    return here + pltpu.roll(below, 1, 1) + pltpu.roll(above, lanes - 1, 1)


def fine_stencil(matrix, values):
    planes = values.shape[0] - 2
    flat = values.reshape((planes + 2) * SLAB, LANES)
    outs = []
    at = 0
    while at < planes:
        size = min(GROUP, planes - at)
        if planes - at == 4:
            size = 2
        height, depth = size * 3 * SLAB, (size + 2) * SLAB
        product = banded(
            matrix[0, :height, :depth],
            matrix[1, :height, :depth],
            flat[at * SLAB : at * SLAB + depth],
        )
        outs.append(shifted_sum(product, size, SLAB, LANES))
        at += size
    return jnp.concatenate(outs, axis=0).reshape(planes, 3, ROWS, LANES)


def panels(blocks, rows, circular, width):
    column = iota((8, width), 1)
    which = column // rows
    row_in = column % rows
    result = {}
    for step_x in range(3):
        for comp in range(3):
            coeffs = []
            for step_y in range(3):
                coeff = jnp.zeros((8, width), F32)
                for plane in range(3):
                    for other in range(3):
                        value = blocks[(plane * 9 + step_y * 3 + step_x) * 9 + comp * 3 + other]
                        coeff = jnp.where(which == plane * 3 + other, value, coeff)
                coeffs.append(coeff)
            pieces = []
            for block in range(rows // 8):
                gap = row_in - (iota((8, width), 0) + block * 8)
                if circular:
                    gap = jnp.where(gap == rows - 1, -1, jnp.where(gap == 1 - rows, 1, gap))
                piece = jnp.zeros((8, width), F32)
                for step_y in range(3):
                    piece = jnp.where(gap == step_y - 1, coeffs[step_y], piece)
                pieces.append(piece)
            result[step_x, comp] = jnp.concatenate(pieces, axis=0)
    return result


def put(ref, start, value):
    high, low = split(value)
    size = value.shape[0]
    ref[0, start : start + size, :] = high
    ref[1, start : start + size, :] = low


def matrices_kernel(mid_rows, mid_planes, blocks, fine, fine_abs, mid, local_abs):
    found = panels(blocks, ROWS, True, LANES)
    for plane in range(GROUP):
        for step_x in range(3):
            rows = [
                found[step_x, comp] if plane == 0 else pltpu.roll(found[step_x, comp], plane * SLAB, 1)
                for comp in range(3)
            ]
            value = jnp.concatenate(rows, axis=0)
            start = (plane * 3 + step_x) * SLAB
            put(fine, start, value)
            put(fine_abs, start, jnp.abs(value))
    found = panels(blocks, 8, True, 128)
    for plane in range(2):
        for step_x in range(3):
            rows = [
                found[step_x, comp] if plane == 0 else pltpu.roll(found[step_x, comp], plane * 24, 1)
                for comp in range(3)
            ]
            put(local_abs, (plane * 3 + step_x) * 24, jnp.abs(jnp.concatenate(rows, axis=0)))
    slab = 3 * mid_rows
    width = mid.shape[2]
    found = panels(blocks, mid_rows, False, width)
    column = iota((slab, width), 1)
    for plane in range(mid_planes):
        for step_x in range(3):
            value = jnp.concatenate([found[step_x, comp] for comp in range(3)], axis=0)
            if plane == 0:
                value = jnp.where(column < slab, 0.0, value)
            if plane == mid_planes - 1:
                value = jnp.where(column >= 2 * slab, 0.0, value)
            turn = ((plane - 1) * slab) % width
            if turn:
                value = pltpu.roll(value, turn, 1)
            put(mid, (plane * 3 + step_x) * slab, value)


def even_index(axis):
    return lax.rem(lax.axis_index(axis), 2) == 0


def halves(planes, axis, size, low):
    first, second = planes[:10], pltpu.roll(planes[10:], size // 2, axis)
    return jnp.where(low, second, first), jnp.where(low, first, second)


def unhalve(from_above, from_below, axis, size, low):
    first = jnp.where(low, from_above, from_below)
    second = jnp.where(low, pltpu.roll(from_above, size // 2, axis), pltpu.roll(from_below, size // 2, axis))
    return jnp.concatenate([first, second], axis=0)


def neighbours(even, index, count, first, second):
    above = jnp.where(even, first, second)
    below = jnp.where(even, second, first)
    return jnp.where(index < count - 1, above, 0.0), jnp.where(index > 0, below, 0.0)


def pack_x_kernel(source, scale, mass, main, send_a, send_b):
    planes = jnp.concatenate([source[...].reshape(12, 8, 128), scale[...], mass[...]], axis=0)
    main[...] = planes
    high, low = halves(planes, 2, 128, iota((10, 8, 128), 2) < 64)
    even = even_index("gx")
    send_a[...] = jnp.where(even, high, low)
    send_b[...] = jnp.where(even, low, high)


def pack_y_kernel(count, main, got_a, got_b, wide, *sends):
    even = even_index("gx")
    above, below = neighbours(even, lax.axis_index("gx"), count, got_a[...], got_b[...])
    halo = unhalve(above, below, 2, 128, iota((10, 8, 128), 2) < 64)
    wide[:, :, :128] = main[...]
    wide[:, :, 128:] = halo
    planes = wide[...]
    high, low = halves(planes, 1, 8, iota((10, 8, LANES), 1) < 4)
    even = even_index("gy")
    sends[0][...] = jnp.where(even, high, low)
    if len(sends) > 1:
        sends[1][...] = jnp.where(even, low, high)


def pack_z_kernel(count, wide, *refs):
    *gots, whole, send_a, send_b = refs
    even = even_index("gy")
    above, below = neighbours(even, lax.axis_index("gy"), count, gots[0][...], gots[-1][...])
    halo = unhalve(above, below, 1, 8, iota((10, 8, LANES), 1) < 4)
    whole[:, :8, :] = wide[...]
    whole[:, 8:, :] = halo
    planes = whole[...]
    even = even_index("gz")
    for send, up in ((send_a, even), (send_b, jnp.logical_not(even))):
        for slot, field in enumerate((0, 1, 2, 4)):
            send[slot * 3 : slot * 3 + 3] = jnp.where(
                up, planes[field * 4 + 1 : field * 4 + 4], planes[field * 4 : field * 4 + 3]
            )
        send[12:16] = planes[12:16]


def restrict_lanes(width):
    return ones_where(iota((width, 128), 0) // 2 == iota((width, 128), 1))


def inverse_diagonal(scale, mass, blocks, factor):
    square = scale * scale
    parts = []
    for comp in range(3):
        diag = factor * blocks[13 * 9 + comp * 4] * square + mass
        parts.append(jnp.where(scale > 0.0, 1.0 / diag, 0.0)[:, None])
    return jnp.concatenate(parts, axis=1)


def worst_ratio(scale, mass, total, blocks, factor, rows, lanes):
    inverse = inverse_diagonal(scale, mass, blocks, factor)
    ratio = (factor * scale[:, None] * total + mass[:, None]) * inverse
    shape = ratio.shape
    own = jnp.logical_and(iota(shape, 2) < rows, iota(shape, 3) < lanes)
    return jnp.full((8, 128), jnp.max(jnp.where(own, ratio, -jnp.inf)), F32)


def window_kernel(count, blocks, whole, got_a, got_b, fine_abs, local_abs, scale_w, mass_w, source_w, bounds):
    even = even_index("gz")
    above, below = neighbours(even, lax.axis_index("gz"), count, got_a[...], got_b[...])
    planes = whole[...]
    for comp in range(3):
        source_w[0:3, comp] = below[comp * 3 : comp * 3 + 3]
        source_w[3:7, comp] = planes[comp * 4 : comp * 4 + 4]
        source_w[7:10, comp] = above[comp * 3 : comp * 3 + 3]
    mass_w[0:3] = below[9:12]
    mass_w[3:7] = planes[16:20]
    mass_w[7:10] = above[9:12]
    scale_w[0:4] = below[12:16]
    scale_w[4:8] = planes[12:16]
    scale_w[8:12] = above[12:16]

    scale = scale_w[...]
    mass = mass_w[3:7]
    spread = jnp.broadcast_to(scale[3:9][:, None], (6, 3, ROWS, LANES))
    total = fine_stencil(fine_abs, spread)
    bounds[0] = worst_ratio(scale[4:8], mass, total, blocks, 1.0, 8, 128)

    paired = jnp.concatenate(
        [scale.reshape(6, 2, ROWS, LANES).sum(axis=1), mass.reshape(2, 2, ROWS, LANES).sum(axis=1)], axis=0
    )
    squeezed = dot_select(paired.reshape(8 * ROWS, LANES), restrict_lanes(LANES))
    middle = dot_select(ones_where(iota((64, 128), 0) == iota((64, 128), 1) // 2), squeezed).reshape(8, 8, 128)
    scale_1 = middle[:6] * 0.125
    mass_1 = middle[6:]
    spread = jnp.broadcast_to(scale_1[1:5][:, None], (4, 3, 8, 128)).reshape(96, 128)
    product = banded(local_abs[0, :, :96], local_abs[1, :, :96], spread)
    total = shifted_sum(product, 2, 24, 128).reshape(2, 3, 8, 128)
    bounds[1] = worst_ratio(scale_1[2:4], mass_1, total, blocks, 2.0, 4, 64)

    paired = jnp.concatenate([scale_1.reshape(3, 2, 8, 128).sum(axis=1), mass_1.sum(axis=0)[None]], axis=0)
    fold = ones_where(iota((128, 128), 0) // 2 == iota((128, 128), 1) % 64)
    squeezed = dot_select(paired.reshape(32, 128), fold)
    out_row, in_row = iota((32, 32), 0), iota((32, 32), 1)
    same = jnp.logical_and(out_row // 8 == in_row // 8, out_row % 4 == (in_row % 8) // 2)
    coarse = dot_select(ones_where(same), squeezed).reshape(4, 8, 128)
    scale_2 = coarse[:3] * 0.125
    mass_2 = coarse[3:]
    spread = jnp.broadcast_to(scale_2[:, None], (3, 3, 8, 128)).reshape(72, 128)
    product = banded(local_abs[0, :72, :72], local_abs[1, :72, :72], spread)
    total = shifted_sum(product, 1, 24, 128).reshape(1, 3, 8, 128)
    bounds[2] = worst_ratio(scale_2[1:2], mass_2, total, blocks, 4.0, 2, 32)


def fine_operator(matrix, scale, mass, values):
    total = fine_stencil(matrix, scale[:, None] * values)
    return scale[1:-1][:, None] * total + mass[:, None] * values[1:-1]


def power_kernel(blocks, scale_w, mass_w, source_w, fine, power_1):
    scale, mass = scale_w[1:11], mass_w[...]
    inverse = inverse_diagonal(scale, mass, blocks, 1.0)
    power_1[...] = fine_operator(fine, scale, mass[1:9], inverse * source_w[...])


def restrict_kernel(blocks, scale_w, mass_w, source_w, power_1, fine, bounds, *refs):
    *others, power_2, message = refs
    scale, mass = scale_w[2:10], mass_w[1:9]
    inverse = inverse_diagonal(scale, mass, blocks, 1.0)
    second = fine_operator(fine, scale, mass[1:7], inverse * power_1[...])
    power_2[...] = second
    third = fine_operator(fine, scale[1:7], mass[2:6], inverse[1:7] * second)
    fields = []
    for values in (source_w[3:7], power_1[2:6], second[1:5], third):
        pairs = values[:, :, :8].reshape(2, 2, 3, 8, LANES).sum(axis=1)
        fields += [pairs[:, comp] for comp in range(3)]
    for values in (scale[2:6], mass[2:6]):
        fields.append(values[:, :8].reshape(2, 2, 8, LANES).sum(axis=1))
    stacked = jnp.concatenate(fields, axis=0).reshape(224, LANES)
    squeezed = dot_select(stacked, restrict_lanes(LANES))
    pair = ones_where(iota((112, 224), 0) == iota((112, 224), 1) // 2)
    message[0:14] = dot_select(pair, squeezed).reshape(14, 8, 128)
    worst = bounds[...]
    for other in others:
        worst = jnp.maximum(worst, other[...])
    message[14:17] = worst


def chebyshev_scalars(bound, ratio):
    lower = bound / ratio
    return 0.5 * (bound + lower), 0.5 * (bound - lower)


def scaled(coeff, values):
    lanes = values.shape[-1]
    if lanes != 128:
        coeff = jnp.concatenate([coeff] * (lanes // 128), axis=1)
    flat = values.reshape(-1, 8, lanes)
    return (coeff[None] * flat).reshape(values.shape)


def chebyshev(residue, degree, inverse, bound, ratio, operate, keep):
    centre, spread = chebyshev_scalars(bound, ratio)
    sigma = centre / spread
    rho = 1.0 / sigma
    direction = scaled(1.0 / centre, inverse * residue)
    total = direction
    for step in range(degree):
        if step < degree - 1 or keep:
            residue = residue - operate(direction)
        if step < degree - 1:
            rho_next = 1.0 / (2.0 * sigma - rho)
            direction = scaled(rho_next * rho, direction) + scaled(2.0 * rho_next / spread, inverse * residue)
            total = total + direction
            rho = rho_next
    return total, residue


def final_kernel(
    gzs, gys, ordered, blocks, gathered, scale_w, mass_w, source_w, power_1, power_2, fine, mid, result, held, middle, lifted_w
):
    planes, rows = 2 * gzs, 4 * gys
    slab = 3 * rows
    gz, gy = lax.axis_index("gz"), lax.axis_index("gy")
    bounds = jnp.max(gathered[:, 14:17], axis=0)

    centre, spread = chebyshev_scalars(bounds[0], SMOOTH_RATIO)
    sigma = centre / spread
    rho = 1.0 / sigma
    rho_next = 1.0 / (2.0 * sigma - rho)
    keep, push = rho_next * rho, 2.0 * rho_next / spread
    beta = push / centre
    gamma = 1.0 / centre + keep / centre + push
    omega = (4.0 / 3.0) / bounds[0]

    for block in range(gzs * gys):
        part = gathered[block]
        source = (
            part[0:3]
            - (gamma + omega)[None] * part[3:6]
            + (beta + omega * gamma)[None] * part[6:9]
            - (omega * beta)[None] * part[9:12]
        )
        if ordered:
            place_z, place_y = block // gys, block % gys
        else:
            place_z = lax.bitwise_xor(gz, (block // 4) + 2 * (block % 2))
            place_y = lax.bitwise_xor(gy, (block % 4) // 2)
        held[place_z, place_y, 0:3] = source
        held[place_z, place_y, 3] = part[12] * 0.125
        held[place_z, place_y, 4] = part[13]
    first = iota((5, 8, 128), 1) < 4
    for place_z in range(gzs):
        for pair in range(gys // 2):
            low, high = held[place_z, 2 * pair], held[place_z, 2 * pair + 1]
            middle[2 * place_z, :, pair * 8 : pair * 8 + 8] = jnp.where(first, low, pltpu.roll(high, 4, 1))
            middle[2 * place_z + 1, :, pair * 8 : pair * 8 + 8] = jnp.where(first, pltpu.roll(low, 4, 1), high)

    everything = middle[...]
    source_1 = everything[:, :3].reshape(planes * slab, 128)
    scale_1 = everything[:, 3]
    mass_1 = everything[:, 4]
    inverse_1 = inverse_diagonal(scale_1, mass_1, blocks, 2.0).reshape(planes * slab, 128)
    spread_1 = jnp.broadcast_to(scale_1[:, None], (planes, 3, rows, 128)).reshape(planes * slab, 128)
    weight_1 = jnp.broadcast_to(mass_1[:, None], (planes, 3, rows, 128)).reshape(planes * slab, 128)

    def operate_1(values):
        product = banded(mid[0, :, : planes * slab], mid[1, :, : planes * slab], spread_1 * values)
        return 2.0 * spread_1 * shifted_sum(product, planes, slab, 128) + weight_1 * values

    half = planes // 2
    small = half * slab
    out_row, in_row = iota((small, planes * slab), 0), iota((small, planes * slab), 1)
    gather_rows = ones_where(
        jnp.logical_and(
            jnp.logical_and(out_row // slab == in_row // (2 * slab), (out_row % slab) // rows == (in_row % slab) // rows),
            out_row % rows == (in_row % rows) // 2,
        )
    )
    fold = ones_where(iota((128, 128), 0) // 2 == iota((128, 128), 1) % 64)
    column, lane = iota((128, 128), 0), iota((128, 128), 1)
    unfold = ones_where(column == lane // 2)

    def coarsen(values):
        return dot_select(dot_select(gather_rows, values), fold)

    scale_2 = coarsen(spread_1) * 0.125
    mass_2 = coarsen(weight_1)
    inverse_2 = inverse_diagonal(
        scale_2.reshape(half, 3, rows, 128)[:, 0], mass_2.reshape(half, 3, rows, 128)[:, 0], blocks, 4.0
    ).reshape(small, 128)

    def operate_2(values):
        product = banded(mid[0, : small * 3, :small], mid[1, : small * 3, :small], scale_2 * values)
        return 4.0 * scale_2 * shifted_sum(product, half, slab, 128) + mass_2 * values

    omega_1 = (4.0 / 3.0) / bounds[1]
    iterate, residue = chebyshev(source_1, 2, inverse_1, bounds[1], SMOOTH_RATIO, operate_1, True)
    smoothed = residue - scaled(omega_1, operate_1(inverse_1 * residue))
    source_2 = coarsen(smoothed)
    error_2, _ = chebyshev(source_2, COARSE_ITERS, inverse_2, bounds[2], COARSE_RATIO, operate_2, False)
    spread_rows = ones_where(
        jnp.logical_and(
            jnp.logical_and(
                iota((planes * slab, small), 1) // slab == iota((planes * slab, small), 0) // (2 * slab),
                (iota((planes * slab, small), 1) % slab) // rows == (iota((planes * slab, small), 0) % slab) // rows,
            ),
            iota((planes * slab, small), 1) % rows == (iota((planes * slab, small), 0) % rows) // 2,
        )
    )
    lifted = dot_select(dot_select(spread_rows, error_2), unfold)
    iterate = iterate + lifted - scaled(omega_1, inverse_1 * operate_1(lifted))
    residue = source_1 - operate_1(iterate)
    more, _ = chebyshev(residue, 2, inverse_1, bounds[1], SMOOTH_RATIO, operate_1, False)
    error_1 = iterate + more

    lifted_w[0:2] = jnp.zeros((2, slab, 128), F32)
    lifted_w[planes + 2 : planes + 4] = jnp.zeros((2, slab, 128), F32)
    lifted_w[2 : planes + 2] = error_1.reshape(planes, slab, 128)
    near = lifted_w[pl.ds(2 * gz, 6)]
    out_row, in_row = iota((SLAB, slab), 0), iota((SLAB, slab), 1)
    place = out_row % ROWS
    wanted = 4 * gy + place // 2 - jnp.where(place < 12, 0, 8)
    expand = ones_where(jnp.logical_and(out_row // ROWS == in_row // rows, in_row % rows == wanted))
    side = jnp.concatenate([near[plane] for plane in range(6)], axis=1)
    tall = dot_select(expand, side)
    tall = jnp.concatenate([tall[:, plane * 128 : plane * 128 + 128] for plane in range(6)], axis=0)
    stretch = ones_where(iota((128, LANES), 0) == iota((128, LANES), 1) // 2)
    sparse = dot_select(tall, stretch).reshape(6, 3, ROWS, LANES)
    error = jnp.stack([sparse[(plane + 1) // 2] for plane in range(10)], axis=0)

    scale, mass = scale_w[1:11], mass_w[...]
    inverse = inverse_diagonal(scale[1:9], mass[1:9], blocks, 1.0)
    image = fine_operator(fine, scale, mass[1:9], error)
    source = source_w[1:9]
    iterate = inverse * (scaled(gamma, source) - scaled(beta, power_1[...]) - scaled(omega, image)) + error[1:9]
    residue = source[1:7] - fine_operator(fine, scale[1:9], mass[2:8], iterate)
    direction = scaled(1.0 / centre, inverse[1:7] * residue)
    last = residue[1:5] - fine_operator(fine, scale[2:8], mass[3:7], direction)
    answer = iterate[2:6] + scaled(1.0 + keep, direction[1:5]) + scaled(push, inverse[2:6] * last)
    for comp in range(3):
        result[comp] = answer[:, comp, :8, :128]


def devices(counts):
    return [(x, y, z) for x in range(counts[0]) for y in range(counts[1]) for z in range(counts[2])]


def pairs(counts, target):
    def number(place):
        return (place[0] * counts[1] + place[1]) * counts[2] + place[2]

    return [(number(place), number(target(*place))) for place in devices(counts)]


def odd_partner(index):
    return index - 1 if index % 2 == 0 else index + 1


def on_device(right_side, stiff_scale, nodal_mass, stencil_blocks):
    counts = tuple(lax.axis_size(axis) for axis in AXES)
    gxs, gys, gzs = counts
    blocks = stencil_blocks.reshape(243)

    def send(values, target):
        return lax.ppermute(values, AXES, pairs(counts, target))

    def x_second(x, y, z):
        return (x, y, z ^ 1) if x in (0, gxs - 1) else (odd_partner(x), y, z)

    def z_second(x, y, z):
        return (x, y ^ 1, z) if z in (0, gzs - 1) else (x, y, odd_partner(z))

    planes, rows = 2 * gzs, 4 * gys
    width = -(-planes * 3 * rows // 128) * 128
    fine, fine_abs, mid, local_abs = call(
        functools.partial(matrices_kernel, rows, planes),
        [
            ((2, GROUP * 3 * SLAB, LANES), BF16),
            ((2, GROUP * 3 * SLAB, LANES), BF16),
            ((2, planes * 9 * rows, width), BF16),
            ((2, 144, 128), BF16),
        ],
        specs=[SM],
    )(blocks)

    half = ((10, 8, 128), F32)
    main, send_a, send_b = call(pack_x_kernel, [((20, 8, 128), F32), half, half])(right_side, stiff_scale, nodal_mass)
    got_a = send(send_a, lambda x, y, z: (x ^ 1, y, z))
    got_b = send(send_b, x_second)
    half = ((10, 8, LANES), F32)
    wide, *sends = call(
        functools.partial(pack_y_kernel, gxs), [((20, 8, LANES), F32)] + [half] * (1 if gys == 2 else 2)
    )(main, got_a, got_b)
    gots = [send(sends[0], lambda x, y, z: (x, y ^ 1, z))]
    if gys > 2:
        gots.append(send(sends[1], lambda x, y, z: (x, odd_partner(y) % gys, z)))
    part = ((16, ROWS, LANES), F32)
    whole, send_a, send_b = call(functools.partial(pack_z_kernel, gys), [((20, ROWS, LANES), F32), part, part])(wide, *gots)
    got_a = send(send_a, lambda x, y, z: (x, y, z ^ 1))
    got_b = send(send_b, z_second)

    scale_w, mass_w, source_w, bounds = call(
        functools.partial(window_kernel, gzs),
        [
            ((12, ROWS, LANES), F32),
            ((10, ROWS, LANES), F32),
            ((10, 3, ROWS, LANES), F32),
            ((3, 8, 128), F32),
        ],
        specs=[SM] + [VM] * 5,
    )(blocks, whole, got_a, got_b, fine_abs, local_abs)

    step = 4
    while step < gxs:
        bounds = jnp.maximum(bounds, send(bounds, lambda x, y, z: (x ^ step, y, z)))
        step *= 2
    others = [send(bounds, lambda x, y, z, flip=flip: (x ^ flip, y, z)) for flip in (1, 2, 3)]
    (power_1,) = call(
        power_kernel, [((8, 3, ROWS, LANES), F32)], specs=[SM] + [VM] * 4, flops=500000000, size=1000000
    )(blocks, scale_w, mass_w, source_w, fine)
    power_2, message = call(
        restrict_kernel, [((6, 3, ROWS, LANES), F32), ((17, 8, 128), F32)], specs=[SM] + [VM] * 9
    )(blocks, scale_w, mass_w, source_w, power_1, fine, bounds, *others)

    ordered = not (gys == 2 and gzs == 4)
    if ordered:
        gathered = lax.all_gather(message, ("gz", "gy"), tiled=False)
    else:
        four = jnp.stack(
            [
                message,
                send(message, lambda x, y, z: (x, y, z ^ 2)),
                send(message, lambda x, y, z: (x, y ^ 1, z)),
                send(message, lambda x, y, z: (x, y ^ 1, z ^ 2)),
            ]
        )
        gathered = jnp.concatenate([four, send(four, lambda x, y, z: (x, y, z ^ 1))])

    (result,) = call(
        functools.partial(final_kernel, gzs, gys, ordered),
        [(right_side.shape, F32)],
        specs=[SM] + [VM] * 8,
        scratch=[
            pltpu.VMEM((gzs, gys, 5, 8, 128), F32),
            pltpu.VMEM((planes, 5, rows, 128), F32),
            pltpu.VMEM((planes + 4, 3 * rows, 128), F32),
        ],
    )(blocks, gathered, scale_w, mass_w, source_w, power_1, power_2, fine, mid)
    return result


def solution(mesh):
    placed = (P(None, "gz", "gy", "gx"), P("gz", "gy", "gx"), P("gz", "gy", "gx"), P())
    return jax.shard_map(
        on_device, mesh=mesh, in_specs=placed, out_specs=P(None, "gz", "gy", "gx"), check_vma=False
    )
```

time: 716 us -> 54.6 us (0.08)
  the two profiles are of different devices: /device:TPU:26 before, /device:TPU:0 now
where the time goes in v1:
time: 54.6 us; the launch traced here: 54.3 us
  Pallas kernels  18.7 us (34%)
  starting transfers between devices  17 us (31%)
  waiting for transfers between devices  15.9 us (29%)
  local copies, waits for them, and re-layouts  2.57 us (5%)
    pallas_call x8, Pallas kernels, run(): pl.pallas_call(kernel, out_shape=outs, in_specs=specs or [VM] * len(args)...  18.7 us
    ppermute x12, starting transfers between devices, send(): return lax.ppermute(values, AXES, pairs(counts, target))  17 us
    ppermute x12, waiting for transfers between devices, send(): return lax.ppermute(values, AXES, pairs(counts, target))  15.9 us
    unnamed x13, local copies, waits for them, and re-layouts  2.38 us
  transfers between devices with their start and end apart: 12, of which 9 were waited for; matrix products, arithmetic and copies ran while one was open for 1% of the time, Pallas kernels for 4%

profile of v1, /device:TPU:0, one launch (start us, length us, event | category | flops | bytes accessed | tf_op | source)
XLA Modules:
  0.0 54.3 jit_solution(1943219673878992064)
XLA Ops:
  0.0 0.8 %copy-done = f32[3,4,8,128]{3,2,1,0:T(8,128)S(1)} copy-done((f32[3,4,8,128]{3,2,1,0:T(8,128)S(1)}, f32[3,4,8,128]{3,2,1,0:T(8,128)}, u32[]{:S(2)}) %copy-start) | copy-done | bytes 49176
  0.8 0.7 %copy-done.1 = f32[4,8,128]{2,1,0:T(8,128)S(1)} copy-done((f32[4,8,128]{2,1,0:T(8,128)S(1)}, f32[4,8,128]{2,1,0:T(8,128)}, u32[]{:S(2)}) %copy-start.1) | copy-done | bytes 16408
  1.5 0.7 %copy-done.2 = f32[4,8,128]{2,1,0:T(8,128)S(1)} copy-done((f32[4,8,128]{2,1,0:T(8,128)S(1)}, f32[4,8,128]{2,1,0:T(8,128)}, u32[]{:S(2)}) %copy-start.2) | copy-done | bytes 16408
  2.2 0.1 shard_map.46
  2.3 3.1 %collective-permute-start = (f32[10,8,128]{2,1,0:T(8,128)S(1)}, f32[10,8,128]{2,1,0:T(8,128)S(1)}, u32[]{:S(2)}, u32[]{:S(2)}) collective-permute-start(f32[10,8,128]{2,1,0:T(8,128)S(1)} %get-tuple-element.24), channel_id=1, source_target_pairs={{0,8},{1,9},{2,10},{3,11},{4,12},{5,13},{6,14},{7,15},{8,0},{9,1},... | collective-permute-start | bytes 122888 | tf_op jit(solution)/shard_map/ppermute | solution.py:506
  5.4 2.0 %collective-permute-done.got_a = f32[10,8,128]{2,1,0:T(8,128)S(1)} collective-permute-done((f32[10,8,128]{2,1,0:T(8,128)S(1)}, f32[10,8,128]{2,1,0:T(8,128)S(1)}, u32[]{:S(2)}, u32[]{:S(2)}) %collective-permute-start) | collective-permute-done | bytes 40992 | tf_op jit(solution)/shard_map/ppermute | solution.py:506
  7.4 0.1 shard_map.47
  7.5 2.0 %collective-permute-start.2 = (f32[10,8,256]{2,1,0:T(8,128)S(1)}, f32[10,8,256]{2,1,0:T(8,128)S(1)}, u32[]{:S(2)}, u32[]{:S(2)}) collective-permute-start(f32[10,8,256]{2,1,0:T(8,128)S(1)} %get-tuple-element.27), channel_id=1, source_target_pairs={{0,4},{1,5},{2,6},{3,7},{4,0},{5,1},{6,2},{7,3},{8,12},{9,13},{10,... | collective-permute-start | bytes 245768 | tf_op jit(solution)/shard_map/ppermute | solution.py:506
  9.5 2.5 %collective-permute-done.2.refs_0_ = f32[10,8,256]{2,1,0:T(8,128)S(1)} collective-permute-done((f32[10,8,256]{2,1,0:T(8,128)S(1)}, f32[10,8,256]{2,1,0:T(8,128)S(1)}, u32[]{:S(2)}, u32[]{:S(2)}) %collective-permute-start.2) | collective-permute-done | bytes 81952 | tf_op jit(solution)/shard_map/ppermute | solution.py:506
  12.0 0.1 shard_map.48
  12.1 0.1 collective-permute-start.3
  12.2 2.0 %collective-permute-start.4 = (f32[16,16,256]{2,1,0:T(8,128)S(1)}, f32[16,16,256]{2,1,0:T(8,128)S(1)}, u32[]{:S(2)}, u32[]{:S(2)}) collective-permute-start(f32[16,16,256]{2,1,0:T(8,128)S(1)} %get-tuple-element.30), channel_id=1, source_target_pairs={{0,4},{1,2},{2,1},{3,7},{4,0},{5,6},{6,5},{7,3},{8,12},{9,10},{10,... | collective-permute-start | bytes 786440 | tf_op jit(solution)/shard_map/ppermute | solution.py:506
  14.2 0.1 copy.5
  14.3 0.2 reshape.3.blocks
  14.5 1.0 %shard_map.49 = (bf16[2,432,256]{2,1,0:T(8,128)(2,1)S(1)}, bf16[2,432,256]{2,1,0:T(8,128)(2,1)S(1)}, bf16[2,576,256]{2,1,0:T(8,128)(2,1)S(1)}, bf16[2,144,128]{2,1,0:T(8,128)(2,1)S(1)}) custom-call(f32[243]{0:T(256)S(1)} %reshape.3.blocks), custom_call_target="tpu_custom_call" | custom-call | flops 1000000 | bytes 100000 | tf_op jit(solution)/shard_map/pallas_call | solution.py:27
  15.5 3.1 %collective-permute-done.4.got_b = f32[16,16,256]{2,1,0:T(8,128)S(1)} collective-permute-done((f32[16,16,256]{2,1,0:T(8,128)S(1)}, f32[16,16,256]{2,1,0:T(8,128)S(1)}, u32[]{:S(2)}, u32[]{:S(2)}) %collective-permute-start.4) | collective-permute-done | bytes 262176 | tf_op jit(solution)/shard_map/ppermute | solution.py:506
  18.6 2.1 %shard_map.50 = (f32[12,16,256]{2,1,0:T(8,128)S(1)}, f32[10,16,256]{2,1,0:T(8,128)S(1)}, f32[10,3,16,256]{3,2,1,0:T(8,128)S(1)}, f32[3,8,128]{2,1,0:T(8,128)S(1)}) custom-call(f32[243]{0:T(256)S(1)} %reshape.3.blocks, f32[20,16,256]{2,1,0:T(8,128)S(1)} %get-tuple-element.28.whole, f32[16,16,256]{2,1,0:T(8,128)S(1)} %collective-permute-done.3.got_a, ...), custom_call_target="tpu_custom_call" | custom-call | flops 1000000 | bytes 100000 | tf_op jit(solution)/shard_map/pallas_call | solution.py:27
  20.7 3.2 %collective-permute-start.5 = (f32[3,8,128]{2,1,0:T(8,128)S(1)}, f32[3,8,128]{2,1,0:T(8,128)S(1)}, u32[]{:S(2)}, u32[]{:S(2)}) collective-permute-start(f32[3,8,128]{2,1,0:T(8,128)S(1)} %get-tuple-element.37.bounds), channel_id=1, source_target_pairs={{0,8},{1,9},{2,10},{3,11},{4,12},{5,13},{6,14},{7,15},{8,0},{9,1},... | collective-permute-start | bytes 36872 | tf_op jit(solution)/shard_map/ppermute | solution.py:506
  23.9 1.5 %collective-permute-start.6 = (f32[3,8,128]{2,1,0:T(8,128)S(1)}, f32[3,8,128]{2,1,0:T(8,128)S(1)}, u32[]{:S(2)}, u32[]{:S(2)}) collective-permute-start(f32[3,8,128]{2,1,0:T(8,128)S(1)} %get-tuple-element.37.bounds), channel_id=1, source_target_pairs={{0,16},{1,17},{2,18},{3,19},{4,20},{5,21},{6,22},{7,23},{8,24},{9,... | collective-permute-start | bytes 36872 | tf_op jit(solution)/shard_map/ppermute | solution.py:506
  25.4 1.4 %collective-permute-start.7 = (f32[3,8,128]{2,1,0:T(8,128)S(1)}, f32[3,8,128]{2,1,0:T(8,128)S(1)}, u32[]{:S(2)}, u32[]{:S(2)}) collective-permute-start(f32[3,8,128]{2,1,0:T(8,128)S(1)} %get-tuple-element.37.bounds), channel_id=1, source_target_pairs={{0,24},{1,25},{2,26},{3,27},{4,28},{5,29},{6,30},{7,31},{8,16},{9,... | collective-permute-start | bytes 36872 | tf_op jit(solution)/shard_map/ppermute | solution.py:506
  26.8 1.3 %shard_map.51.power_1 = f32[8,3,16,256]{3,2,1,0:T(8,128)S(1)} custom-call(f32[243]{0:T(256)S(1)} %reshape.3.blocks, f32[12,16,256]{2,1,0:T(8,128)S(1)} %get-tuple-element.33.scale_w, f32[10,16,256]{2,1,0:T(8,128)S(1)} %get-tuple-element.34.mass_w, f32[10,3,16,256]{3,2,1,0:T(8,128)S(1)} %get-tuple-element.35.source_w, ...), custom_call_target="tpu_custom_call" | custom-call | flops 500000000 | bytes 1000000 | tf_op jit(solution)/shard_map/pallas_call | solution.py:27
  28.1 0.3 collective-permute-done.6.refs_1_
  28.5 2.4 %collective-permute-done.7.refs_2_ = f32[3,8,128]{2,1,0:T(8,128)S(1)} collective-permute-done((f32[3,8,128]{2,1,0:T(8,128)S(1)}, f32[3,8,128]{2,1,0:T(8,128)S(1)}, u32[]{:S(2)}, u32[]{:S(2)}) %collective-permute-start.7) | collective-permute-done | bytes 12320 | tf_op jit(solution)/shard_map/ppermute | solution.py:506
  30.9 2.4 %shard_map.52 = (f32[6,3,16,256]{3,2,1,0:T(8,128)S(1)}, f32[17,8,128]{2,1,0:T(8,128)S(1)}) custom-call(f32[243]{0:T(256)S(1)} %reshape.3.blocks, f32[12,16,256]{2,1,0:T(8,128)S(1)} %get-tuple-element.33.scale_w, f32[10,16,256]{2,1,0:T(8,128)S(1)} %get-tuple-element.34.mass_w, f32[10,3,16,256]{3,2,1,0:T(8,128)S(1)} %get-tuple-element.35.source_w, ...), custom_call_target="tpu_custom_call" | custom-call | flops 1000000 | bytes 100000 | tf_op jit(solution)/shard_map/pallas_call | solution.py:27
  33.3 1.0 %collective-permute-start.8 = (f32[17,8,128]{2,1,0:T(8,128)S(1)}, f32[17,8,128]{2,1,0:T(8,128)S(1)}, u32[]{:S(2)}, u32[]{:S(2)}) collective-permute-start(f32[17,8,128]{2,1,0:T(8,128)S(1)} %get-tuple-element.38), channel_id=1, source_target_pairs={{0,2},{1,3},{2,0},{3,1},{4,6},{5,7},{6,4},{7,5},{8,10},{9,11},{10,... | collective-permute-start | bytes 208904 | tf_op jit(solution)/shard_map/ppermute | solution.py:506
  34.3 1.5 %collective-permute-start.9 = (f32[17,8,128]{2,1,0:T(8,128)S(1)}, f32[17,8,128]{2,1,0:T(8,128)S(1)}, u32[]{:S(2)}, u32[]{:S(2)}) collective-permute-start(f32[17,8,128]{2,1,0:T(8,128)S(1)} %get-tuple-element.38), channel_id=1, source_target_pairs={{0,4},{1,5},{2,6},{3,7},{4,0},{5,1},{6,2},{7,3},{8,12},{9,13},{10,... | collective-permute-start | bytes 208904 | tf_op jit(solution)/shard_map/ppermute | solution.py:506
  35.8 1.1 %collective-permute-start.10 = (f32[17,8,128]{2,1,0:T(8,128)S(1)}, f32[17,8,128]{2,1,0:T(8,128)S(1)}, u32[]{:S(2)}, u32[]{:S(2)}) collective-permute-start(f32[17,8,128]{2,1,0:T(8,128)S(1)} %get-tuple-element.38), channel_id=1, source_target_pairs={{0,6},{1,7},{2,4},{3,5},{4,2},{5,3},{6,0},{7,1},{8,14},{9,15},{10,... | collective-permute-start | bytes 208904 | tf_op jit(solution)/shard_map/ppermute | solution.py:506
  36.9 1.1 %collective-permute-done.8 = f32[17,8,128]{2,1,0:T(8,128)S(1)} collective-permute-done((f32[17,8,128]{2,1,0:T(8,128)S(1)}, f32[17,8,128]{2,1,0:T(8,128)S(1)}, u32[]{:S(2)}, u32[]{:S(2)}) %collective-permute-start.8) | collective-permute-done | bytes 69664 | tf_op jit(solution)/shard_map/ppermute | solution.py:506
  38.0 1.0 %collective-permute-done.9 = f32[17,8,128]{2,1,0:T(8,128)S(1)} collective-permute-done((f32[17,8,128]{2,1,0:T(8,128)S(1)}, f32[17,8,128]{2,1,0:T(8,128)S(1)}, u32[]{:S(2)}, u32[]{:S(2)}) %collective-permute-start.9) | collective-permute-done | bytes 69664 | tf_op jit(solution)/shard_map/ppermute | solution.py:506
  39.0 2.1 %collective-permute-done.10 = f32[17,8,128]{2,1,0:T(8,128)S(1)} collective-permute-done((f32[17,8,128]{2,1,0:T(8,128)S(1)}, f32[17,8,128]{2,1,0:T(8,128)S(1)}, u32[]{:S(2)}, u32[]{:S(2)}) %collective-permute-start.10) | collective-permute-done | bytes 69664 | tf_op jit(solution)/shard_map/ppermute | solution.py:506
  41.2 1.5 %collective-permute-done.11 = f32[4,17,8,128]{3,2,1,0:T(8,128)S(1)} collective-permute-done((f32[4,17,8,128]{3,2,1,0:T(8,128)S(1)}, f32[4,17,8,128]{3,2,1,0:T(8,128)S(1)}, u32[]{:S(2)}, u32[]{:S(2)}) %collective-permute-start.11) | collective-permute-done | bytes 278560 | tf_op jit(solution)/shard_map/ppermute | solution.py:506
  42.7 11.6 %shard_map.53 = f32[3,4,8,128]{3,2,1,0:T(8,128)} custom-call(f32[243]{0:T(256)S(1)} %reshape.3.blocks, f32[8,17,8,128]{3,2,1,0:T(8,128)S(1)} %constant_dynamic-update-slice_fusion.gathered, f32[12,16,256]{2,1,0:T(8,128)S(1)} %get-tuple-element.33.scale_w, f32[10,16,256]{2,1,0:T(8,128)S(1)} %get-tuple-element.34.mass_w, ...), custom_call_target="tpu_custom_call" | custom-call | flops 1000000 | bytes 100000 | tf_op jit(solution)/shard_map/pallas_call | solution.py:27
  (16 shorter events, 0.2 us)
Async XLA Ops:
  0.0 0.8 %copy-start = (f32[3,4,8,128]{3,2,1,0:T(8,128)S(1)}, f32[3,4,8,128]{3,2,1,0:T(8,128)}, u32[]{:S(2)}) copy-start(f32[3,4,8,128]{3,2,1,0:T(8,128)} %source.1) | copy-start | bytes 147460
  0.8 0.7 %copy-start.1 = (f32[4,8,128]{2,1,0:T(8,128)S(1)}, f32[4,8,128]{2,1,0:T(8,128)}, u32[]{:S(2)}) copy-start(f32[4,8,128]{2,1,0:T(8,128)} %scale.1) | copy-start | bytes 49156
  1.5 0.7 %copy-start.2 = (f32[4,8,128]{2,1,0:T(8,128)S(1)}, f32[4,8,128]{2,1,0:T(8,128)}, u32[]{:S(2)}) copy-start(f32[4,8,128]{2,1,0:T(8,128)} %mass.1) | copy-start | bytes 49156
  2.3 5.1 %collective-permute-start = (f32[10,8,128]{2,1,0:T(8,128)S(1)}, f32[10,8,128]{2,1,0:T(8,128)S(1)}, u32[]{:S(2)}, u32[]{:S(2)}) collective-permute-start(f32[10,8,128]{2,1,0:T(8,128)S(1)} %get-tuple-element.24), channel_id=1, source_target_pairs={{0,8},{1,9},{2,10},{3,11},{4,12},{5,13},{6,14},{7,15},{8,0},{9,1},... | collective-permute-start | bytes 122888 | tf_op jit(solution)/shard_map/ppermute | solution.py:506
  5.4 2.0 %collective-permute-start.1 = (f32[10,8,128]{2,1,0:T(8,128)S(1)}, f32[10,8,128]{2,1,0:T(8,128)S(1)}, u32[]{:S(2)}, u32[]{:S(2)}) collective-permute-start(f32[10,8,128]{2,1,0:T(8,128)S(1)} %get-tuple-element.25), channel_id=1, source_target_pairs={{0,1},{1,0},{2,3},{3,2},{4,5},{5,4},{6,7},{7,6},{8,16},{9,17},{10,... | collective-permute-start | bytes 122888 | tf_op jit(solution)/shard_map/ppermute | solution.py:506
  7.5 4.5 %collective-permute-start.2 = (f32[10,8,256]{2,1,0:T(8,128)S(1)}, f32[10,8,256]{2,1,0:T(8,128)S(1)}, u32[]{:S(2)}, u32[]{:S(2)}) collective-permute-start(f32[10,8,256]{2,1,0:T(8,128)S(1)} %get-tuple-element.27), channel_id=1, source_target_pairs={{0,4},{1,5},{2,6},{3,7},{4,0},{5,1},{6,2},{7,3},{8,12},{9,13},{10,... | collective-permute-start | bytes 245768 | tf_op jit(solution)/shard_map/ppermute | solution.py:506
  12.0 2.2 %copy-start.3 = (f32[27,3,3]{0,2,1:T(4,128)S(1)}, f32[27,3,3]{0,2,1:T(4,128)}, u32[]{:S(2)}) copy-start(f32[27,3,3]{0,2,1:T(4,128)} %param.7) | copy-start | bytes 2920
  12.1 3.5 %collective-permute-start.3 = (f32[16,16,256]{2,1,0:T(8,128)S(1)}, f32[16,16,256]{2,1,0:T(8,128)S(1)}, u32[]{:S(2)}, u32[]{:S(2)}) collective-permute-start(f32[16,16,256]{2,1,0:T(8,128)S(1)} %get-tuple-element.29), channel_id=1, source_target_pairs={{0,1},{1,0},{2,3},{3,2},{4,5},{5,4},{6,7},{7,6},{8,9},{9,8},{10,11... | collective-permute-start | bytes 786440 | tf_op jit(solution)/shard_map/ppermute | solution.py:506
  12.2 6.4 %collective-permute-start.4 = (f32[16,16,256]{2,1,0:T(8,128)S(1)}, f32[16,16,256]{2,1,0:T(8,128)S(1)}, u32[]{:S(2)}, u32[]{:S(2)}) collective-permute-start(f32[16,16,256]{2,1,0:T(8,128)S(1)} %get-tuple-element.30), channel_id=1, source_target_pairs={{0,4},{1,2},{2,1},{3,7},{4,0},{5,6},{6,5},{7,3},{8,12},{9,10},{10,... | collective-permute-start | bytes 786440 | tf_op jit(solution)/shard_map/ppermute | solution.py:506
  20.7 7.5 %collective-permute-start.5 = (f32[3,8,128]{2,1,0:T(8,128)S(1)}, f32[3,8,128]{2,1,0:T(8,128)S(1)}, u32[]{:S(2)}, u32[]{:S(2)}) collective-permute-start(f32[3,8,128]{2,1,0:T(8,128)S(1)} %get-tuple-element.37.bounds), channel_id=1, source_target_pairs={{0,8},{1,9},{2,10},{3,11},{4,12},{5,13},{6,14},{7,15},{8,0},{9,1},... | collective-permute-start | bytes 36872 | tf_op jit(solution)/shard_map/ppermute | solution.py:506
  23.9 4.6 %collective-permute-start.6 = (f32[3,8,128]{2,1,0:T(8,128)S(1)}, f32[3,8,128]{2,1,0:T(8,128)S(1)}, u32[]{:S(2)}, u32[]{:S(2)}) collective-permute-start(f32[3,8,128]{2,1,0:T(8,128)S(1)} %get-tuple-element.37.bounds), channel_id=1, source_target_pairs={{0,16},{1,17},{2,18},{3,19},{4,20},{5,21},{6,22},{7,23},{8,24},{9,... | collective-permute-start | bytes 36872 | tf_op jit(solution)/shard_map/ppermute | solution.py:506
  25.4 5.5 %collective-permute-start.7 = (f32[3,8,128]{2,1,0:T(8,128)S(1)}, f32[3,8,128]{2,1,0:T(8,128)S(1)}, u32[]{:S(2)}, u32[]{:S(2)}) collective-permute-start(f32[3,8,128]{2,1,0:T(8,128)S(1)} %get-tuple-element.37.bounds), channel_id=1, source_target_pairs={{0,24},{1,25},{2,26},{3,27},{4,28},{5,29},{6,30},{7,31},{8,16},{9,... | collective-permute-start | bytes 36872 | tf_op jit(solution)/shard_map/ppermute | solution.py:506
  33.3 4.7 %collective-permute-start.8 = (f32[17,8,128]{2,1,0:T(8,128)S(1)}, f32[17,8,128]{2,1,0:T(8,128)S(1)}, u32[]{:S(2)}, u32[]{:S(2)}) collective-permute-start(f32[17,8,128]{2,1,0:T(8,128)S(1)} %get-tuple-element.38), channel_id=1, source_target_pairs={{0,2},{1,3},{2,0},{3,1},{4,6},{5,7},{6,4},{7,5},{8,10},{9,11},{10,... | collective-permute-start | bytes 208904 | tf_op jit(solution)/shard_map/ppermute | solution.py:506
  34.3 4.6 %collective-permute-start.9 = (f32[17,8,128]{2,1,0:T(8,128)S(1)}, f32[17,8,128]{2,1,0:T(8,128)S(1)}, u32[]{:S(2)}, u32[]{:S(2)}) collective-permute-start(f32[17,8,128]{2,1,0:T(8,128)S(1)} %get-tuple-element.38), channel_id=1, source_target_pairs={{0,4},{1,5},{2,6},{3,7},{4,0},{5,1},{6,2},{7,3},{8,12},{9,13},{10,... | collective-permute-start | bytes 208904 | tf_op jit(solution)/shard_map/ppermute | solution.py:506
  35.8 5.2 %collective-permute-start.10 = (f32[17,8,128]{2,1,0:T(8,128)S(1)}, f32[17,8,128]{2,1,0:T(8,128)S(1)}, u32[]{:S(2)}, u32[]{:S(2)}) collective-permute-start(f32[17,8,128]{2,1,0:T(8,128)S(1)} %get-tuple-element.38), channel_id=1, source_target_pairs={{0,6},{1,7},{2,4},{3,5},{4,2},{5,3},{6,0},{7,1},{8,14},{9,15},{10,... | collective-permute-start | bytes 208904 | tf_op jit(solution)/shard_map/ppermute | solution.py:506
  41.1 1.6 %collective-permute-start.11 = (f32[4,17,8,128]{3,2,1,0:T(8,128)S(1)}, f32[4,17,8,128]{3,2,1,0:T(8,128)S(1)}, u32[]{:S(2)}, u32[]{:S(2)}) collective-permute-start(f32[4,17,8,128]{3,2,1,0:T(8,128)S(1)} %pad_maximum_fusion), channel_id=1, source_target_pairs={{0,1},{1,0},{2,3},{3,2},{4,5},{5,4},{6,7},{7,6},{8,9},{9,8},{10,11... | collective-permute-start | bytes 835592 | tf_op jit(solution)/shard_map/ppermute | solution.py:506

commit v2 on v0

v2 whole, which is shorter than its diff:
```python
import functools

import jax
import jax.numpy as jnp
from jax import lax
from jax.experimental import pallas as pl
from jax.experimental.pallas import tpu as pltpu
from jax.sharding import PartitionSpec as P

AXES = ("gx", "gy", "gz")
COARSE_ITERS = 8
SMOOTH_RATIO = 20.0
COARSE_RATIO = 200.0
F32, BF16 = jnp.float32, jnp.bfloat16
VM = pl.BlockSpec(memory_space=pltpu.VMEM)
SM = pl.BlockSpec(memory_space=pltpu.SMEM)
HB = pl.BlockSpec(memory_space=pltpu.HBM)
LANES = 256
PAD = 3


def call(kernel, outs, specs=None, scratch=(), flops=1000000, size=100000, grant=None):
    params = pltpu.CompilerParams(vmem_limit_bytes=grant * 1024 * 1024) if grant else None
    outs = [jax.ShapeDtypeStruct(shape, dtype) for shape, dtype in outs]

    def run(*args):
        return pl.pallas_call(
            kernel,
            out_shape=outs,
            in_specs=specs or [VM] * len(args),
            out_specs=[VM] * len(outs),
            scratch_shapes=scratch,
            compiler_params=params,
            cost_estimate=pl.CostEstimate(flops=flops, bytes_accessed=size, transcendentals=0),
        )(*args)

    return run


def iota(shape, dim):
    return lax.broadcasted_iota(jnp.int32, shape, dim)


def ones_where(mask):
    return jnp.where(mask, 1.0, 0.0).astype(BF16)


def split(values):
    high = values.astype(BF16)
    return high, (values - high.astype(F32)).astype(BF16)


def dot(left, right):
    return jnp.dot(left, right, preferred_element_type=F32)


def lanes_apply(values, stacked):
    return dot(jnp.concatenate(split(values), axis=1), stacked)


def rows_apply(selection, values):
    width = values.shape[1]
    product = dot(selection, jnp.concatenate(split(values), axis=1))
    return product[:, :width] + product[:, width:]


def banded(matrix_high, matrix_low, values):
    high, low = split(values)
    return dot(matrix_high, high) + dot(matrix_low, high) + dot(matrix_high, low)


def banded_stacked(matrix, values):
    high, low = split(values)
    return dot(matrix, jnp.concatenate([high, high, low], axis=0))


def shifted_sum(product, slabs, rows, lanes):
    parts = product.reshape(slabs, 3, rows, lanes)
    below = parts[:, 0].reshape(slabs * rows, lanes)
    above = parts[:, 2].reshape(slabs * rows, lanes)
    here = parts[:, 1].reshape(slabs * rows, lanes)
    return here + pltpu.roll(below, 1, 1) + pltpu.roll(above, lanes - 1, 1)


def group_of(slab):
    return max(1, 256 // slab - 2)


def groups(planes, most):
    sizes = []
    while planes:
        size = min(most, planes)
        if most > 2 and planes == most + 1:
            size = 2
        sizes.append(size)
        planes -= size
    return sizes


def fine_stencil(matrix, values):
    planes, rows = values.shape[0] - 2, values.shape[2]
    slab = 3 * rows
    flat = values.reshape((planes + 2) * slab, LANES)
    outs = []
    at = 0
    for size in groups(planes, group_of(slab)):
        height, depth = size * 3 * slab, (size + 2) * slab
        product = banded(
            matrix[0, :height, :depth], matrix[1, :height, :depth], flat[at * slab : at * slab + depth]
        )
        outs.append(shifted_sum(product, size, slab, LANES))
        at += size
    return jnp.concatenate(outs, axis=0).reshape(planes, 3, rows, LANES)


def panels(value_of, others, rows, width):
    column = iota((8, width), 1)
    which = column // rows
    row_in = column % rows
    result = {}
    for step_x in range(3):
        for comp in range(3):
            coeffs = []
            for step_y in range(3):
                coeff = jnp.zeros((8, width), F32)
                for plane in range(3):
                    for other in range(others):
                        value = value_of(plane * 9 + step_y * 3 + step_x, comp, other)
                        coeff = jnp.where(which == plane * others + other, value, coeff)
                coeffs.append(coeff)
            pieces = []
            for block in range(rows // 8):
                gap = row_in - (iota((8, width), 0) + block * 8)
                piece = jnp.zeros((8, width), F32)
                for step_y in range(3):
                    piece = jnp.where(gap == step_y - 1, coeffs[step_y], piece)
                pieces.append(piece)
            result[step_x, comp] = jnp.concatenate(pieces, axis=0)
    return result


def turned(value, turn):
    turn %= value.shape[1]
    return pltpu.roll(value, turn, 1) if turn else value


def parts_of(value):
    high = value.astype(BF16).astype(F32)
    return high, value - high


def stack3(value, size):
    high, low = parts_of(value)
    return (high + turned(low, size) + turned(high, 2 * size)).astype(BF16)


def up128(size):
    return -(-size // 128) * 128


def matrices_kernel(
    rows, planes, blocks, fine, fine_bound, mid, mid_bound, coarse, coarse_bound, coarse_diag,
    gather_rows, spread_rows, expand, fold, unfold, squeeze, stretch,
):
    def direct(offset, comp, other):
        return blocks[offset * 9 + comp * 3 + other]

    def absolute(offset, comp, other):
        at = offset * 9 + comp * 3
        return jnp.abs(blocks[at]) + jnp.abs(blocks[at + 1]) + jnp.abs(blocks[at + 2])

    slab = 3 * rows
    group = group_of(slab)
    found = panels(direct, 3, rows, fine.shape[2])
    bound = panels(absolute, 1, rows, fine_bound.shape[1])
    for plane in range(group):
        for step_x in range(3):
            start = (plane * 3 + step_x) * slab
            value = turned(jnp.concatenate([found[step_x, comp] for comp in range(3)], axis=0), plane * slab)
            high, low = split(value)
            fine[0, start : start + slab, :] = high
            fine[1, start : start + slab, :] = low
            value = turned(jnp.concatenate([bound[step_x, comp] for comp in range(3)], axis=0), plane * rows)
            fine_bound[start : start + slab, :] = stack3(value, (group + 2) * rows)

    rows, planes = rows // 2, planes // 2
    slab = 3 * rows
    width, bound_width = mid.shape[2], mid_bound.shape[1]
    found = panels(direct, 3, rows, width)
    bound = panels(absolute, 1, rows, bound_width)

    def cut(value, plane, size):
        column = iota(value.shape, 1)
        if plane == 0:
            value = jnp.where(column < size, 0.0, value)
        if plane == planes - 1:
            value = jnp.where(column >= 2 * size, 0.0, value)
        return turned(value, (plane - 1) * size)

    for plane in range(planes):
        for step_x in range(3):
            start = (plane * 3 + step_x) * slab
            value = jnp.concatenate([found[step_x, comp] for comp in range(3)], axis=0)
            high, low = split(cut(value, plane, slab))
            mid[0, start : start + slab, :] = high
            mid[1, start : start + slab, :] = low
            value = jnp.concatenate([bound[step_x, comp] for comp in range(3)], axis=0)
            mid_bound[start : start + slab, :] = stack3(cut(value, plane, rows), planes * rows)

    few, half = rows // 2, planes // 2
    tall, wide = half * 9 * few, half * 3 * few
    place = iota((tall, 2 * tall), 0)
    choose = ones_where(iota((tall, 2 * tall), 1) == place // few * rows + place % few)

    def smaller(matrix, count, size):
        place = iota((2 * count, size), 1)
        pick = ones_where(iota((2 * count, size), 0) == place // few * rows + place % few)
        return dot(dot(choose, matrix).astype(BF16), pick)

    high = smaller(mid[0, : 2 * tall, : 2 * wide], wide, coarse.shape[1])
    low = smaller(mid[1, : 2 * tall, : 2 * wide], wide, coarse.shape[1])
    keep = iota(high.shape, 1) < wide
    high, low = jnp.where(keep, high, 0.0), jnp.where(keep, low, 0.0)
    coarse[...] = (high + turned(low, wide) + turned(high, 2 * wide)).astype(BF16)
    count = half * few
    size = planes * rows
    whole = mid_bound[: 2 * tall, :]
    high = smaller(whole[:, : 2 * count], count, coarse_bound.shape[1])
    low = smaller(whole[:, size : size + 2 * count], count, coarse_bound.shape[1])
    keep = iota(high.shape, 1) < count
    high, low = jnp.where(keep, high, 0.0), jnp.where(keep, low, 0.0)
    coarse_bound[...] = (high + turned(low, count) + turned(high, 2 * count)).astype(BF16)
    comp = (iota((wide, 128), 0) // few) % 3
    diag = [blocks[13 * 9 + 4 * at] for at in range(3)]
    coarse_diag[...] = jnp.where(comp == 0, diag[0], jnp.where(comp == 1, diag[1], diag[2]))

    def same_aggregate(out_row, in_row, out_rows, in_rows, ratio_z):
        same_plane = out_row // (3 * out_rows) == in_row // (3 * in_rows * ratio_z)
        same_comp = out_row // out_rows % 3 == in_row // in_rows % 3
        return jnp.logical_and(jnp.logical_and(same_plane, same_comp), out_row % out_rows == in_row % in_rows // 2)

    big = planes * slab
    shape = (wide, big)
    gather_rows[...] = ones_where(same_aggregate(iota(shape, 0), iota(shape, 1), few, rows, 2))
    shape = (big, 2 * wide)
    spread_rows[...] = ones_where(same_aggregate(iota(shape, 1) % wide, iota(shape, 0), few, rows, 2))
    shape = (2 * slab, 2 * slab)
    expand[...] = ones_where(same_aggregate(iota(shape, 1) % slab, iota(shape, 0), rows, 2 * rows, 1))
    shape = (256, 128)
    fold[...] = ones_where(iota(shape, 0) % 128 // 2 == iota(shape, 1) % 64)
    unfold[...] = ones_where(iota(shape, 0) % 128 == iota(shape, 1) // 2)
    shape = (2 * LANES, 128)
    squeeze[...] = ones_where(iota(shape, 0) % LANES // 2 == iota(shape, 1))
    shape = (256, LANES)
    stretch[...] = ones_where(iota(shape, 0) % 128 == iota(shape, 1) // 2)


def halves(planes, low):
    first, second = planes[:10], pltpu.roll(planes[10:], 64, 2)
    return jnp.where(low, second, first), jnp.where(low, first, second)


def pack_kernel(source, scale, mass, main, send_a, send_b, sems):
    copies = [
        pltpu.make_async_copy(source.at[comp], main.at[pl.ds(comp * 4, 4)], sems.at[comp]) for comp in range(3)
    ]
    copies.append(pltpu.make_async_copy(scale, main.at[pl.ds(12, 4)], sems.at[3]))
    copies.append(pltpu.make_async_copy(mass, main.at[pl.ds(16, 4)], sems.at[4]))
    for copy in copies:
        copy.start()
    for copy in copies:
        copy.wait()
    high, low = halves(main[...], iota((10, 8, 128), 2) < 64)
    even = lax.rem(lax.axis_index("gx"), 2) == 0
    send_a[...] = jnp.where(even, high, low)
    send_b[...] = jnp.where(even, low, high)


def widen_kernel(count, main, got_a, got_b, wide):
    index = lax.axis_index("gx")
    even = lax.rem(index, 2) == 0
    first, second = got_a[...], got_b[...]
    above = jnp.where(index < count - 1, jnp.where(even, first, second), 0.0)
    below = jnp.where(index > 0, jnp.where(even, second, first), 0.0)
    low = iota((10, 8, 128), 2) < 64
    wide[:, :, :128] = main[...]
    wide[:10, :, 128:] = jnp.where(low, above, below)
    wide[10:, :, 128:] = jnp.where(low, pltpu.roll(above, 64, 2), pltpu.roll(below, 64, 2))


def inverse_diagonal(scale, mass, blocks, factor):
    square = scale * scale
    parts = []
    for comp in range(3):
        diag = factor * blocks[13 * 9 + comp * 4] * square + mass
        parts.append(jnp.where(scale > 0.0, 1.0 / diag, 0.0)[:, None])
    return jnp.concatenate(parts, axis=1)


def largest(ratio, lanes):
    width = ratio.shape[1]
    flat = jnp.max(ratio.reshape(-1, 8, width), axis=0)
    own = jnp.where(iota((8, width), 1) < lanes, flat, -jnp.inf)
    return jnp.full((8, 128), jnp.max(own), F32)


def paired_planes(values):
    pairs = values.reshape((-1, 2) + values.shape[1:])
    return pairs[:, 0] + pairs[:, 1]


def paired_rows(held, values):
    for half in (0, 1):
        held[half] = values[:, half * 128 : half * 128 + 128]
    count = held.shape[1] // 2
    return jnp.concatenate(
        [held[half, pl.ds(0, count, stride=2)] + held[half, pl.ds(1, count, stride=2)] for half in (0, 1)], axis=1
    )


def window_kernel(
    gys, ordered, blocks, *refs
):
    (*blocks_in, fine_bound, mid_bound, coarse_bound, coarse_diag, gather_rows, fold, squeeze,
     source_w, scale_w, mass_w, inverse_w, spread_1w, weight_1w, inverse_1w, spread_2w, weight_2w, inverse_2w, bounds, held) = refs
    planes, rows = scale_w.shape[0] - 2 * PAD, scale_w.shape[1]
    gz, gy = lax.axis_index("gz"), lax.axis_index("gy")
    for at in (0, planes + PAD):
        source_w[at : at + PAD] = jnp.zeros((PAD, 3, rows, LANES), F32)
        inverse_w[at : at + PAD] = jnp.zeros((PAD, 3, rows, LANES), F32)
        scale_w[at : at + PAD] = jnp.zeros((PAD, rows, LANES), F32)
        mass_w[at : at + PAD] = jnp.zeros((PAD, rows, LANES), F32)
    number = 0
    for ref in blocks_in:
        for block in range(ref.shape[0]):
            if ordered:
                place_z, place_y = number // gys, number % gys
            else:
                place_z = lax.bitwise_xor(gz, number // 4 + 2 * (number % 2))
                place_y = lax.bitwise_xor(gy, number % 4 // 2)
            at_z = pl.ds(PAD + 4 * place_z, 4)
            at_y = pl.ds(pl.multiple_of(8 * place_y, 8), 8)
            for comp in range(3):
                source_w[at_z, comp, at_y, :] = ref[block, comp * 4 : comp * 4 + 4]
            scale_w[at_z, at_y, :] = ref[block, 12:16]
            mass_w[at_z, at_y, :] = ref[block, 16:20]
            number += 1

    scale, mass = scale_w[PAD : PAD + planes], mass_w[PAD : PAD + planes]
    inverse = inverse_diagonal(scale, mass, blocks, 1.0)
    inverse_w[PAD : PAD + planes] = inverse
    slab = 3 * rows
    outs = []
    at = 0
    for size in groups(planes, group_of(slab)):
        near = scale_w[PAD - 1 + at : PAD + 1 + at + size].reshape((size + 2) * rows, LANES)
        if size < group_of(slab):
            near = jnp.concatenate([near, jnp.zeros(((group_of(slab) - size) * rows, LANES), F32)], axis=0)
        depth = 3 * (group_of(slab) + 2) * rows
        outs.append(shifted_sum(banded_stacked(fine_bound[: size * 3 * slab, :depth], near), size, slab, LANES))
        at += size
    total = jnp.concatenate(outs, axis=0).reshape(planes, 3, rows, LANES)
    ratio = (scale[:, None] * total + mass[:, None]) * inverse
    bounds[0] = largest(ratio.reshape(planes * slab, LANES), 128)

    rows, planes = rows // 2, planes // 2
    slab = 3 * rows
    count = planes * rows
    pairs = [
        paired_rows(held.at[at], paired_planes(values).reshape(2 * count, LANES))
        for at, values in enumerate((scale, mass))
    ]
    middle = lanes_apply(jnp.concatenate(pairs, axis=0), squeeze[...])
    scale_1 = (middle[:count] * 0.125).reshape(planes, rows, 128)
    mass_1 = middle[count:].reshape(planes, rows, 128)
    inverse_1 = inverse_diagonal(scale_1, mass_1, blocks, 2.0).reshape(planes * slab, 128)
    spread_1 = jnp.broadcast_to(scale_1[:, None], (planes, 3, rows, 128)).reshape(planes * slab, 128)
    weight_1 = jnp.broadcast_to(mass_1[:, None], (planes, 3, rows, 128)).reshape(planes * slab, 128)
    product = banded_stacked(mid_bound[:, : 3 * count], scale_1.reshape(count, 128))
    total = shifted_sum(product, planes, slab, 128)
    bounds[1] = largest((2.0 * spread_1 * total + weight_1) * inverse_1, 64)
    spread_1w[...], weight_1w[...], inverse_1w[...] = spread_1, weight_1, inverse_1

    both = rows_apply(gather_rows[...], jnp.concatenate([spread_1, weight_1], axis=1))
    spread_2 = lanes_apply(both[:, :128], fold[...]) * 0.125
    weight_2 = lanes_apply(both[:, 128:], fold[...])
    inverse_2 = jnp.where(spread_2 > 0.0, 1.0 / (4.0 * coarse_diag[...] * spread_2 * spread_2 + weight_2), 0.0)
    rows, planes = rows // 2, planes // 2
    single = spread_2.reshape(planes, 3, rows, 128)[:, 0].reshape(planes * rows, 128)
    total = shifted_sum(banded_stacked(coarse_bound[:, : 3 * planes * rows], single), planes, 3 * rows, 128)
    bounds[2] = largest((4.0 * spread_2 * total + weight_2) * inverse_2, 32)
    spread_2w[...], weight_2w[...], inverse_2w[...] = spread_2, weight_2, inverse_2


def fine_operator(matrix, scale, mass, values):
    total = fine_stencil(matrix, scale[:, None] * values)
    return scale[1:-1][:, None] * total + mass[:, None] * values[1:-1]


def inner_power(scale_w, mass_w, inverse_w, matrix, values):
    planes = scale_w.shape[0] - 2 * PAD
    near = slice(PAD - 1, PAD + planes + 1)
    return fine_operator(matrix, scale_w[near], mass_w[PAD : PAD + planes], inverse_w[near] * values[near])


def power_kernel(scale_w, mass_w, inverse_w, source_w, fine, power):
    planes, shape = scale_w.shape[0] - 2 * PAD, power.shape[1:]
    power[:PAD] = jnp.zeros((PAD,) + shape, F32)
    power[PAD + planes :] = jnp.zeros((PAD,) + shape, F32)
    power[PAD : PAD + planes] = inner_power(scale_w, mass_w, inverse_w, fine, source_w)


def restrict_kernel(scale_w, mass_w, inverse_w, source_w, power_1, fine, squeeze, power_2, basis, held):
    planes, rows = scale_w.shape[0] - 2 * PAD, scale_w.shape[1]
    power_kernel(scale_w, mass_w, inverse_w, power_1, fine, power_2)
    third = inner_power(scale_w, mass_w, inverse_w, fine, power_2)
    inner = slice(PAD, PAD + planes)
    size = planes // 2 * 3 * rows
    for at, values in enumerate((source_w[inner], power_1[inner], power_2[inner], third)):
        pairs = paired_rows(held.at[at], paired_planes(values).reshape(size, LANES))
        basis[at] = lanes_apply(pairs, squeeze[...])


def chebyshev_scalars(bound, ratio):
    lower = bound / ratio
    return 0.5 * (bound + lower), 0.5 * (bound - lower)


def scaled(coeff, values):
    lanes = values.shape[-1]
    if lanes != 128:
        coeff = jnp.concatenate([coeff] * (lanes // 128), axis=1)
    flat = values.reshape(-1, 8, lanes)
    return (coeff[None] * flat).reshape(values.shape)


def chebyshev(residue, degree, inverse, bound, ratio, operate, keep):
    centre, spread = chebyshev_scalars(bound, ratio)
    sigma = centre / spread
    rho = 1.0 / sigma
    direction = scaled(1.0 / centre, inverse * residue)
    total = direction
    for step in range(degree):
        if step < degree - 1 or keep:
            residue = residue - operate(direction)
        if step < degree - 1:
            rho_next = 1.0 / (2.0 * sigma - rho)
            direction = scaled(rho_next * rho, direction) + scaled(2.0 * rho_next / spread, inverse * residue)
            total = total + direction
            rho = rho_next
    return total, residue


def final_kernel(
    bounds_a, bounds_b, source_w, scale_w, mass_w, inverse_w, power_1, power_2, basis,
    spread_1w, weight_1w, inverse_1w, spread_2w, weight_2w, inverse_2w,
    fine, mid, coarse, gather_rows, spread_rows, expand, fold, unfold, stretch, result, lifted_w, answer_w,
):
    rows = scale_w.shape[1] // 2
    planes = (scale_w.shape[0] - 2 * PAD) // 2
    slab = 3 * rows
    size = planes * slab
    small = size // 4
    gz, gy = lax.axis_index("gz"), lax.axis_index("gy")
    bounds = jnp.maximum(bounds_a[...], bounds_b[...])

    centre, spread = chebyshev_scalars(bounds[0], SMOOTH_RATIO)
    sigma = centre / spread
    rho = 1.0 / sigma
    rho_next = 1.0 / (2.0 * sigma - rho)
    keep, push = rho_next * rho, 2.0 * rho_next / spread
    beta = push / centre
    gamma = 1.0 / centre + keep / centre + push
    omega = (4.0 / 3.0) / bounds[0]

    source_1 = (
        basis[0]
        - scaled(gamma + omega, basis[1])
        + scaled(beta + omega * gamma, basis[2])
        - scaled(omega * beta, basis[3])
    )
    spread_1, weight_1, inverse_1 = spread_1w[...], weight_1w[...], inverse_1w[...]
    spread_2, weight_2, inverse_2 = spread_2w[...], weight_2w[...], inverse_2w[...]

    def operate_1(values):
        product = banded(mid[0, :, :size], mid[1, :, :size], spread_1 * values)
        return 2.0 * spread_1 * shifted_sum(product, planes, slab, 128) + weight_1 * values

    def operate_2(values):
        product = banded_stacked(coarse[:, : 3 * small], spread_2 * values)
        return 4.0 * spread_2 * shifted_sum(product, planes // 2, slab // 2, 128) + weight_2 * values

    omega_1 = (4.0 / 3.0) / bounds[1]
    iterate, residue = chebyshev(source_1, 2, inverse_1, bounds[1], SMOOTH_RATIO, operate_1, True)
    smoothed = residue - scaled(omega_1, operate_1(inverse_1 * residue))
    source_2 = lanes_apply(rows_apply(gather_rows[...], smoothed), fold[...])
    error_2, _ = chebyshev(source_2, COARSE_ITERS, inverse_2, bounds[2], COARSE_RATIO, operate_2, False)
    lifted = lanes_apply(error_2, unfold[...])
    lifted = dot(spread_rows[...], jnp.concatenate(split(lifted), axis=0))
    iterate = iterate + lifted - scaled(omega_1, inverse_1 * operate_1(lifted))
    residue = source_1 - operate_1(iterate)
    more, _ = chebyshev(residue, 2, inverse_1, bounds[1], SMOOTH_RATIO, operate_1, False)
    error_1 = iterate + more

    lifted_w[0:2] = jnp.zeros((2, slab, 128), F32)
    lifted_w[planes + 2 : planes + 4] = jnp.zeros((2, slab, 128), F32)
    lifted_w[2 : planes + 2] = error_1.reshape(planes, slab, 128)
    near = lifted_w[pl.ds(2 * gz, 6)].reshape(6 * slab, 128)
    wide = lanes_apply(near, stretch[...]).reshape(6, slab, LANES)
    side = jnp.concatenate([wide[plane] for plane in range(6)], axis=1)
    tall = dot(expand[...], jnp.concatenate(split(side), axis=0))
    slabs = [tall[:, plane * LANES : plane * LANES + LANES] for plane in range(6)]
    error = jnp.stack([slabs[(plane + 1) // 2] for plane in range(10)], axis=0).reshape(10, 3, 2 * rows, LANES)

    def near_own(ref, reach):
        return ref[pl.ds(4 * gz + PAD - reach, 4 + 2 * reach)]

    scale, mass, inverse = near_own(scale_w, 3), near_own(mass_w, 2), near_own(inverse_w, 2)
    source = near_own(source_w, 2)
    image = fine_operator(fine, scale, mass, error)
    iterate = inverse * (scaled(gamma, source) - scaled(beta, near_own(power_1, 2)) - scaled(omega, image)) + error[1:9]
    residue = source[1:7] - fine_operator(fine, scale[1:9], mass[1:7], iterate)
    direction = scaled(1.0 / centre, inverse[1:7] * residue)
    last = residue[1:5] - fine_operator(fine, scale[2:8], mass[2:6], direction)
    answer = iterate[2:6] + scaled(1.0 + keep, direction[1:5]) + scaled(push, inverse[2:6] * last)
    answer_w[...] = answer[:, :, :, :128]
    for comp in range(3):
        result[comp] = answer_w[:, comp, pl.ds(pl.multiple_of(8 * gy, 8), 8), :]


def swap_pairs(counts, target):
    def number(place):
        return (place[0] * counts[1] + place[1]) * counts[2] + place[2]

    places = [(x, y, z) for x in range(counts[0]) for y in range(counts[1]) for z in range(counts[2])]
    return [(number(place), number(target(*place))) for place in places]


def odd_partner(index):
    return index - 1 if index % 2 == 0 else index + 1


def on_device(right_side, stiff_scale, nodal_mass, stencil_blocks):
    counts = tuple(lax.axis_size(axis) for axis in AXES)
    gxs, gys, gzs = counts
    blocks = stencil_blocks.reshape(243)

    def send(values, target):
        return lax.ppermute(values, AXES, swap_pairs(counts, target))

    def x_second(x, y, z):
        return (x, y, z ^ 1) if x in (0, gxs - 1) else (odd_partner(x), y, z)

    rows, planes = 8 * gys, 4 * gzs
    grant = 20 if planes * rows <= 256 else 48
    slab = 3 * rows
    group = group_of(slab)
    size_1, count_1 = planes * slab // 4, planes * rows // 4
    size_2, count_2 = size_1 // 4, count_1 // 4
    (
        fine, fine_bound, mid, mid_bound, coarse, coarse_bound, coarse_diag,
        gather_rows, spread_rows, expand, fold, unfold, squeeze, stretch,
    ) = call(
        functools.partial(matrices_kernel, rows, planes),
        [
            ((2, group * 3 * slab, up128((group + 2) * slab)), BF16),
            ((group * 3 * slab, up128(3 * (group + 2) * rows)), BF16),
            ((2, 3 * size_1, up128(size_1)), BF16),
            ((3 * size_1, up128(3 * count_1)), BF16),
            ((3 * size_2, up128(3 * size_2)), BF16),
            ((3 * size_2, up128(3 * count_2)), BF16),
            ((size_2, 128), F32),
            ((size_2, size_1), BF16),
            ((size_1, 2 * size_2), BF16),
            ((slab, slab), BF16),
            ((256, 128), BF16),
            ((256, 128), BF16),
            ((2 * LANES, 128), BF16),
            ((256, LANES), BF16),
        ],
        specs=[SM],
        flops=5000000000,
        size=8000000,
        grant=grant,
    )(blocks)

    half = ((10, 8, 128), F32)
    main, send_a, send_b = call(
        pack_kernel,
        [((20, 8, 128), F32), half, half],
        specs=[HB] * 3,
        scratch=[pltpu.SemaphoreType.DMA((5,))],
        grant=8,
    )(right_side, stiff_scale, nodal_mass)
    got_a = send(send_a, lambda x, y, z: (x ^ 1, y, z))
    got_b = send(send_b, x_second)
    (wide,) = call(functools.partial(widen_kernel, gxs), [((20, 8, LANES), F32)], grant=8)(main, got_a, got_b)
    ordered = not (gys == 2 and gzs == 4)
    if ordered:
        gathered = [lax.all_gather(wide, ("gz", "gy"), tiled=False)]
    else:
        near = [
            wide,
            send(wide, lambda x, y, z: (x, y, z ^ 2)),
            send(wide, lambda x, y, z: (x, y ^ 1, z)),
            send(wide, lambda x, y, z: (x, y ^ 1, z ^ 2)),
        ]
        near[3], fine = lax.optimization_barrier((near[3], fine))
        gathered = [block[None] for block in near + [send(block, lambda x, y, z: (x, y, z ^ 1)) for block in near]]

    field = ((planes + 2 * PAD, 3, rows, LANES), F32)
    single = ((planes + 2 * PAD, rows, LANES), F32)
    source_w, scale_w, mass_w, inverse_w, *levels, bounds = call(
        functools.partial(window_kernel, gys, ordered),
        [field, single, single, field] + [((size_1, 128), F32)] * 3 + [((size_2, 128), F32)] * 3 + [((3, 8, 128), F32)],
        specs=[SM] + [VM] * (len(gathered) + 7),
        scratch=[pltpu.VMEM((2, 2, planes * rows // 2, 128), F32)],
        grant=grant,
    )(blocks, *gathered, fine_bound, mid_bound, coarse_bound, coarse_diag, gather_rows, fold, squeeze)

    step = 4
    while step < gxs:
        bounds = jnp.maximum(bounds, send(bounds, lambda x, y, z: (x ^ step, y, z)))
        step *= 2
    bounds = jnp.maximum(bounds, send(bounds, lambda x, y, z: (x ^ 1, y, z ^ 1)))
    other = send(bounds, lambda x, y, z: (x ^ 2, y, z ^ 1))
    (power_1,) = call(power_kernel, [field], flops=1000000000, size=4000000, grant=grant)(scale_w, mass_w, inverse_w, source_w, fine)
    power_2, basis = call(
        restrict_kernel,
        [field, ((4, size_1, 128), F32)],
        scratch=[pltpu.VMEM((4, 2, 2 * size_1, 128), F32)],
        flops=2000000000,
        size=8000000,
        grant=grant,
    )(scale_w, mass_w, inverse_w, source_w, power_1, fine, squeeze)
    (result,) = call(
        final_kernel,
        [(right_side.shape, F32)],
        scratch=[
            pltpu.VMEM((planes // 2 + 4, slab // 2, 128), F32),
            pltpu.VMEM((4, 3, rows, 128), F32),
        ],
        grant=grant,
    )(
        bounds, other, source_w, scale_w, mass_w, inverse_w, power_1, power_2, basis, *levels,
        fine, mid, coarse, gather_rows, spread_rows, expand, fold, unfold, stretch,
    )
    return result


def solution(mesh):
    placed = (P(None, "gz", "gy", "gx"), P("gz", "gy", "gx"), P("gz", "gy", "gx"), P())
    return jax.shard_map(
        on_device, mesh=mesh, in_specs=placed, out_specs=P(None, "gz", "gy", "gx"), check_vma=False
    )
```

time: 716 us -> 40.1 us (0.06)
  the two profiles are of different devices: /device:TPU:26 before, /device:TPU:0 now
where the time goes in v2:
time: 40.1 us; the launch traced here: 39.8 us
  Pallas kernels  18.5 us (46%)
  starting transfers between devices  12.6 us (31%)
  waiting for transfers between devices  5.4 us (13%)
  local copies, waits for them, and re-layouts  3.2 us (8%)
    pallas_call x7, Pallas kernels, run(): pl.pallas_call(kernel, out_shape=outs, in_specs=specs or [VM] * len(args)...  18.5 us
    ppermute x11, starting transfers between devices, send(): return lax.ppermute(values, AXES, swap_pairs(counts, target))  12.6 us
    ppermute x11, waiting for transfers between devices, send(): return lax.ppermute(values, AXES, swap_pairs(counts, target))  5.4 us
    unnamed x7, local copies, waits for them, and re-layouts  3.03 us
  transfers between devices with their start and end apart: 11, of which 6 were waited for; matrix products, arithmetic and copies ran while one was open for 2% of the time, Pallas kernels for 18%

profile of v2, /device:TPU:0, one launch (start us, length us, event | category | flops | bytes accessed | tf_op | source)
XLA Modules:
  0.0 39.8 jit_solution(7372057012994095389)
XLA Ops:
  0.0 0.8 %copy-done = f32[3,4,8,128]{3,2,1,0:T(8,128)S(1)} copy-done((f32[3,4,8,128]{3,2,1,0:T(8,128)S(1)}, f32[3,4,8,128]{3,2,1,0:T(8,128)}, u32[]{:S(2)}) %copy-start) | copy-done | bytes 49176
  0.8 0.7 %copy-done.1 = f32[4,8,128]{2,1,0:T(8,128)S(1)} copy-done((f32[4,8,128]{2,1,0:T(8,128)S(1)}, f32[4,8,128]{2,1,0:T(8,128)}, u32[]{:S(2)}) %copy-start.1) | copy-done | bytes 16408
  1.5 0.7 %copy-done.2 = f32[4,8,128]{2,1,0:T(8,128)S(1)} copy-done((f32[4,8,128]{2,1,0:T(8,128)S(1)}, f32[4,8,128]{2,1,0:T(8,128)}, u32[]{:S(2)}) %copy-start.2) | copy-done | bytes 16408
  2.2 0.2 shard_map.46
  2.5 3.1 %collective-permute-start = (f32[10,8,128]{2,1,0:T(8,128)S(1)}, f32[10,8,128]{2,1,0:T(8,128)S(1)}, u32[]{:S(2)}, u32[]{:S(2)}) collective-permute-start(f32[10,8,128]{2,1,0:T(8,128)S(1)} %get-tuple-element.38), channel_id=1, source_target_pairs={{0,8},{1,9},{2,10},{3,11},{4,12},{5,13},{6,14},{7,15},{8,0},{9,1},... | collective-permute-start | bytes 122888 | tf_op jit(solution)/shard_map/ppermute | solution.py:549
  5.5 0.8 %copy.5 = f32[27,3,3]{2,1,0:T(4,128)S(1)} copy(f32[27,3,3]{0,2,1:T(4,128)} %param.7) | data formatting | bytes 1944 | tf_op args[3]
  6.3 0.2 reshape.3.blocks
  6.5 1.0 %collective-permute-done.got_a = f32[10,8,128]{2,1,0:T(8,128)S(1)} collective-permute-done((f32[10,8,128]{2,1,0:T(8,128)S(1)}, f32[10,8,128]{2,1,0:T(8,128)S(1)}, u32[]{:S(2)}, u32[]{:S(2)}) %collective-permute-start) | collective-permute-done | bytes 40992 | tf_op jit(solution)/shard_map/ppermute | solution.py:549
  7.5 0.0 collective-permute-done.1.got_b
  7.5 0.1 shard_map.47
  7.6 3.0 %collective-permute-start.4 = (f32[20,8,256]{2,1,0:T(8,128)S(1)}, f32[20,8,256]{2,1,0:T(8,128)S(1)}, u32[]{:S(2)}, u32[]{:S(2)}) collective-permute-start(f32[20,8,256]{2,1,0:T(8,128)S(1)} %shard_map.47), channel_id=1, source_target_pairs={{0,6},{1,7},{2,4},{3,5},{4,2},{5,3},{6,0},{7,1},{8,14},{9,15},{10,... | collective-permute-start | bytes 491528 | tf_op jit(solution)/shard_map/ppermute | solution.py:549
  10.6 0.5 %collective-permute-start.2 = (f32[20,8,256]{2,1,0:T(8,128)S(1)}, f32[20,8,256]{2,1,0:T(8,128)S(1)}, u32[]{:S(2)}, u32[]{:S(2)}) collective-permute-start(f32[20,8,256]{2,1,0:T(8,128)S(1)} %shard_map.47), channel_id=1, source_target_pairs={{0,2},{1,3},{2,0},{3,1},{4,6},{5,7},{6,4},{7,5},{8,10},{9,11},{10,... | collective-permute-start | bytes 491528 | tf_op jit(solution)/shard_map/ppermute | solution.py:549
  11.1 0.1 collective-permute-start.3
  11.2 3.3 %shard_map.48 = (bf16[2,432,256]{2,1,0:T(8,128)(2,1)S(1)}, bf16[432,256]{1,0:T(8,128)(2,1)S(1)}, bf16[2,576,256]{2,1,0:T(8,128)(2,1)S(1)}, bf16[576,256]{1,0:T(8...) custom-call(f32[243]{0:T(256)S(1)} %reshape.3.blocks), custom_call_target="tpu_custom_call" | custom-call | flops 5000000000 | bytes 8000000 | tf_op jit(solution)/shard_map/pallas_call | solution.py:27
  14.5 0.1 collective-permute-start.5
  14.6 1.1 %collective-permute-done.4 = f32[20,8,256]{2,1,0:T(8,128)S(1)} collective-permute-done((f32[20,8,256]{2,1,0:T(8,128)S(1)}, f32[20,8,256]{2,1,0:T(8,128)S(1)}, u32[]{:S(2)}, u32[]{:S(2)}) %collective-permute-start.4) | collective-permute-done | bytes 163872 | tf_op jit(solution)/shard_map/ppermute | solution.py:549
  15.7 0.0 collective-permute-start.8
  15.7 2.1 %collective-permute-done.2 = f32[20,8,256]{2,1,0:T(8,128)S(1)} collective-permute-done((f32[20,8,256]{2,1,0:T(8,128)S(1)}, f32[20,8,256]{2,1,0:T(8,128)S(1)}, u32[]{:S(2)}, u32[]{:S(2)}) %collective-permute-start.2) | collective-permute-done | bytes 163872 | tf_op jit(solution)/shard_map/ppermute | solution.py:549
  17.8 0.0 collective-permute-start.6
  17.8 0.0 collective-permute-done.3
  17.8 0.5 %collective-permute-start.7 = (f32[20,8,256]{2,1,0:T(8,128)S(1)}, f32[20,8,256]{2,1,0:T(8,128)S(1)}, u32[]{:S(2)}, u32[]{:S(2)}) collective-permute-start(f32[20,8,256]{2,1,0:T(8,128)S(1)} %collective-permute-done.3), channel_id=1, source_target_pairs={{0,1},{1,0},{2,3},{3,2},{4,5},{5,4},{6,7},{7,6},{8,9},{9,8},{10,11... | collective-permute-start | bytes 491528 | tf_op jit(solution)/shard_map/ppermute | solution.py:549
  18.3 0.0 collective-permute-done.5
  18.3 0.0 collective-permute-done.8
  18.3 0.9 %collective-permute-done.6 = f32[20,8,256]{2,1,0:T(8,128)S(1)} collective-permute-done((f32[20,8,256]{2,1,0:T(8,128)S(1)}, f32[20,8,256]{2,1,0:T(8,128)S(1)}, u32[]{:S(2)}, u32[]{:S(2)}) %collective-permute-start.6) | collective-permute-done | bytes 163872 | tf_op jit(solution)/shard_map/ppermute | solution.py:549
  19.2 0.2 collective-permute-done.7
  19.4 2.1 %shard_map.49 = (f32[22,3,16,256]{3,2,1,0:T(8,128)S(1)}, f32[22,16,256]{2,1,0:T(8,128)S(1)}, f32[22,16,256]{2,1,0:T(8,128)S(1)}, f32[22,3,16,256]{3,2,1,0:T(8,12...) custom-call(f32[243]{0:T(256)S(1)} %reshape.3.blocks, ...), custom_call_target="tpu_custom_call" | custom-call | flops 1000000 | bytes 100000 | tf_op jit(solution)/shard_map/pallas_call | solution.py:27
  21.5 2.6 %collective-permute-start.9 = (f32[3,8,128]{2,1,0:T(8,128)S(1)}, f32[3,8,128]{2,1,0:T(8,128)S(1)}, u32[]{:S(2)}, u32[]{:S(2)}) collective-permute-start(f32[3,8,128]{2,1,0:T(8,128)S(1)} %get-tuple-element.49), channel_id=1, source_target_pairs={{0,9},{1,8},{2,11},{3,10},{4,13},{5,12},{6,15},{7,14},{8,1},{9,0},... | collective-permute-start | bytes 36872 | tf_op jit(solution)/shard_map/ppermute | solution.py:549
  24.1 1.3 %shard_map.50.power_1 = f32[22,3,16,256]{3,2,1,0:T(8,128)S(1)} custom-call(f32[22,16,256]{2,1,0:T(8,128)S(1)} %get-tuple-element.51.scale_w, f32[22,16,256]{2,1,0:T(8,128)S(1)} %get-tuple-element.52.mass_w, f32[22,3,16,256]{3,2,1,0:T(8,128)S(1)} %get-tuple-element.53.inverse_w, f32[22,3,16,256]{3,2,1,0:T(8,128)S(1)} %get-tuple-element.50.source_w, ...), custom_call_target="tpu_custom_call" | custom-call | flops 1000000000 | bytes 4000000 | tf_op jit(solution)/shard_map/pallas_call | solution.py:27
  25.4 0.1 collective-permute-done.9
  25.5 2.7 %collective-permute-start.10 = (f32[3,8,128]{2,1,0:T(8,128)S(1)}, f32[3,8,128]{2,1,0:T(8,128)S(1)}, u32[]{:S(2)}, u32[]{:S(2)}) collective-permute-start(f32[3,8,128]{2,1,0:T(8,128)S(1)} %max.3.bounds_a), channel_id=1, source_target_pairs={{0,17},{1,16},{2,19},{3,18},{4,21},{5,20},{6,23},{7,22},{8,25},{9,... | collective-permute-start | bytes 36872 | tf_op jit(solution)/shard_map/ppermute | solution.py:549
  28.2 2.6 %shard_map.51 = (f32[22,3,16,256]{3,2,1,0:T(8,128)S(1)}, f32[4,192,128]{2,1,0:T(8,128)S(1)}) custom-call(f32[22,16,256]{2,1,0:T(8,128)S(1)} %get-tuple-element.51.scale_w, f32[22,16,256]{2,1,0:T(8,128)S(1)} %get-tuple-element.52.mass_w, f32[22,3,16,256]{3,2,1,0:T(8,128)S(1)} %get-tuple-element.53.inverse_w, ...), custom_call_target="tpu_custom_call" | custom-call | flops 2000000000 | bytes 8000000 | tf_op jit(solution)/shard_map/pallas_call | solution.py:27
  30.8 9.0 %shard_map.52 = f32[3,4,8,128]{3,2,1,0:T(8,128)} custom-call(f32[3,8,128]{2,1,0:T(8,128)S(1)} %max.3.bounds_a, f32[3,8,128]{2,1,0:T(8,128)S(1)} %collective-permute-done.10.bounds_b, f32[22,3,16,256]{3,2,1,0:T(8,128)S(1)} %get-tuple-element.50.source_w, f32[22,16,256]{2,1,0:T(8,128)S(1)} %get-tuple-element.51.scale_w, ...), custom_call_target="tpu_custom_call" | custom-call | flops 1000000 | bytes 100000 | tf_op jit(solution)/shard_map/pallas_call | solution.py:27
  (6 shorter events, 0.0 us)
Async XLA Ops:
  0.0 0.8 %copy-start = (f32[3,4,8,128]{3,2,1,0:T(8,128)S(1)}, f32[3,4,8,128]{3,2,1,0:T(8,128)}, u32[]{:S(2)}) copy-start(f32[3,4,8,128]{3,2,1,0:T(8,128)} %source.1) | copy-start | bytes 147460
  0.8 0.7 %copy-start.1 = (f32[4,8,128]{2,1,0:T(8,128)S(1)}, f32[4,8,128]{2,1,0:T(8,128)}, u32[]{:S(2)}) copy-start(f32[4,8,128]{2,1,0:T(8,128)} %scale.1) | copy-start | bytes 49156
  1.5 0.7 %copy-start.2 = (f32[4,8,128]{2,1,0:T(8,128)S(1)}, f32[4,8,128]{2,1,0:T(8,128)}, u32[]{:S(2)}) copy-start(f32[4,8,128]{2,1,0:T(8,128)} %mass.1) | copy-start | bytes 49156
  2.5 5.1 %collective-permute-start = (f32[10,8,128]{2,1,0:T(8,128)S(1)}, f32[10,8,128]{2,1,0:T(8,128)S(1)}, u32[]{:S(2)}, u32[]{:S(2)}) collective-permute-start(f32[10,8,128]{2,1,0:T(8,128)S(1)} %get-tuple-element.38), channel_id=1, source_target_pairs={{0,8},{1,9},{2,10},{3,11},{4,12},{5,13},{6,14},{7,15},{8,0},{9,1},... | collective-permute-start | bytes 122888 | tf_op jit(solution)/shard_map/ppermute | solution.py:549
  5.5 2.0 %collective-permute-start.1 = (f32[10,8,128]{2,1,0:T(8,128)S(1)}, f32[10,8,128]{2,1,0:T(8,128)S(1)}, u32[]{:S(2)}, u32[]{:S(2)}) collective-permute-start(f32[10,8,128]{2,1,0:T(8,128)S(1)} %get-tuple-element.39), channel_id=1, source_target_pairs={{0,1},{1,0},{2,3},{3,2},{4,5},{5,4},{6,7},{7,6},{8,16},{9,17},{10,... | collective-permute-start | bytes 122888 | tf_op jit(solution)/shard_map/ppermute | solution.py:549
  7.6 8.1 %collective-permute-start.4 = (f32[20,8,256]{2,1,0:T(8,128)S(1)}, f32[20,8,256]{2,1,0:T(8,128)S(1)}, u32[]{:S(2)}, u32[]{:S(2)}) collective-permute-start(f32[20,8,256]{2,1,0:T(8,128)S(1)} %shard_map.47), channel_id=1, source_target_pairs={{0,6},{1,7},{2,4},{3,5},{4,2},{5,3},{6,0},{7,1},{8,14},{9,15},{10,... | collective-permute-start | bytes 491528 | tf_op jit(solution)/shard_map/ppermute | solution.py:549
  10.6 7.2 %collective-permute-start.2 = (f32[20,8,256]{2,1,0:T(8,128)S(1)}, f32[20,8,256]{2,1,0:T(8,128)S(1)}, u32[]{:S(2)}, u32[]{:S(2)}) collective-permute-start(f32[20,8,256]{2,1,0:T(8,128)S(1)} %shard_map.47), channel_id=1, source_target_pairs={{0,2},{1,3},{2,0},{3,1},{4,6},{5,7},{6,4},{7,5},{8,10},{9,11},{10,... | collective-permute-start | bytes 491528 | tf_op jit(solution)/shard_map/ppermute | solution.py:549
  11.1 6.7 %collective-permute-start.3 = (f32[20,8,256]{2,1,0:T(8,128)S(1)}, f32[20,8,256]{2,1,0:T(8,128)S(1)}, u32[]{:S(2)}, u32[]{:S(2)}) collective-permute-start(f32[20,8,256]{2,1,0:T(8,128)S(1)} %shard_map.47), channel_id=1, source_target_pairs={{0,4},{1,5},{2,6},{3,7},{4,0},{5,1},{6,2},{7,3},{8,12},{9,13},{10,... | collective-permute-start | bytes 491528 | tf_op jit(solution)/shard_map/ppermute | solution.py:549
  14.5 3.8 %collective-permute-start.5 = (f32[20,8,256]{2,1,0:T(8,128)S(1)}, f32[20,8,256]{2,1,0:T(8,128)S(1)}, u32[]{:S(2)}, u32[]{:S(2)}) collective-permute-start(f32[20,8,256]{2,1,0:T(8,128)S(1)} %shard_map.47), channel_id=1, source_target_pairs={{0,1},{1,0},{2,3},{3,2},{4,5},{5,4},{6,7},{7,6},{8,9},{9,8},{10,11... | collective-permute-start | bytes 491528 | tf_op jit(solution)/shard_map/ppermute | solution.py:549
  15.7 2.6 %collective-permute-start.8 = (f32[20,8,256]{2,1,0:T(8,128)S(1)}, f32[20,8,256]{2,1,0:T(8,128)S(1)}, u32[]{:S(2)}, u32[]{:S(2)}) collective-permute-start(f32[20,8,256]{2,1,0:T(8,128)S(1)} %collective-permute-done.4), channel_id=1, source_target_pairs={{0,1},{1,0},{2,3},{3,2},{4,5},{5,4},{6,7},{7,6},{8,9},{9,8},{10,11... | collective-permute-start | bytes 491528 | tf_op jit(solution)/shard_map/ppermute | solution.py:549
  17.8 1.4 %collective-permute-start.6 = (f32[20,8,256]{2,1,0:T(8,128)S(1)}, f32[20,8,256]{2,1,0:T(8,128)S(1)}, u32[]{:S(2)}, u32[]{:S(2)}) collective-permute-start(f32[20,8,256]{2,1,0:T(8,128)S(1)} %collective-permute-done.2), channel_id=1, source_target_pairs={{0,1},{1,0},{2,3},{3,2},{4,5},{5,4},{6,7},{7,6},{8,9},{9,8},{10,11... | collective-permute-start | bytes 491528 | tf_op jit(solution)/shard_map/ppermute | solution.py:549
  17.8 1.6 %collective-permute-start.7 = (f32[20,8,256]{2,1,0:T(8,128)S(1)}, f32[20,8,256]{2,1,0:T(8,128)S(1)}, u32[]{:S(2)}, u32[]{:S(2)}) collective-permute-start(f32[20,8,256]{2,1,0:T(8,128)S(1)} %collective-permute-done.3), channel_id=1, source_target_pairs={{0,1},{1,0},{2,3},{3,2},{4,5},{5,4},{6,7},{7,6},{8,9},{9,8},{10,11... | collective-permute-start | bytes 491528 | tf_op jit(solution)/shard_map/ppermute | solution.py:549
  21.5 4.0 %collective-permute-start.9 = (f32[3,8,128]{2,1,0:T(8,128)S(1)}, f32[3,8,128]{2,1,0:T(8,128)S(1)}, u32[]{:S(2)}, u32[]{:S(2)}) collective-permute-start(f32[3,8,128]{2,1,0:T(8,128)S(1)} %get-tuple-element.49), channel_id=1, source_target_pairs={{0,9},{1,8},{2,11},{3,10},{4,13},{5,12},{6,15},{7,14},{8,1},{9,0},... | collective-permute-start | bytes 36872 | tf_op jit(solution)/shard_map/ppermute | solution.py:549
  25.5 5.3 %collective-permute-start.10 = (f32[3,8,128]{2,1,0:T(8,128)S(1)}, f32[3,8,128]{2,1,0:T(8,128)S(1)}, u32[]{:S(2)}, u32[]{:S(2)}) collective-permute-start(f32[3,8,128]{2,1,0:T(8,128)S(1)} %max.3.bounds_a), channel_id=1, source_target_pairs={{0,17},{1,16},{2,19},{3,18},{4,21},{5,20},{6,23},{7,22},{8,25},{9,... | collective-permute-start | bytes 36872 | tf_op jit(solution)/shard_map/ppermute | solution.py:549

commit v3 on v2

--- a/solution.py
+++ b/solution.py
@@ -14,7 +14,6 @@
 F32, BF16 = jnp.float32, jnp.bfloat16
 VM = pl.BlockSpec(memory_space=pltpu.VMEM)
 SM = pl.BlockSpec(memory_space=pltpu.SMEM)
-HB = pl.BlockSpec(memory_space=pltpu.HBM)
 LANES = 256
 PAD = 3
 
@@ -67,6 +66,13 @@
 def banded(matrix_high, matrix_low, values):
     high, low = split(values)
     return dot(matrix_high, high) + dot(matrix_low, high) + dot(matrix_high, low)
+
+
+def banded_beside(matrix_high, matrix_low, values):
+    high, low = split(values)
+    width = values.shape[1]
+    product = dot(matrix_high, jnp.concatenate([high, low], axis=1))
+    return product[:, :width] + product[:, width:] + dot(matrix_low, high)
 
 
 def banded_stacked(matrix, values):
@@ -260,23 +266,14 @@
     return jnp.where(low, second, first), jnp.where(low, first, second)
 
 
-def pack_kernel(source, scale, mass, main, send_a, send_b, sems):
-    copies = [
-        pltpu.make_async_copy(source.at[comp], main.at[pl.ds(comp * 4, 4)], sems.at[comp]) for comp in range(3)
-    ]
-    copies.append(pltpu.make_async_copy(scale, main.at[pl.ds(12, 4)], sems.at[3]))
-    copies.append(pltpu.make_async_copy(mass, main.at[pl.ds(16, 4)], sems.at[4]))
-    for copy in copies:
-        copy.start()
-    for copy in copies:
-        copy.wait()
+def pack_kernel(main, send_a, send_b):
     high, low = halves(main[...], iota((10, 8, 128), 2) < 64)
     even = lax.rem(lax.axis_index("gx"), 2) == 0
     send_a[...] = jnp.where(even, high, low)
     send_b[...] = jnp.where(even, low, high)
 
 
-def widen_kernel(count, main, got_a, got_b, wide):
+def widen_kernel(count, main, got_b, got_a, wide):
     index = lax.axis_index("gx")
     even = lax.rem(index, 2) == 0
     first, second = got_a[...], got_b[...]
@@ -483,7 +480,7 @@
     spread_2, weight_2, inverse_2 = spread_2w[...], weight_2w[...], inverse_2w[...]
 
     def operate_1(values):
-        product = banded(mid[0, :, :size], mid[1, :, :size], spread_1 * values)
+        product = banded_beside(mid[0, :, :size], mid[1, :, :size], spread_1 * values)
         return 2.0 * spread_1 * shifted_sum(product, planes, slab, 128) + weight_1 * values
 
     def operate_2(values):
@@ -585,16 +582,11 @@
     )(blocks)
 
     half = ((10, 8, 128), F32)
-    main, send_a, send_b = call(
-        pack_kernel,
-        [((20, 8, 128), F32), half, half],
-        specs=[HB] * 3,
-        scratch=[pltpu.SemaphoreType.DMA((5,))],
-        grant=8,
-    )(right_side, stiff_scale, nodal_mass)
+    main = jnp.concatenate([right_side.reshape(12, 8, 128), stiff_scale, nodal_mass], axis=0)
+    send_a, send_b = call(pack_kernel, [half, half], grant=8)(main)
+    got_b = send(send_b, x_second)
     got_a = send(send_a, lambda x, y, z: (x ^ 1, y, z))
-    got_b = send(send_b, x_second)
-    (wide,) = call(functools.partial(widen_kernel, gxs), [((20, 8, LANES), F32)], grant=8)(main, got_a, got_b)
+    (wide,) = call(functools.partial(widen_kernel, gxs), [((20, 8, LANES), F32)], grant=8)(main, got_b, got_a)
     ordered = not (gys == 2 and gzs == 4)
     if ordered:
         gathered = [lax.all_gather(wide, ("gz", "gy"), tiled=False)]

time: 40.1 us -> 35.9 us (0.90)
  local copies, waits for them, and re-layouts: 3.2 us -> 0.97 us
  Pallas kernels: 18.5 us -> 16.7 us
  other arithmetic: 0.01 us -> 0.84 us
  waiting for transfers between devices: 5.4 us -> 4.6 us
    unnamed x7 -> x1, local copies, waits for them, and re-layouts: 3.03 us -> 0.8 us
    pallas_call x7, Pallas kernels: 18.5 us -> 16.7 us  [run(): pl.pallas_call(kernel, out_shape=outs, in_specs=specs or [VM] * len(args)...]
    concatenate x0 -> x1, other arithmetic: none -> 0.84 us  [on_device(): jnp.concatenate([right_side.reshape(12, 8, 128), stiff_scale, nodal_mass]...]
    ppermute x11, waiting for transfers between devices: 5.4 us -> 4.6 us  [send(): return lax.ppermute(values, AXES, swap_pairs(counts, target))]
  transfers between devices with their start and end apart: 11 -> 11, of which waited for: 6 -> 6; matrix products, arithmetic and copies ran while one was open for 2% -> 3% of each run, Pallas kernels for 18% -> 20%
where the time goes in v3:
time: 35.9 us; the launch traced here: 35.7 us
  Pallas kernels  16.7 us (47%)
  starting transfers between devices  12.4 us (35%)
  waiting for transfers between devices  4.6 us (13%)
  local copies, waits for them, and re-layouts  0.97 us (3%)
  other arithmetic  0.84 us (2%)
    pallas_call x7, Pallas kernels, run(): pl.pallas_call(kernel, out_shape=outs, in_specs=specs or [VM] * len(args)...  16.7 us
    ppermute x11, starting transfers between devices, send(): return lax.ppermute(values, AXES, swap_pairs(counts, target))  12.4 us
    ppermute x11, waiting for transfers between devices, send(): return lax.ppermute(values, AXES, swap_pairs(counts, target))  4.6 us
    concatenate x1, other arithmetic, on_device(): jnp.concatenate([right_side.reshape(12, 8, 128), stiff_scale, nodal_mass]...  0.84 us
    unnamed x1, local copies, waits for them, and re-layouts  0.8 us
  transfers between devices with their start and end apart: 11, of which 6 were waited for; matrix products, arithmetic and copies ran while one was open for 3% of the time, Pallas kernels for 20%

profile of v3, /device:TPU:0, one launch (start us, length us, event | category | flops | bytes accessed | tf_op | source)
XLA Modules:
  0.0 35.7 jit_solution(15481746829213460873)
XLA Ops:
  0.0 0.8 %pad_maximum_fusion.main = f32[20,8,128]{2,1,0:T(8,128)S(1)} fusion(f32[4,8,128]{2,1,0:T(8,128)} %param.6, f32[4,8,128]{2,1,0:T(8,128)} %param.5, f32[12,8,128]{2,1,0:T(8,128)} %bitcast.17), kind=kLoop, calls=%fused_computation | loop fusion | flops 40960 | bytes 163840 | tf_op jit(solution)/shard_map/concatenate | solution.py:585
  0.8 0.1 shard_map.46
  0.9 0.5 %collective-permute-start = (f32[10,8,128]{2,1,0:T(8,128)S(1)}, f32[10,8,128]{2,1,0:T(8,128)S(1)}, u32[]{:S(2)}, u32[]{:S(2)}) collective-permute-start(f32[10,8,128]{2,1,0:T(8,128)S(1)} %get-tuple-element.36), channel_id=1, source_target_pairs={{0,1},{1,0},{2,3},{3,2},{4,5},{5,4},{6,7},{7,6},{8,16},{9,17},{10,... | collective-permute-start | bytes 122888 | tf_op jit(solution)/shard_map/ppermute | solution.py:546
  1.4 4.1 %collective-permute-start.1 = (f32[10,8,128]{2,1,0:T(8,128)S(1)}, f32[10,8,128]{2,1,0:T(8,128)S(1)}, u32[]{:S(2)}, u32[]{:S(2)}) collective-permute-start(f32[10,8,128]{2,1,0:T(8,128)S(1)} %get-tuple-element.37), channel_id=1, source_target_pairs={{0,8},{1,9},{2,10},{3,11},{4,12},{5,13},{6,14},{7,15},{8,0},{9,1},... | collective-permute-start | bytes 122888 | tf_op jit(solution)/shard_map/ppermute | solution.py:546
  5.6 0.8 %copy.5 = f32[27,3,3]{2,1,0:T(4,128)S(1)} copy(f32[27,3,3]{0,2,1:T(4,128)} %param.7) | data formatting | bytes 1944 | tf_op args[3]
  6.4 0.2 reshape.6.blocks
  6.6 0.0 collective-permute-done.got_b
  6.6 1.0 %collective-permute-done.1.got_a = f32[10,8,128]{2,1,0:T(8,128)S(1)} collective-permute-done((f32[10,8,128]{2,1,0:T(8,128)S(1)}, f32[10,8,128]{2,1,0:T(8,128)S(1)}, u32[]{:S(2)}, u32[]{:S(2)}) %collective-permute-start.1) | collective-permute-done | bytes 40992 | tf_op jit(solution)/shard_map/ppermute | solution.py:546
  7.6 0.1 shard_map.47
  7.7 2.5 %collective-permute-start.4 = (f32[20,8,256]{2,1,0:T(8,128)S(1)}, f32[20,8,256]{2,1,0:T(8,128)S(1)}, u32[]{:S(2)}, u32[]{:S(2)}) collective-permute-start(f32[20,8,256]{2,1,0:T(8,128)S(1)} %shard_map.47), channel_id=1, source_target_pairs={{0,6},{1,7},{2,4},{3,5},{4,2},{5,3},{6,0},{7,1},{8,14},{9,15},{10,... | collective-permute-start | bytes 491528 | tf_op jit(solution)/shard_map/ppermute | solution.py:546
  10.2 0.5 %collective-permute-start.2 = (f32[20,8,256]{2,1,0:T(8,128)S(1)}, f32[20,8,256]{2,1,0:T(8,128)S(1)}, u32[]{:S(2)}, u32[]{:S(2)}) collective-permute-start(f32[20,8,256]{2,1,0:T(8,128)S(1)} %shard_map.47), channel_id=1, source_target_pairs={{0,2},{1,3},{2,0},{3,1},{4,6},{5,7},{6,4},{7,5},{8,10},{9,11},{10,... | collective-permute-start | bytes 491528 | tf_op jit(solution)/shard_map/ppermute | solution.py:546
  10.7 0.5 %collective-permute-start.3 = (f32[20,8,256]{2,1,0:T(8,128)S(1)}, f32[20,8,256]{2,1,0:T(8,128)S(1)}, u32[]{:S(2)}, u32[]{:S(2)}) collective-permute-start(f32[20,8,256]{2,1,0:T(8,128)S(1)} %shard_map.47), channel_id=1, source_target_pairs={{0,4},{1,5},{2,6},{3,7},{4,0},{5,1},{6,2},{7,3},{8,12},{9,13},{10,... | collective-permute-start | bytes 491528 | tf_op jit(solution)/shard_map/ppermute | solution.py:546
  11.2 3.3 %shard_map.48 = (bf16[2,432,256]{2,1,0:T(8,128)(2,1)S(1)}, bf16[432,256]{1,0:T(8,128)(2,1)S(1)}, bf16[2,576,256]{2,1,0:T(8,128)(2,1)S(1)}, bf16[576,256]{1,0:T(8...) custom-call(f32[243]{0:T(256)S(1)} %reshape.6.blocks), custom_call_target="tpu_custom_call" | custom-call | flops 5000000000 | bytes 8000000 | tf_op jit(solution)/shard_map/pallas_call | solution.py:26
  14.5 0.1 collective-permute-start.5
  14.6 0.7 %collective-permute-done.4 = f32[20,8,256]{2,1,0:T(8,128)S(1)} collective-permute-done((f32[20,8,256]{2,1,0:T(8,128)S(1)}, f32[20,8,256]{2,1,0:T(8,128)S(1)}, u32[]{:S(2)}, u32[]{:S(2)}) %collective-permute-start.4) | collective-permute-done | bytes 163872 | tf_op jit(solution)/shard_map/ppermute | solution.py:546
  15.3 0.0 collective-permute-start.8
  15.3 1.7 %collective-permute-done.2 = f32[20,8,256]{2,1,0:T(8,128)S(1)} collective-permute-done((f32[20,8,256]{2,1,0:T(8,128)S(1)}, f32[20,8,256]{2,1,0:T(8,128)S(1)}, u32[]{:S(2)}, u32[]{:S(2)}) %collective-permute-start.2) | collective-permute-done | bytes 163872 | tf_op jit(solution)/shard_map/ppermute | solution.py:546
  17.0 0.0 collective-permute-start.6
  17.0 0.0 collective-permute-done.3
  17.0 0.5 %collective-permute-start.7 = (f32[20,8,256]{2,1,0:T(8,128)S(1)}, f32[20,8,256]{2,1,0:T(8,128)S(1)}, u32[]{:S(2)}, u32[]{:S(2)}) collective-permute-start(f32[20,8,256]{2,1,0:T(8,128)S(1)} %collective-permute-done.3), channel_id=1, source_target_pairs={{0,1},{1,0},{2,3},{3,2},{4,5},{5,4},{6,7},{7,6},{8,9},{9,8},{10,11... | collective-permute-start | bytes 491528 | tf_op jit(solution)/shard_map/ppermute | solution.py:546
  17.5 0.0 collective-permute-done.5
  17.5 0.0 collective-permute-done.8
  17.5 0.9 %collective-permute-done.6 = f32[20,8,256]{2,1,0:T(8,128)S(1)} collective-permute-done((f32[20,8,256]{2,1,0:T(8,128)S(1)}, f32[20,8,256]{2,1,0:T(8,128)S(1)}, u32[]{:S(2)}, u32[]{:S(2)}) %collective-permute-start.6) | collective-permute-done | bytes 163872 | tf_op jit(solution)/shard_map/ppermute | solution.py:546
  18.4 0.2 collective-permute-done.7
  18.6 2.1 %shard_map.49 = (f32[22,3,16,256]{3,2,1,0:T(8,128)S(1)}, f32[22,16,256]{2,1,0:T(8,128)S(1)}, f32[22,16,256]{2,1,0:T(8,128)S(1)}, f32[22,3,16,256]{3,2,1,0:T(8,12...) custom-call(f32[243]{0:T(256)S(1)} %reshape.6.blocks, ...), custom_call_target="tpu_custom_call" | custom-call | flops 1000000 | bytes 100000 | tf_op jit(solution)/shard_map/pallas_call | solution.py:26
  20.7 1.8 %collective-permute-start.9 = (f32[3,8,128]{2,1,0:T(8,128)S(1)}, f32[3,8,128]{2,1,0:T(8,128)S(1)}, u32[]{:S(2)}, u32[]{:S(2)}) collective-permute-start(f32[3,8,128]{2,1,0:T(8,128)S(1)} %get-tuple-element.47), channel_id=1, source_target_pairs={{0,9},{1,8},{2,11},{3,10},{4,13},{5,12},{6,15},{7,14},{8,1},{9,0},... | collective-permute-start | bytes 36872 | tf_op jit(solution)/shard_map/ppermute | solution.py:546
  22.5 1.3 %shard_map.50.power_1 = f32[22,3,16,256]{3,2,1,0:T(8,128)S(1)} custom-call(f32[22,16,256]{2,1,0:T(8,128)S(1)} %get-tuple-element.49.scale_w, f32[22,16,256]{2,1,0:T(8,128)S(1)} %get-tuple-element.50.mass_w, f32[22,3,16,256]{3,2,1,0:T(8,128)S(1)} %get-tuple-element.51.inverse_w, f32[22,3,16,256]{3,2,1,0:T(8,128)S(1)} %get-tuple-element.48.source_w, ...), custom_call_target="tpu_custom_call" | custom-call | flops 1000000000 | bytes 4000000 | tf_op jit(solution)/shard_map/pallas_call | solution.py:26
  23.8 0.1 collective-permute-done.9
  24.0 1.8 %collective-permute-start.10 = (f32[3,8,128]{2,1,0:T(8,128)S(1)}, f32[3,8,128]{2,1,0:T(8,128)S(1)}, u32[]{:S(2)}, u32[]{:S(2)}) collective-permute-start(f32[3,8,128]{2,1,0:T(8,128)S(1)} %max.3.bounds_a), channel_id=1, source_target_pairs={{0,17},{1,16},{2,19},{3,18},{4,21},{5,20},{6,23},{7,22},{8,25},{9,... | collective-permute-start | bytes 36872 | tf_op jit(solution)/shard_map/ppermute | solution.py:546
  25.8 2.6 %shard_map.51 = (f32[22,3,16,256]{3,2,1,0:T(8,128)S(1)}, f32[4,192,128]{2,1,0:T(8,128)S(1)}) custom-call(f32[22,16,256]{2,1,0:T(8,128)S(1)} %get-tuple-element.49.scale_w, f32[22,16,256]{2,1,0:T(8,128)S(1)} %get-tuple-element.50.mass_w, f32[22,3,16,256]{3,2,1,0:T(8,128)S(1)} %get-tuple-element.51.inverse_w, ...), custom_call_target="tpu_custom_call" | custom-call | flops 2000000000 | bytes 8000000 | tf_op jit(solution)/shard_map/pallas_call | solution.py:26
  28.3 0.0 collective-permute-done.10.bounds_b
  28.3 7.3 %shard_map.52 = f32[3,4,8,128]{3,2,1,0:T(8,128)} custom-call(f32[3,8,128]{2,1,0:T(8,128)S(1)} %max.3.bounds_a, f32[3,8,128]{2,1,0:T(8,128)S(1)} %collective-permute-done.10.bounds_b, f32[22,3,16,256]{3,2,1,0:T(8,128)S(1)} %get-tuple-element.48.source_w, f32[22,16,256]{2,1,0:T(8,128)S(1)} %get-tuple-element.49.scale_w, ...), custom_call_target="tpu_custom_call" | custom-call | flops 1000000 | bytes 100000 | tf_op jit(solution)/shard_map/pallas_call | solution.py:26
  (1 shorter events, 0.0 us)
Async XLA Ops:
  0.9 5.6 %collective-permute-start = (f32[10,8,128]{2,1,0:T(8,128)S(1)}, f32[10,8,128]{2,1,0:T(8,128)S(1)}, u32[]{:S(2)}, u32[]{:S(2)}) collective-permute-start(f32[10,8,128]{2,1,0:T(8,128)S(1)} %get-tuple-element.36), channel_id=1, source_target_pairs={{0,1},{1,0},{2,3},{3,2},{4,5},{5,4},{6,7},{7,6},{8,16},{9,17},{10,... | collective-permute-start | bytes 122888 | tf_op jit(solution)/shard_map/ppermute | solution.py:546
  1.4 6.1 %collective-permute-start.1 = (f32[10,8,128]{2,1,0:T(8,128)S(1)}, f32[10,8,128]{2,1,0:T(8,128)S(1)}, u32[]{:S(2)}, u32[]{:S(2)}) collective-permute-start(f32[10,8,128]{2,1,0:T(8,128)S(1)} %get-tuple-element.37), channel_id=1, source_target_pairs={{0,8},{1,9},{2,10},{3,11},{4,12},{5,13},{6,14},{7,15},{8,0},{9,1},... | collective-permute-start | bytes 122888 | tf_op jit(solution)/shard_map/ppermute | solution.py:546
  7.7 7.6 %collective-permute-start.4 = (f32[20,8,256]{2,1,0:T(8,128)S(1)}, f32[20,8,256]{2,1,0:T(8,128)S(1)}, u32[]{:S(2)}, u32[]{:S(2)}) collective-permute-start(f32[20,8,256]{2,1,0:T(8,128)S(1)} %shard_map.47), channel_id=1, source_target_pairs={{0,6},{1,7},{2,4},{3,5},{4,2},{5,3},{6,0},{7,1},{8,14},{9,15},{10,... | collective-permute-start | bytes 491528 | tf_op jit(solution)/shard_map/ppermute | solution.py:546
  10.2 6.8 %collective-permute-start.2 = (f32[20,8,256]{2,1,0:T(8,128)S(1)}, f32[20,8,256]{2,1,0:T(8,128)S(1)}, u32[]{:S(2)}, u32[]{:S(2)}) collective-permute-start(f32[20,8,256]{2,1,0:T(8,128)S(1)} %shard_map.47), channel_id=1, source_target_pairs={{0,2},{1,3},{2,0},{3,1},{4,6},{5,7},{6,4},{7,5},{8,10},{9,11},{10,... | collective-permute-start | bytes 491528 | tf_op jit(solution)/shard_map/ppermute | solution.py:546
  10.7 6.3 %collective-permute-start.3 = (f32[20,8,256]{2,1,0:T(8,128)S(1)}, f32[20,8,256]{2,1,0:T(8,128)S(1)}, u32[]{:S(2)}, u32[]{:S(2)}) collective-permute-start(f32[20,8,256]{2,1,0:T(8,128)S(1)} %shard_map.47), channel_id=1, source_target_pairs={{0,4},{1,5},{2,6},{3,7},{4,0},{5,1},{6,2},{7,3},{8,12},{9,13},{10,... | collective-permute-start | bytes 491528 | tf_op jit(solution)/shard_map/ppermute | solution.py:546
  14.5 3.0 %collective-permute-start.5 = (f32[20,8,256]{2,1,0:T(8,128)S(1)}, f32[20,8,256]{2,1,0:T(8,128)S(1)}, u32[]{:S(2)}, u32[]{:S(2)}) collective-permute-start(f32[20,8,256]{2,1,0:T(8,128)S(1)} %shard_map.47), channel_id=1, source_target_pairs={{0,1},{1,0},{2,3},{3,2},{4,5},{5,4},{6,7},{7,6},{8,9},{9,8},{10,11... | collective-permute-start | bytes 491528 | tf_op jit(solution)/shard_map/ppermute | solution.py:546
  15.3 2.2 %collective-permute-start.8 = (f32[20,8,256]{2,1,0:T(8,128)S(1)}, f32[20,8,256]{2,1,0:T(8,128)S(1)}, u32[]{:S(2)}, u32[]{:S(2)}) collective-permute-start(f32[20,8,256]{2,1,0:T(8,128)S(1)} %collective-permute-done.4), channel_id=1, source_target_pairs={{0,1},{1,0},{2,3},{3,2},{4,5},{5,4},{6,7},{7,6},{8,9},{9,8},{10,11... | collective-permute-start | bytes 491528 | tf_op jit(solution)/shard_map/ppermute | solution.py:546
  17.0 1.4 %collective-permute-start.6 = (f32[20,8,256]{2,1,0:T(8,128)S(1)}, f32[20,8,256]{2,1,0:T(8,128)S(1)}, u32[]{:S(2)}, u32[]{:S(2)}) collective-permute-start(f32[20,8,256]{2,1,0:T(8,128)S(1)} %collective-permute-done.2), channel_id=1, source_target_pairs={{0,1},{1,0},{2,3},{3,2},{4,5},{5,4},{6,7},{7,6},{8,9},{9,8},{10,11... | collective-permute-start | bytes 491528 | tf_op jit(solution)/shard_map/ppermute | solution.py:546
  17.0 1.6 %collective-permute-start.7 = (f32[20,8,256]{2,1,0:T(8,128)S(1)}, f32[20,8,256]{2,1,0:T(8,128)S(1)}, u32[]{:S(2)}, u32[]{:S(2)}) collective-permute-start(f32[20,8,256]{2,1,0:T(8,128)S(1)} %collective-permute-done.3), channel_id=1, source_target_pairs={{0,1},{1,0},{2,3},{3,2},{4,5},{5,4},{6,7},{7,6},{8,9},{9,8},{10,11... | collective-permute-start | bytes 491528 | tf_op jit(solution)/shard_map/ppermute | solution.py:546
  20.7 3.2 %collective-permute-start.9 = (f32[3,8,128]{2,1,0:T(8,128)S(1)}, f32[3,8,128]{2,1,0:T(8,128)S(1)}, u32[]{:S(2)}, u32[]{:S(2)}) collective-permute-start(f32[3,8,128]{2,1,0:T(8,128)S(1)} %get-tuple-element.47), channel_id=1, source_target_pairs={{0,9},{1,8},{2,11},{3,10},{4,13},{5,12},{6,15},{7,14},{8,1},{9,0},... | collective-permute-start | bytes 36872 | tf_op jit(solution)/shard_map/ppermute | solution.py:546
  24.0 4.4 %collective-permute-start.10 = (f32[3,8,128]{2,1,0:T(8,128)S(1)}, f32[3,8,128]{2,1,0:T(8,128)S(1)}, u32[]{:S(2)}, u32[]{:S(2)}) collective-permute-start(f32[3,8,128]{2,1,0:T(8,128)S(1)} %max.3.bounds_a), channel_id=1, source_target_pairs={{0,17},{1,16},{2,19},{3,18},{4,21},{5,20},{6,23},{7,22},{8,25},{9,... | collective-permute-start | bytes 36872 | tf_op jit(solution)/shard_map/ppermute | solution.py:546

commit v4 on v3

--- a/solution.py
+++ b/solution.py
@@ -68,16 +68,31 @@
     return dot(matrix_high, high) + dot(matrix_low, high) + dot(matrix_high, low)
 
 
-def banded_beside(matrix_high, matrix_low, values):
-    high, low = split(values)
-    width = values.shape[1]
-    product = dot(matrix_high, jnp.concatenate([high, low], axis=1))
-    return product[:, :width] + product[:, width:] + dot(matrix_low, high)
-
-
 def banded_stacked(matrix, values):
     high, low = split(values)
     return dot(matrix, jnp.concatenate([high, high, low], axis=0))
+
+
+def banded_planes(matrix, values, planes, step):
+    slab = values.shape[0] // planes
+    edge = jnp.zeros((slab, 128), F32)
+    padded = jnp.concatenate([edge, values, edge], axis=0)
+    beside = jnp.concatenate([padded[at * slab : (at + 3) * slab] for at in range(planes)], axis=1)
+    high = beside.astype(BF16).astype(F32)
+    stacked = jnp.concatenate([high, high, beside - high], axis=0).astype(BF16)
+    product = dot(matrix[:, : 9 * slab], stacked)
+    outs = []
+    for at in range(planes):
+        below, here, above = (
+            product[part * slab : part * slab + slab, at * 128 : at * 128 + 128] for part in range(3)
+        )
+        outs.append(here + pltpu.roll(below, step, 1) + pltpu.roll(above, 128 - step, 1))
+    return jnp.concatenate(outs, axis=0)
+
+
+def paired_lanes(values):
+    even = iota(values.shape, 1) % 2 == 0
+    return values + jnp.where(even, pltpu.roll(values, 127, 1), pltpu.roll(values, 1, 1))
 
 
 def shifted_sum(product, slabs, rows, lanes):
@@ -164,9 +179,13 @@
     return -(-size // 128) * 128
 
 
+def coarse_slab(few):
+    return -(-3 * few // 16) * 16
+
+
 def matrices_kernel(
     rows, planes, blocks, fine, fine_bound, mid, mid_bound, coarse, coarse_bound, coarse_diag,
-    gather_rows, spread_rows, expand, fold, unfold, squeeze, stretch,
+    gather_rows, spread_rows, squeeze, stretch,
 ):
     def direct(offset, comp, other):
         return blocks[offset * 9 + comp * 3 + other]
@@ -191,70 +210,46 @@
 
     rows, planes = rows // 2, planes // 2
     slab = 3 * rows
-    width, bound_width = mid.shape[2], mid_bound.shape[1]
-    found = panels(direct, 3, rows, width)
-    bound = panels(absolute, 1, rows, bound_width)
-
-    def cut(value, plane, size):
-        column = iota(value.shape, 1)
-        if plane == 0:
-            value = jnp.where(column < size, 0.0, value)
-        if plane == planes - 1:
-            value = jnp.where(column >= 2 * size, 0.0, value)
-        return turned(value, (plane - 1) * size)
-
-    for plane in range(planes):
-        for step_x in range(3):
-            start = (plane * 3 + step_x) * slab
-            value = jnp.concatenate([found[step_x, comp] for comp in range(3)], axis=0)
-            high, low = split(cut(value, plane, slab))
-            mid[0, start : start + slab, :] = high
-            mid[1, start : start + slab, :] = low
-            value = jnp.concatenate([bound[step_x, comp] for comp in range(3)], axis=0)
-            mid_bound[start : start + slab, :] = stack3(cut(value, plane, rows), planes * rows)
-
+    found = panels(direct, 3, rows, mid.shape[1])
+    whole = jnp.concatenate([found[step_x, comp] for step_x in range(3) for comp in range(3)], axis=0)
     few, half = rows // 2, planes // 2
-    tall, wide = half * 9 * few, half * 3 * few
-    place = iota((tall, 2 * tall), 0)
-    choose = ones_where(iota((tall, 2 * tall), 1) == place // few * rows + place % few)
-
-    def smaller(matrix, count, size):
-        place = iota((2 * count, size), 1)
-        pick = ones_where(iota((2 * count, size), 0) == place // few * rows + place % few)
-        return dot(dot(choose, matrix).astype(BF16), pick)
-
-    high = smaller(mid[0, : 2 * tall, : 2 * wide], wide, coarse.shape[1])
-    low = smaller(mid[1, : 2 * tall, : 2 * wide], wide, coarse.shape[1])
-    keep = iota(high.shape, 1) < wide
-    high, low = jnp.where(keep, high, 0.0), jnp.where(keep, low, 0.0)
-    coarse[...] = (high + turned(low, wide) + turned(high, 2 * wide)).astype(BF16)
-    count = half * few
-    size = planes * rows
-    whole = mid_bound[: 2 * tall, :]
-    high = smaller(whole[:, : 2 * count], count, coarse_bound.shape[1])
-    low = smaller(whole[:, size : size + 2 * count], count, coarse_bound.shape[1])
-    keep = iota(high.shape, 1) < count
-    high, low = jnp.where(keep, high, 0.0), jnp.where(keep, low, 0.0)
-    coarse_bound[...] = (high + turned(low, count) + turned(high, 2 * count)).astype(BF16)
-    comp = (iota((wide, 128), 0) // few) % 3
+    size = coarse_slab(few)
+
+    def choose(out, source):
+        place = out % size
+        wanted = out // size * slab + place // few * rows + place % few
+        return ones_where(jnp.logical_and(source == wanted, place < 3 * few))
+
+    shape = (3 * size, 3 * slab)
+    choose_rows = choose(iota(shape, 0), iota(shape, 1))
+    shape = (mid.shape[1], up128(3 * size))
+    choose_columns = jnp.where(iota(shape, 1) < 3 * size, choose(iota(shape, 1), iota(shape, 0)), 0.0).astype(BF16)
+
+    def smaller(matrix):
+        return dot(dot(choose_rows, matrix.astype(BF16)).astype(BF16), choose_columns)
+
+    for target, small_target, value in ((mid, coarse, whole), (mid_bound, coarse_bound, jnp.abs(whole))):
+        target[...] = stack3(value, 3 * slab)
+        high, low = parts_of(value)
+        high, low = smaller(high), smaller(low)
+        width = small_target.shape[1]
+        if width > high.shape[1]:
+            more = jnp.zeros((3 * size, width - high.shape[1]), F32)
+            high, low = jnp.concatenate([high, more], axis=1), jnp.concatenate([low, more], axis=1)
+        small_target[...] = (high + turned(low, 3 * size) + turned(high, 6 * size)).astype(BF16)
+    comp = iota((half * size, 128), 0) % size // few
     diag = [blocks[13 * 9 + 4 * at] for at in range(3)]
     coarse_diag[...] = jnp.where(comp == 0, diag[0], jnp.where(comp == 1, diag[1], diag[2]))
 
-    def same_aggregate(out_row, in_row, out_rows, in_rows, ratio_z):
-        same_plane = out_row // (3 * out_rows) == in_row // (3 * in_rows * ratio_z)
-        same_comp = out_row // out_rows % 3 == in_row // in_rows % 3
-        return jnp.logical_and(jnp.logical_and(same_plane, same_comp), out_row % out_rows == in_row % in_rows // 2)
-
-    big = planes * slab
-    shape = (wide, big)
-    gather_rows[...] = ones_where(same_aggregate(iota(shape, 0), iota(shape, 1), few, rows, 2))
-    shape = (big, 2 * wide)
-    spread_rows[...] = ones_where(same_aggregate(iota(shape, 1) % wide, iota(shape, 0), few, rows, 2))
-    shape = (2 * slab, 2 * slab)
-    expand[...] = ones_where(same_aggregate(iota(shape, 1) % slab, iota(shape, 0), rows, 2 * rows, 1))
-    shape = (256, 128)
-    fold[...] = ones_where(iota(shape, 0) % 128 // 2 == iota(shape, 1) % 64)
-    unfold[...] = ones_where(iota(shape, 0) % 128 == iota(shape, 1) // 2)
+    def same_aggregate(small, large):
+        place, inner = small % size, large % slab
+        same = jnp.logical_and(small // size == large // (2 * slab), place // few == inner // rows)
+        return jnp.logical_and(same, place % few == inner % rows // 2)
+
+    shape = (half * size, planes * slab)
+    gather_rows[...] = ones_where(same_aggregate(iota(shape, 0), iota(shape, 1)))
+    shape = (planes * slab, 2 * half * size)
+    spread_rows[...] = ones_where(same_aggregate(iota(shape, 1) % (half * size), iota(shape, 0)))
     shape = (2 * LANES, 128)
     squeeze[...] = ones_where(iota(shape, 0) % LANES // 2 == iota(shape, 1))
     shape = (256, LANES)
@@ -298,7 +293,7 @@
     width = ratio.shape[1]
     flat = jnp.max(ratio.reshape(-1, 8, width), axis=0)
     own = jnp.where(iota((8, width), 1) < lanes, flat, -jnp.inf)
-    return jnp.full((8, 128), jnp.max(own), F32)
+    return functools.reduce(jnp.maximum, [own[:, at : at + 128] for at in range(0, width, 128)])
 
 
 def paired_planes(values):
@@ -318,7 +313,7 @@
 def window_kernel(
     gys, ordered, blocks, *refs
 ):
-    (*blocks_in, fine_bound, mid_bound, coarse_bound, coarse_diag, gather_rows, fold, squeeze,
+    (*blocks_in, fine_bound, mid_bound, coarse_bound, coarse_diag, gather_rows, squeeze,
      source_w, scale_w, mass_w, inverse_w, spread_1w, weight_1w, inverse_1w, spread_2w, weight_2w, inverse_2w, bounds, held) = refs
     planes, rows = scale_w.shape[0] - 2 * PAD, scale_w.shape[1]
     gz, gy = lax.axis_index("gz"), lax.axis_index("gy")
@@ -373,19 +368,16 @@
     inverse_1 = inverse_diagonal(scale_1, mass_1, blocks, 2.0).reshape(planes * slab, 128)
     spread_1 = jnp.broadcast_to(scale_1[:, None], (planes, 3, rows, 128)).reshape(planes * slab, 128)
     weight_1 = jnp.broadcast_to(mass_1[:, None], (planes, 3, rows, 128)).reshape(planes * slab, 128)
-    product = banded_stacked(mid_bound[:, : 3 * count], scale_1.reshape(count, 128))
-    total = shifted_sum(product, planes, slab, 128)
+    total = banded_planes(mid_bound, spread_1, planes, 1)
     bounds[1] = largest((2.0 * spread_1 * total + weight_1) * inverse_1, 64)
     spread_1w[...], weight_1w[...], inverse_1w[...] = spread_1, weight_1, inverse_1
 
     both = rows_apply(gather_rows[...], jnp.concatenate([spread_1, weight_1], axis=1))
-    spread_2 = lanes_apply(both[:, :128], fold[...]) * 0.125
-    weight_2 = lanes_apply(both[:, 128:], fold[...])
+    spread_2 = paired_lanes(both[:, :128]) * 0.125
+    weight_2 = paired_lanes(both[:, 128:])
     inverse_2 = jnp.where(spread_2 > 0.0, 1.0 / (4.0 * coarse_diag[...] * spread_2 * spread_2 + weight_2), 0.0)
-    rows, planes = rows // 2, planes // 2
-    single = spread_2.reshape(planes, 3, rows, 128)[:, 0].reshape(planes * rows, 128)
-    total = shifted_sum(banded_stacked(coarse_bound[:, : 3 * planes * rows], single), planes, 3 * rows, 128)
-    bounds[2] = largest((4.0 * spread_2 * total + weight_2) * inverse_2, 32)
+    total = banded_planes(coarse_bound, spread_2, planes // 2, 2)
+    bounds[2] = largest((4.0 * spread_2 * total + weight_2) * inverse_2, 64)
     spread_2w[...], weight_2w[...], inverse_2w[...] = spread_2, weight_2, inverse_2
 
 
@@ -407,7 +399,7 @@
     power[PAD : PAD + planes] = inner_power(scale_w, mass_w, inverse_w, fine, source_w)
 
 
-def restrict_kernel(scale_w, mass_w, inverse_w, source_w, power_1, fine, squeeze, power_2, basis, held):
+def restrict_kernel(scale_w, mass_w, inverse_w, source_w, power_1, fine, squeeze, basis, power_2, held):
     planes, rows = scale_w.shape[0] - 2 * PAD, scale_w.shape[1]
     power_kernel(scale_w, mass_w, inverse_w, power_1, fine, power_2)
     third = inner_power(scale_w, mass_w, inverse_w, fine, power_2)
@@ -418,9 +410,28 @@
         basis[at] = lanes_apply(pairs, squeeze[...])
 
 
-def chebyshev_scalars(bound, ratio):
-    lower = bound / ratio
-    return 0.5 * (bound + lower), 0.5 * (bound - lower)
+def chebyshev_constants(ratio, degree):
+    sigma = (ratio + 1.0) / (ratio - 1.0)
+    rho = 1.0 / sigma
+    steps = []
+    for _ in range(degree - 1):
+        rho_next = 1.0 / (2.0 * sigma - rho)
+        steps.append((rho_next * rho, 4.0 * rho_next / (1.0 - 1.0 / ratio)))
+        rho = rho_next
+    return 2.0 / (1.0 + 1.0 / ratio), steps
+
+
+def chebyshev(residue, degree, inverse, ratio, operate, keep):
+    first, steps = chebyshev_constants(ratio, degree)
+    direction = first * (inverse * residue)
+    total = direction
+    for hold, push in steps:
+        residue = residue - operate(direction)
+        direction = hold * direction + push * (inverse * residue)
+        total = total + direction
+    if keep:
+        residue = residue - operate(direction)
+    return total, residue
 
 
 def scaled(coeff, values):
@@ -431,95 +442,75 @@
     return (coeff[None] * flat).reshape(values.shape)
 
 
-def chebyshev(residue, degree, inverse, bound, ratio, operate, keep):
-    centre, spread = chebyshev_scalars(bound, ratio)
-    sigma = centre / spread
-    rho = 1.0 / sigma
-    direction = scaled(1.0 / centre, inverse * residue)
-    total = direction
-    for step in range(degree):
-        if step < degree - 1 or keep:
-            residue = residue - operate(direction)
-        if step < degree - 1:
-            rho_next = 1.0 / (2.0 * sigma - rho)
-            direction = scaled(rho_next * rho, direction) + scaled(2.0 * rho_next / spread, inverse * residue)
-            total = total + direction
-            rho = rho_next
-    return total, residue
-
-
 def final_kernel(
-    bounds_a, bounds_b, source_w, scale_w, mass_w, inverse_w, power_1, power_2, basis,
+    bounds_a, bounds_b, source_w, scale_w, mass_w, inverse_w, power_1, basis,
     spread_1w, weight_1w, inverse_1w, spread_2w, weight_2w, inverse_2w,
-    fine, mid, coarse, gather_rows, spread_rows, expand, fold, unfold, stretch, result, lifted_w, answer_w,
+    fine, mid, coarse, gather_rows, spread_rows, stretch, result, lifted_w, doubled_w, answer_w,
 ):
     rows = scale_w.shape[1] // 2
     planes = (scale_w.shape[0] - 2 * PAD) // 2
     slab = 3 * rows
-    size = planes * slab
-    small = size // 4
     gz, gy = lax.axis_index("gz"), lax.axis_index("gy")
-    bounds = jnp.maximum(bounds_a[...], bounds_b[...])
-
-    centre, spread = chebyshev_scalars(bounds[0], SMOOTH_RATIO)
-    sigma = centre / spread
-    rho = 1.0 / sigma
-    rho_next = 1.0 / (2.0 * sigma - rho)
-    keep, push = rho_next * rho, 2.0 * rho_next / spread
-    beta = push / centre
-    gamma = 1.0 / centre + keep / centre + push
-    omega = (4.0 / 3.0) / bounds[0]
-
-    source_1 = (
-        basis[0]
-        - scaled(gamma + omega, basis[1])
-        + scaled(beta + omega * gamma, basis[2])
-        - scaled(omega * beta, basis[3])
+    worst = jnp.maximum(bounds_a[...], bounds_b[...])
+    inverse_bounds = [1.0 / jnp.full((8, 128), jnp.max(worst[level]), F32) for level in range(3)]
+    over_0 = inverse_bounds[0]
+
+    first, ((hold, push),) = chebyshev_constants(SMOOTH_RATIO, 2)
+    beta = push * first
+    gamma = first * (1.0 + hold) + push
+    omega = 4.0 / 3.0
+    source_1 = basis[0] - scaled(
+        over_0,
+        (gamma + omega) * basis[1]
+        - scaled(over_0, (beta + omega * gamma) * basis[2] - scaled(over_0, (omega * beta) * basis[3])),
     )
-    spread_1, weight_1, inverse_1 = spread_1w[...], weight_1w[...], inverse_1w[...]
-    spread_2, weight_2, inverse_2 = spread_2w[...], weight_2w[...], inverse_2w[...]
+
+    spread_1, weight_1 = spread_1w[...], weight_1w[...]
+    spread_2, weight_2 = spread_2w[...], weight_2w[...]
+    inverse_1 = scaled(inverse_bounds[1], inverse_1w[...])
+    inverse_2 = scaled(inverse_bounds[2], inverse_2w[...])
+    double_1, double_2 = 2.0 * spread_1, 4.0 * spread_2
 
     def operate_1(values):
-        product = banded_beside(mid[0, :, :size], mid[1, :, :size], spread_1 * values)
-        return 2.0 * spread_1 * shifted_sum(product, planes, slab, 128) + weight_1 * values
+        return double_1 * banded_planes(mid, spread_1 * values, planes, 1) + weight_1 * values
 
     def operate_2(values):
-        product = banded_stacked(coarse[:, : 3 * small], spread_2 * values)
-        return 4.0 * spread_2 * shifted_sum(product, planes // 2, slab // 2, 128) + weight_2 * values
-
-    omega_1 = (4.0 / 3.0) / bounds[1]
-    iterate, residue = chebyshev(source_1, 2, inverse_1, bounds[1], SMOOTH_RATIO, operate_1, True)
-    smoothed = residue - scaled(omega_1, operate_1(inverse_1 * residue))
-    source_2 = lanes_apply(rows_apply(gather_rows[...], smoothed), fold[...])
-    error_2, _ = chebyshev(source_2, COARSE_ITERS, inverse_2, bounds[2], COARSE_RATIO, operate_2, False)
-    lifted = lanes_apply(error_2, unfold[...])
-    lifted = dot(spread_rows[...], jnp.concatenate(split(lifted), axis=0))
-    iterate = iterate + lifted - scaled(omega_1, inverse_1 * operate_1(lifted))
+        return double_2 * banded_planes(coarse, spread_2 * values, planes // 2, 2) + weight_2 * values
+
+    iterate, residue = chebyshev(source_1, 2, inverse_1, SMOOTH_RATIO, operate_1, True)
+    smoothed = residue - omega * operate_1(inverse_1 * residue)
+    source_2 = paired_lanes(rows_apply(gather_rows[...], smoothed))
+    error_2, _ = chebyshev(source_2, COARSE_ITERS, inverse_2, COARSE_RATIO, operate_2, False)
+    lifted = dot(spread_rows[...], jnp.concatenate(split(error_2), axis=0))
+    iterate = iterate + lifted - omega * (inverse_1 * operate_1(lifted))
     residue = source_1 - operate_1(iterate)
-    more, _ = chebyshev(residue, 2, inverse_1, bounds[1], SMOOTH_RATIO, operate_1, False)
+    more, _ = chebyshev(residue, 2, inverse_1, SMOOTH_RATIO, operate_1, False)
     error_1 = iterate + more
 
     lifted_w[0:2] = jnp.zeros((2, slab, 128), F32)
     lifted_w[planes + 2 : planes + 4] = jnp.zeros((2, slab, 128), F32)
     lifted_w[2 : planes + 2] = error_1.reshape(planes, slab, 128)
     near = lifted_w[pl.ds(2 * gz, 6)].reshape(6 * slab, 128)
-    wide = lanes_apply(near, stretch[...]).reshape(6, slab, LANES)
-    side = jnp.concatenate([wide[plane] for plane in range(6)], axis=1)
-    tall = dot(expand[...], jnp.concatenate(split(side), axis=0))
-    slabs = [tall[:, plane * LANES : plane * LANES + LANES] for plane in range(6)]
-    error = jnp.stack([slabs[(plane + 1) // 2] for plane in range(10)], axis=0).reshape(10, 3, 2 * rows, LANES)
+    wide = lanes_apply(near, stretch[...])
+    for half in (0, 1):
+        for odd in (0, 1):
+            doubled_w[half, pl.ds(odd, 6 * slab, stride=2)] = wide[:, half * 128 : half * 128 + 128]
+    slabs = jnp.concatenate([doubled_w[0], doubled_w[1]], axis=1).reshape(6, 3, 2 * rows, LANES)
+    error = jnp.stack([slabs[(plane + 1) // 2] for plane in range(10)], axis=0)
 
     def near_own(ref, reach):
         return ref[pl.ds(4 * gz + PAD - reach, 4 + 2 * reach)]
 
-    scale, mass, inverse = near_own(scale_w, 3), near_own(mass_w, 2), near_own(inverse_w, 2)
+    scale, mass = near_own(scale_w, 3), near_own(mass_w, 2)
+    inverse = scaled(over_0, near_own(inverse_w, 2))
     source = near_own(source_w, 2)
+    before = gamma * source - scaled(over_0, beta * near_own(power_1, 2))
     image = fine_operator(fine, scale, mass, error)
-    iterate = inverse * (scaled(gamma, source) - scaled(beta, near_own(power_1, 2)) - scaled(omega, image)) + error[1:9]
+    iterate = inverse * (before - omega * image) + error[1:9]
     residue = source[1:7] - fine_operator(fine, scale[1:9], mass[1:7], iterate)
-    direction = scaled(1.0 / centre, inverse[1:7] * residue)
+    direction = first * (inverse[1:7] * residue)
     last = residue[1:5] - fine_operator(fine, scale[2:8], mass[2:6], direction)
-    answer = iterate[2:6] + scaled(1.0 + keep, direction[1:5]) + scaled(push, inverse[2:6] * last)
+    answer = iterate[2:6] + (1.0 + hold) * direction[1:5] + push * (inverse[2:6] * last)
     answer_w[...] = answer[:, :, :, :128]
     for comp in range(3):
         result[comp] = answer_w[:, comp, pl.ds(pl.multiple_of(8 * gy, 8), 8), :]
@@ -552,26 +543,23 @@
     grant = 20 if planes * rows <= 256 else 48
     slab = 3 * rows
     group = group_of(slab)
-    size_1, count_1 = planes * slab // 4, planes * rows // 4
-    size_2, count_2 = size_1 // 4, count_1 // 4
+    size_1 = planes * slab // 4
+    size = coarse_slab(rows // 4)
+    size_2 = planes // 4 * size
     (
-        fine, fine_bound, mid, mid_bound, coarse, coarse_bound, coarse_diag,
-        gather_rows, spread_rows, expand, fold, unfold, squeeze, stretch,
+        fine, fine_bound, mid, mid_bound, coarse, coarse_bound, coarse_diag, gather_rows, spread_rows, squeeze, stretch,
     ) = call(
         functools.partial(matrices_kernel, rows, planes),
         [
             ((2, group * 3 * slab, up128((group + 2) * slab)), BF16),
             ((group * 3 * slab, up128(3 * (group + 2) * rows)), BF16),
-            ((2, 3 * size_1, up128(size_1)), BF16),
-            ((3 * size_1, up128(3 * count_1)), BF16),
-            ((3 * size_2, up128(3 * size_2)), BF16),
-            ((3 * size_2, up128(3 * count_2)), BF16),
+            ((3 * slab // 2, up128(9 * slab // 2)), BF16),
+            ((3 * slab // 2, up128(9 * slab // 2)), BF16),
+            ((3 * size, up128(9 * size)), BF16),
+            ((3 * size, up128(9 * size)), BF16),
             ((size_2, 128), F32),
             ((size_2, size_1), BF16),
             ((size_1, 2 * size_2), BF16),
-            ((slab, slab), BF16),
-            ((256, 128), BF16),
-            ((256, 128), BF16),
             ((2 * LANES, 128), BF16),
             ((256, LANES), BF16),
         ],
@@ -605,10 +593,10 @@
     source_w, scale_w, mass_w, inverse_w, *levels, bounds = call(
         functools.partial(window_kernel, gys, ordered),
         [field, single, single, field] + [((size_1, 128), F32)] * 3 + [((size_2, 128), F32)] * 3 + [((3, 8, 128), F32)],
-        specs=[SM] + [VM] * (len(gathered) + 7),
+        specs=[SM] + [VM] * (len(gathered) + 6),
         scratch=[pltpu.VMEM((2, 2, planes * rows // 2, 128), F32)],
         grant=grant,
-    )(blocks, *gathered, fine_bound, mid_bound, coarse_bound, coarse_diag, gather_rows, fold, squeeze)
+    )(blocks, *gathered, fine_bound, mid_bound, coarse_bound, coarse_diag, gather_rows, squeeze)
 
     step = 4
     while step < gxs:
@@ -617,10 +605,10 @@
     bounds = jnp.maximum(bounds, send(bounds, lambda x, y, z: (x ^ 1, y, z ^ 1)))
     other = send(bounds, lambda x, y, z: (x ^ 2, y, z ^ 1))
     (power_1,) = call(power_kernel, [field], flops=1000000000, size=4000000, grant=grant)(scale_w, mass_w, inverse_w, source_w, fine)
-    power_2, basis = call(
+    (basis,) = call(
         restrict_kernel,
-        [field, ((4, size_1, 128), F32)],
-        scratch=[pltpu.VMEM((4, 2, 2 * size_1, 128), F32)],
+        [((4, size_1, 128), F32)],
+        scratch=[pltpu.VMEM(*field), pltpu.VMEM((4, 2, 2 * size_1, 128), F32)],
         flops=2000000000,
         size=8000000,
         grant=grant,
@@ -630,12 +618,13 @@
         [(right_side.shape, F32)],
         scratch=[
             pltpu.VMEM((planes // 2 + 4, slab // 2, 128), F32),
+            pltpu.VMEM((2, 6 * slab, 128), F32),
             pltpu.VMEM((4, 3, rows, 128), F32),
         ],
         grant=grant,
     )(
-        bounds, other, source_w, scale_w, mass_w, inverse_w, power_1, power_2, basis, *levels,
-        fine, mid, coarse, gather_rows, spread_rows, expand, fold, unfold, stretch,
+        bounds, other, source_w, scale_w, mass_w, inverse_w, power_1, basis, *levels,
+        fine, mid, coarse, gather_rows, spread_rows, stretch,
     )
     return result
 

time: 35.9 us -> 34.8 us (0.969)
  Pallas kernels: 16.7 us -> 14 us
  waiting for transfers between devices: 4.6 us -> 6.2 us
    pallas_call x7, Pallas kernels: 16.7 us -> 14 us  [run(): pl.pallas_call(kernel, out_shape=outs, in_specs=specs or [VM] * len(args)...]
    ppermute x11, waiting for transfers between devices: 4.6 us -> 6.2 us  [send(): return lax.ppermute(values, AXES, swap_pairs(counts, target))]
  transfers between devices with their start and end apart: 11 -> 11, of which waited for: 6 -> 8; matrix products, arithmetic and copies ran while one was open for 3% -> 3% of each run, Pallas kernels for 20% -> 17%
where the time goes in v4:
time: 34.8 us; the launch traced here: 34.5 us
  Pallas kernels  14 us (40%)
  starting transfers between devices  12.4 us (36%)
  waiting for transfers between devices  6.2 us (18%)
  local copies, waits for them, and re-layouts  0.97 us (3%)
  other arithmetic  0.84 us (2%)
    pallas_call x7, Pallas kernels, run(): pl.pallas_call(kernel, out_shape=outs, in_specs=specs or [VM] * len(args)...  14 us
    ppermute x11, starting transfers between devices, send(): return lax.ppermute(values, AXES, swap_pairs(counts, target))  12.4 us
    ppermute x11, waiting for transfers between devices, send(): return lax.ppermute(values, AXES, swap_pairs(counts, target))  6.2 us
    concatenate x1, other arithmetic, on_device(): jnp.concatenate([right_side.reshape(12, 8, 128), stiff_scale, nodal_mass]...  0.84 us
    unnamed x1, local copies, waits for them, and re-layouts  0.8 us
  transfers between devices with their start and end apart: 11, of which 8 were waited for; matrix products, arithmetic and copies ran while one was open for 3% of the time, Pallas kernels for 17%

profile of v4, /device:TPU:0, one launch (start us, length us, event | category | flops | bytes accessed | tf_op | source)
XLA Modules:
  0.0 34.5 jit_solution(9543554275919094914)
XLA Ops:
  0.0 0.8 %pad_maximum_fusion.main = f32[20,8,128]{2,1,0:T(8,128)S(1)} fusion(f32[4,8,128]{2,1,0:T(8,128)} %param.6, f32[4,8,128]{2,1,0:T(8,128)} %param.5, f32[12,8,128]{2,1,0:T(8,128)} %bitcast.17), kind=kLoop, calls=%fused_computation | loop fusion | flops 40960 | bytes 163840 | tf_op jit(solution)/shard_map/concatenate | solution.py:573
  0.8 0.1 shard_map.46
  0.9 0.5 %collective-permute-start = (f32[10,8,128]{2,1,0:T(8,128)S(1)}, f32[10,8,128]{2,1,0:T(8,128)S(1)}, u32[]{:S(2)}, u32[]{:S(2)}) collective-permute-start(f32[10,8,128]{2,1,0:T(8,128)S(1)} %get-tuple-element.31), channel_id=1, source_target_pairs={{0,1},{1,0},{2,3},{3,2},{4,5},{5,4},{6,7},{7,6},{8,16},{9,17},{10,... | collective-permute-start | bytes 122888 | tf_op jit(solution)/shard_map/ppermute | solution.py:537
  1.4 4.1 %collective-permute-start.1 = (f32[10,8,128]{2,1,0:T(8,128)S(1)}, f32[10,8,128]{2,1,0:T(8,128)S(1)}, u32[]{:S(2)}, u32[]{:S(2)}) collective-permute-start(f32[10,8,128]{2,1,0:T(8,128)S(1)} %get-tuple-element.32), channel_id=1, source_target_pairs={{0,8},{1,9},{2,10},{3,11},{4,12},{5,13},{6,14},{7,15},{8,0},{9,1},... | collective-permute-start | bytes 122888 | tf_op jit(solution)/shard_map/ppermute | solution.py:537
  5.6 0.8 %copy.5 = f32[27,3,3]{2,1,0:T(4,128)S(1)} copy(f32[27,3,3]{0,2,1:T(4,128)} %param.7) | data formatting | bytes 1944 | tf_op args[3]
  6.4 0.2 reshape.6.blocks
  6.6 0.0 collective-permute-done.got_b
  6.6 1.0 %collective-permute-done.1.got_a = f32[10,8,128]{2,1,0:T(8,128)S(1)} collective-permute-done((f32[10,8,128]{2,1,0:T(8,128)S(1)}, f32[10,8,128]{2,1,0:T(8,128)S(1)}, u32[]{:S(2)}, u32[]{:S(2)}) %collective-permute-start.1) | collective-permute-done | bytes 40992 | tf_op jit(solution)/shard_map/ppermute | solution.py:537
  7.6 0.1 shard_map.47
  7.7 2.5 %collective-permute-start.4 = (f32[20,8,256]{2,1,0:T(8,128)S(1)}, f32[20,8,256]{2,1,0:T(8,128)S(1)}, u32[]{:S(2)}, u32[]{:S(2)}) collective-permute-start(f32[20,8,256]{2,1,0:T(8,128)S(1)} %shard_map.47), channel_id=1, source_target_pairs={{0,6},{1,7},{2,4},{3,5},{4,2},{5,3},{6,0},{7,1},{8,14},{9,15},{10,... | collective-permute-start | bytes 491528 | tf_op jit(solution)/shard_map/ppermute | solution.py:537
  10.2 0.5 %collective-permute-start.3 = (f32[20,8,256]{2,1,0:T(8,128)S(1)}, f32[20,8,256]{2,1,0:T(8,128)S(1)}, u32[]{:S(2)}, u32[]{:S(2)}) collective-permute-start(f32[20,8,256]{2,1,0:T(8,128)S(1)} %shard_map.47), channel_id=1, source_target_pairs={{0,4},{1,5},{2,6},{3,7},{4,0},{5,1},{6,2},{7,3},{8,12},{9,13},{10,... | collective-permute-start | bytes 491528 | tf_op jit(solution)/shard_map/ppermute | solution.py:537
  10.7 0.5 %collective-permute-start.2 = (f32[20,8,256]{2,1,0:T(8,128)S(1)}, f32[20,8,256]{2,1,0:T(8,128)S(1)}, u32[]{:S(2)}, u32[]{:S(2)}) collective-permute-start(f32[20,8,256]{2,1,0:T(8,128)S(1)} %shard_map.47), channel_id=1, source_target_pairs={{0,2},{1,3},{2,0},{3,1},{4,6},{5,7},{6,4},{7,5},{8,10},{9,11},{10,... | collective-permute-start | bytes 491528 | tf_op jit(solution)/shard_map/ppermute | solution.py:537
  11.2 1.9 %shard_map.48 = (bf16[2,432,256]{2,1,0:T(8,128)(2,1)S(1)}, bf16[432,256]{1,0:T(8,128)(2,1)S(1)}, bf16[72,256]{1,0:T(8,128)(2,1)S(1)}, bf16[72,256]{1,0:T(8,128)(...) custom-call(f32[243]{0:T(256)S(1)} %reshape.6.blocks), custom_call_target="tpu_custom_call" | custom-call | flops 5000000000 | bytes 8000000 | tf_op jit(solution)/shard_map/pallas_call | solution.py:26
  13.1 0.1 collective-permute-start.5
  13.2 2.3 %collective-permute-done.4 = f32[20,8,256]{2,1,0:T(8,128)S(1)} collective-permute-done((f32[20,8,256]{2,1,0:T(8,128)S(1)}, f32[20,8,256]{2,1,0:T(8,128)S(1)}, u32[]{:S(2)}, u32[]{:S(2)}) %collective-permute-start.4) | collective-permute-done | bytes 163872 | tf_op jit(solution)/shard_map/ppermute | solution.py:537
  15.5 1.4 %collective-permute-done.3 = f32[20,8,256]{2,1,0:T(8,128)S(1)} collective-permute-done((f32[20,8,256]{2,1,0:T(8,128)S(1)}, f32[20,8,256]{2,1,0:T(8,128)S(1)}, u32[]{:S(2)}, u32[]{:S(2)}) %collective-permute-start.3) | collective-permute-done | bytes 163872 | tf_op jit(solution)/shard_map/ppermute | solution.py:537
  16.9 0.0 collective-permute-start.7
  16.9 0.1 collective-permute-done.2
  17.0 0.5 %collective-permute-start.6 = (f32[20,8,256]{2,1,0:T(8,128)S(1)}, f32[20,8,256]{2,1,0:T(8,128)S(1)}, u32[]{:S(2)}, u32[]{:S(2)}) collective-permute-start(f32[20,8,256]{2,1,0:T(8,128)S(1)} %collective-permute-done.2), channel_id=1, source_target_pairs={{0,1},{1,0},{2,3},{3,2},{4,5},{5,4},{6,7},{7,6},{8,9},{9,8},{10,11... | collective-permute-start | bytes 491528 | tf_op jit(solution)/shard_map/ppermute | solution.py:537
  17.4 0.1 collective-permute-start.8
  17.5 0.0 collective-permute-done.5
  17.5 0.8 %collective-permute-done.7 = f32[20,8,256]{2,1,0:T(8,128)S(1)} collective-permute-done((f32[20,8,256]{2,1,0:T(8,128)S(1)}, f32[20,8,256]{2,1,0:T(8,128)S(1)}, u32[]{:S(2)}, u32[]{:S(2)}) %collective-permute-start.7) | collective-permute-done | bytes 163872 | tf_op jit(solution)/shard_map/ppermute | solution.py:537
  18.3 0.2 collective-permute-done.6
  18.6 0.3 collective-permute-done.8
  18.8 1.8 %shard_map.49 = (f32[22,3,16,256]{3,2,1,0:T(8,128)S(1)}, f32[22,16,256]{2,1,0:T(8,128)S(1)}, f32[22,16,256]{2,1,0:T(8,128)S(1)}, f32[22,3,16,256]{3,2,1,0:T(8,12...) custom-call(f32[243]{0:T(256)S(1)} %reshape.6.blocks, ...), custom_call_target="tpu_custom_call" | custom-call | flops 1000000 | bytes 100000 | tf_op jit(solution)/shard_map/pallas_call | solution.py:26
  20.6 1.8 %collective-permute-start.9 = (f32[3,8,128]{2,1,0:T(8,128)S(1)}, f32[3,8,128]{2,1,0:T(8,128)S(1)}, u32[]{:S(2)}, u32[]{:S(2)}) collective-permute-start(f32[3,8,128]{2,1,0:T(8,128)S(1)} %get-tuple-element.41), channel_id=1, source_target_pairs={{0,9},{1,8},{2,11},{3,10},{4,13},{5,12},{6,15},{7,14},{8,1},{9,0},... | collective-permute-start | bytes 36872 | tf_op jit(solution)/shard_map/ppermute | solution.py:537
  22.4 1.3 %shard_map.50.power_1 = f32[22,3,16,256]{3,2,1,0:T(8,128)S(1)} custom-call(f32[22,16,256]{2,1,0:T(8,128)S(1)} %get-tuple-element.43.scale_w, f32[22,16,256]{2,1,0:T(8,128)S(1)} %get-tuple-element.44.mass_w, f32[22,3,16,256]{3,2,1,0:T(8,128)S(1)} %get-tuple-element.45.inverse_w, f32[22,3,16,256]{3,2,1,0:T(8,128)S(1)} %get-tuple-element.42.source_w, ...), custom_call_target="tpu_custom_call" | custom-call | flops 1000000000 | bytes 4000000 | tf_op jit(solution)/shard_map/pallas_call | solution.py:26
  23.7 0.1 collective-permute-done.9
  23.8 1.8 %collective-permute-start.10 = (f32[3,8,128]{2,1,0:T(8,128)S(1)}, f32[3,8,128]{2,1,0:T(8,128)S(1)}, u32[]{:S(2)}, u32[]{:S(2)}) collective-permute-start(f32[3,8,128]{2,1,0:T(8,128)S(1)} %max.3.bounds_a), channel_id=1, source_target_pairs={{0,17},{1,16},{2,19},{3,18},{4,21},{5,20},{6,23},{7,22},{8,25},{9,... | collective-permute-start | bytes 36872 | tf_op jit(solution)/shard_map/ppermute | solution.py:537
  25.6 2.6 %shard_map.51.basis = f32[4,192,128]{2,1,0:T(8,128)S(1)} custom-call(f32[22,16,256]{2,1,0:T(8,128)S(1)} %get-tuple-element.43.scale_w, f32[22,16,256]{2,1,0:T(8,128)S(1)} %get-tuple-element.44.mass_w, f32[22,3,16,256]{3,2,1,0:T(8,128)S(1)} %get-tuple-element.45.inverse_w, f32[22,3,16,256]{3,2,1,0:T(8,128)S(1)} %get-tuple-element.42.source_w, ...), custom_call_target="tpu_custom_call" | custom-call | flops 2000000000 | bytes 8000000 | tf_op jit(solution)/shard_map/pallas_call | solution.py:26
  28.2 0.0 collective-permute-done.10.bounds_b
  28.3 6.3 %shard_map.52 = f32[3,4,8,128]{3,2,1,0:T(8,128)} custom-call(f32[3,8,128]{2,1,0:T(8,128)S(1)} %max.3.bounds_a, f32[3,8,128]{2,1,0:T(8,128)S(1)} %collective-permute-done.10.bounds_b, f32[22,3,16,256]{3,2,1,0:T(8,128)S(1)} %get-tuple-element.42.source_w, f32[22,16,256]{2,1,0:T(8,128)S(1)} %get-tuple-element.43.scale_w, ...), custom_call_target="tpu_custom_call" | custom-call | flops 1000000 | bytes 100000 | tf_op jit(solution)/shard_map/pallas_call | solution.py:26
  (1 shorter events, 0.0 us)
Async XLA Ops:
  0.9 5.6 %collective-permute-start = (f32[10,8,128]{2,1,0:T(8,128)S(1)}, f32[10,8,128]{2,1,0:T(8,128)S(1)}, u32[]{:S(2)}, u32[]{:S(2)}) collective-permute-start(f32[10,8,128]{2,1,0:T(8,128)S(1)} %get-tuple-element.31), channel_id=1, source_target_pairs={{0,1},{1,0},{2,3},{3,2},{4,5},{5,4},{6,7},{7,6},{8,16},{9,17},{10,... | collective-permute-start | bytes 122888 | tf_op jit(solution)/shard_map/ppermute | solution.py:537
  1.4 6.1 %collective-permute-start.1 = (f32[10,8,128]{2,1,0:T(8,128)S(1)}, f32[10,8,128]{2,1,0:T(8,128)S(1)}, u32[]{:S(2)}, u32[]{:S(2)}) collective-permute-start(f32[10,8,128]{2,1,0:T(8,128)S(1)} %get-tuple-element.32), channel_id=1, source_target_pairs={{0,8},{1,9},{2,10},{3,11},{4,12},{5,13},{6,14},{7,15},{8,0},{9,1},... | collective-permute-start | bytes 122888 | tf_op jit(solution)/shard_map/ppermute | solution.py:537
  7.7 7.9 %collective-permute-start.4 = (f32[20,8,256]{2,1,0:T(8,128)S(1)}, f32[20,8,256]{2,1,0:T(8,128)S(1)}, u32[]{:S(2)}, u32[]{:S(2)}) collective-permute-start(f32[20,8,256]{2,1,0:T(8,128)S(1)} %shard_map.47), channel_id=1, source_target_pairs={{0,6},{1,7},{2,4},{3,5},{4,2},{5,3},{6,0},{7,1},{8,14},{9,15},{10,... | collective-permute-start | bytes 491528 | tf_op jit(solution)/shard_map/ppermute | solution.py:537
  10.2 6.8 %collective-permute-start.3 = (f32[20,8,256]{2,1,0:T(8,128)S(1)}, f32[20,8,256]{2,1,0:T(8,128)S(1)}, u32[]{:S(2)}, u32[]{:S(2)}) collective-permute-start(f32[20,8,256]{2,1,0:T(8,128)S(1)} %shard_map.47), channel_id=1, source_target_pairs={{0,4},{1,5},{2,6},{3,7},{4,0},{5,1},{6,2},{7,3},{8,12},{9,13},{10,... | collective-permute-start | bytes 491528 | tf_op jit(solution)/shard_map/ppermute | solution.py:537
  10.7 6.3 %collective-permute-start.2 = (f32[20,8,256]{2,1,0:T(8,128)S(1)}, f32[20,8,256]{2,1,0:T(8,128)S(1)}, u32[]{:S(2)}, u32[]{:S(2)}) collective-permute-start(f32[20,8,256]{2,1,0:T(8,128)S(1)} %shard_map.47), channel_id=1, source_target_pairs={{0,2},{1,3},{2,0},{3,1},{4,6},{5,7},{6,4},{7,5},{8,10},{9,11},{10,... | collective-permute-start | bytes 491528 | tf_op jit(solution)/shard_map/ppermute | solution.py:537
  13.1 4.4 %collective-permute-start.5 = (f32[20,8,256]{2,1,0:T(8,128)S(1)}, f32[20,8,256]{2,1,0:T(8,128)S(1)}, u32[]{:S(2)}, u32[]{:S(2)}) collective-permute-start(f32[20,8,256]{2,1,0:T(8,128)S(1)} %shard_map.47), channel_id=1, source_target_pairs={{0,1},{1,0},{2,3},{3,2},{4,5},{5,4},{6,7},{7,6},{8,9},{9,8},{10,11... | collective-permute-start | bytes 491528 | tf_op jit(solution)/shard_map/ppermute | solution.py:537
  16.9 1.4 %collective-permute-start.7 = (f32[20,8,256]{2,1,0:T(8,128)S(1)}, f32[20,8,256]{2,1,0:T(8,128)S(1)}, u32[]{:S(2)}, u32[]{:S(2)}) collective-permute-start(f32[20,8,256]{2,1,0:T(8,128)S(1)} %collective-permute-done.3), channel_id=1, source_target_pairs={{0,1},{1,0},{2,3},{3,2},{4,5},{5,4},{6,7},{7,6},{8,9},{9,8},{10,11... | collective-permute-start | bytes 491528 | tf_op jit(solution)/shard_map/ppermute | solution.py:537
  17.0 1.6 %collective-permute-start.6 = (f32[20,8,256]{2,1,0:T(8,128)S(1)}, f32[20,8,256]{2,1,0:T(8,128)S(1)}, u32[]{:S(2)}, u32[]{:S(2)}) collective-permute-start(f32[20,8,256]{2,1,0:T(8,128)S(1)} %collective-permute-done.2), channel_id=1, source_target_pairs={{0,1},{1,0},{2,3},{3,2},{4,5},{5,4},{6,7},{7,6},{8,9},{9,8},{10,11... | collective-permute-start | bytes 491528 | tf_op jit(solution)/shard_map/ppermute | solution.py:537
  17.4 1.4 %collective-permute-start.8 = (f32[20,8,256]{2,1,0:T(8,128)S(1)}, f32[20,8,256]{2,1,0:T(8,128)S(1)}, u32[]{:S(2)}, u32[]{:S(2)}) collective-permute-start(f32[20,8,256]{2,1,0:T(8,128)S(1)} %collective-permute-done.4), channel_id=1, source_target_pairs={{0,1},{1,0},{2,3},{3,2},{4,5},{5,4},{6,7},{7,6},{8,9},{9,8},{10,11... | collective-permute-start | bytes 491528 | tf_op jit(solution)/shard_map/ppermute | solution.py:537
  20.6 3.2 %collective-permute-start.9 = (f32[3,8,128]{2,1,0:T(8,128)S(1)}, f32[3,8,128]{2,1,0:T(8,128)S(1)}, u32[]{:S(2)}, u32[]{:S(2)}) collective-permute-start(f32[3,8,128]{2,1,0:T(8,128)S(1)} %get-tuple-element.41), channel_id=1, source_target_pairs={{0,9},{1,8},{2,11},{3,10},{4,13},{5,12},{6,15},{7,14},{8,1},{9,0},... | collective-permute-start | bytes 36872 | tf_op jit(solution)/shard_map/ppermute | solution.py:537
  23.8 4.4 %collective-permute-start.10 = (f32[3,8,128]{2,1,0:T(8,128)S(1)}, f32[3,8,128]{2,1,0:T(8,128)S(1)}, u32[]{:S(2)}, u32[]{:S(2)}) collective-permute-start(f32[3,8,128]{2,1,0:T(8,128)S(1)} %max.3.bounds_a), channel_id=1, source_target_pairs={{0,17},{1,16},{2,19},{3,18},{4,21},{5,20},{6,23},{7,22},{8,25},{9,... | collective-permute-start | bytes 36872 | tf_op jit(solution)/shard_map/ppermute | solution.py:537

commit v5 on v4

--- a/solution.py
+++ b/solution.py
@@ -61,11 +61,6 @@
     width = values.shape[1]
     product = dot(selection, jnp.concatenate(split(values), axis=1))
     return product[:, :width] + product[:, width:]
-
-
-def banded(matrix_high, matrix_low, values):
-    high, low = split(values)
-    return dot(matrix_high, high) + dot(matrix_low, high) + dot(matrix_high, low)
 
 
 def banded_stacked(matrix, values):
@@ -118,20 +113,19 @@
     return sizes
 
 
-def fine_stencil(matrix, values):
-    planes, rows = values.shape[0] - 2, values.shape[2]
+def fine_operator(matrix, scale_of, mass_of, weighted_of, value_of, planes, rows, finish):
     slab = 3 * rows
-    flat = values.reshape((planes + 2) * slab, LANES)
-    outs = []
-    at = 0
-    for size in groups(planes, group_of(slab)):
-        height, depth = size * 3 * slab, (size + 2) * slab
-        product = banded(
-            matrix[0, :height, :depth], matrix[1, :height, :depth], flat[at * slab : at * slab + depth]
-        )
-        outs.append(shifted_sum(product, size, slab, LANES))
-        at += size
-    return jnp.concatenate(outs, axis=0).reshape(planes, 3, rows, LANES)
+    parts = {}
+    for plane in range(planes):
+        near = range(plane - 1, plane + 2)
+        for i in near:
+            if i not in parts:
+                parts[i] = split(weighted_of(i).reshape(slab, LANES))
+        high = [parts[i][0] for i in near]
+        low = [parts[i][1] for i in near]
+        product = dot(matrix[:, : 9 * slab], jnp.concatenate(high + high + low, axis=0))
+        total = shifted_sum(product, 1, slab, LANES).reshape(3, rows, LANES)
+        finish(plane, scale_of(plane)[None] * total + mass_of(plane)[None] * value_of(plane))
 
 
 def panels(value_of, others, rows, width):
@@ -196,15 +190,16 @@
 
     slab = 3 * rows
     group = group_of(slab)
-    found = panels(direct, 3, rows, fine.shape[2])
+    width = up128(3 * slab)
+    found = panels(direct, 3, rows, width)
+    value = jnp.concatenate([found[step_x, comp] for step_x in range(3) for comp in range(3)], axis=0)
+    if fine.shape[1] > width:
+        value = jnp.concatenate([value, jnp.zeros((3 * slab, fine.shape[1] - width), F32)], axis=1)
+    fine[...] = stack3(value, 3 * slab)
     bound = panels(absolute, 1, rows, fine_bound.shape[1])
     for plane in range(group):
         for step_x in range(3):
             start = (plane * 3 + step_x) * slab
-            value = turned(jnp.concatenate([found[step_x, comp] for comp in range(3)], axis=0), plane * slab)
-            high, low = split(value)
-            fine[0, start : start + slab, :] = high
-            fine[1, start : start + slab, :] = low
             value = turned(jnp.concatenate([bound[step_x, comp] for comp in range(3)], axis=0), plane * rows)
             fine_bound[start : start + slab, :] = stack3(value, (group + 2) * rows)
 
@@ -381,28 +376,37 @@
     spread_2w[...], weight_2w[...], inverse_2w[...] = spread_2, weight_2, inverse_2
 
 
-def fine_operator(matrix, scale, mass, values):
-    total = fine_stencil(matrix, scale[:, None] * values)
-    return scale[1:-1][:, None] * total + mass[:, None] * values[1:-1]
-
-
-def inner_power(scale_w, mass_w, inverse_w, matrix, values):
-    planes = scale_w.shape[0] - 2 * PAD
-    near = slice(PAD - 1, PAD + planes + 1)
-    return fine_operator(matrix, scale_w[near], mass_w[PAD : PAD + planes], inverse_w[near] * values[near])
+def inner_power(scale_w, mass_w, inverse_w, matrix, values, finish):
+    planes, rows = scale_w.shape[0] - 2 * PAD, scale_w.shape[1]
+    fine_operator(
+        matrix,
+        lambda i: scale_w[PAD + i],
+        lambda i: mass_w[PAD + i],
+        lambda i: scale_w[PAD + i][None] * (inverse_w[PAD + i] * values[PAD + i]),
+        lambda i: inverse_w[PAD + i] * values[PAD + i],
+        planes,
+        rows,
+        finish,
+    )
 
 
 def power_kernel(scale_w, mass_w, inverse_w, source_w, fine, power):
     planes, shape = scale_w.shape[0] - 2 * PAD, power.shape[1:]
     power[:PAD] = jnp.zeros((PAD,) + shape, F32)
     power[PAD + planes :] = jnp.zeros((PAD,) + shape, F32)
-    power[PAD : PAD + planes] = inner_power(scale_w, mass_w, inverse_w, fine, source_w)
+
+    def finish(at, values):
+        power[PAD + at] = values
+
+    inner_power(scale_w, mass_w, inverse_w, fine, source_w, finish)
 
 
 def restrict_kernel(scale_w, mass_w, inverse_w, source_w, power_1, fine, squeeze, basis, power_2, held):
     planes, rows = scale_w.shape[0] - 2 * PAD, scale_w.shape[1]
     power_kernel(scale_w, mass_w, inverse_w, power_1, fine, power_2)
-    third = inner_power(scale_w, mass_w, inverse_w, fine, power_2)
+    third = []
+    inner_power(scale_w, mass_w, inverse_w, fine, power_2, lambda at, values: third.append(values))
+    third = jnp.stack(third, axis=0)
     inner = slice(PAD, PAD + planes)
     size = planes // 2 * 3 * rows
     for at, values in enumerate((source_w[inner], power_1[inner], power_2[inner], third)):
@@ -505,11 +509,26 @@
     inverse = scaled(over_0, near_own(inverse_w, 2))
     source = near_own(source_w, 2)
     before = gamma * source - scaled(over_0, beta * near_own(power_1, 2))
-    image = fine_operator(fine, scale, mass, error)
+
+    def apply(values, edge):
+        outs = []
+        fine_operator(
+            fine,
+            lambda i: scale[i + 4 - edge],
+            lambda i: mass[i + 3 - edge],
+            lambda i: scale[i + 4 - edge][None] * values[i + 1],
+            lambda i: values[i + 1],
+            2 + 2 * edge,
+            2 * rows,
+            lambda at, result: outs.append(result),
+        )
+        return jnp.stack(outs, axis=0)
+
+    image = apply(error, 3)
     iterate = inverse * (before - omega * image) + error[1:9]
-    residue = source[1:7] - fine_operator(fine, scale[1:9], mass[1:7], iterate)
+    residue = source[1:7] - apply(iterate, 2)
     direction = first * (inverse[1:7] * residue)
-    last = residue[1:5] - fine_operator(fine, scale[2:8], mass[2:6], direction)
+    last = residue[1:5] - apply(direction, 1)
     answer = iterate[2:6] + (1.0 + hold) * direction[1:5] + push * (inverse[2:6] * last)
     answer_w[...] = answer[:, :, :, :128]
     for comp in range(3):
@@ -551,7 +570,7 @@
     ) = call(
         functools.partial(matrices_kernel, rows, planes),
         [
-            ((2, group * 3 * slab, up128((group + 2) * slab)), BF16),
+            ((3 * slab, up128(9 * slab)), BF16),
             ((group * 3 * slab, up128(3 * (group + 2) * rows)), BF16),
             ((3 * slab // 2, up128(9 * slab // 2)), BF16),
             ((3 * slab // 2, up128(9 * slab // 2)), BF16),

time: 34.8 us -> 33.8 us (0.971)
  Pallas kernels: 14 us -> 12.4 us
  waiting for transfers between devices: 6.2 us -> 6.82 us
    pallas_call x7, Pallas kernels: 14 us -> 12.4 us  [run(): pl.pallas_call(kernel, out_shape=outs, in_specs=specs or [VM] * len(args)...]
    ppermute x11, waiting for transfers between devices: 6.2 us -> 6.82 us  [send(): return lax.ppermute(values, AXES, swap_pairs(counts, target))]
  transfers between devices with their start and end apart: 11 -> 11, of which waited for: 8 -> 9; matrix products, arithmetic and copies ran while one was open for 3% -> 3% of each run, Pallas kernels for 17% -> 14%
where the time goes in v5:
time: 33.8 us; the launch traced here: 33.5 us
  Pallas kernels  12.4 us (37%)
  starting transfers between devices  12.4 us (37%)
  waiting for transfers between devices  6.82 us (20%)
  local copies, waits for them, and re-layouts  0.97 us (3%)
  other arithmetic  0.84 us (2%)
    pallas_call x7, Pallas kernels, run(): pl.pallas_call(kernel, out_shape=outs, in_specs=specs or [VM] * len(args)...  12.4 us
    ppermute x11, starting transfers between devices, send(): return lax.ppermute(values, AXES, swap_pairs(counts, target))  12.4 us
    ppermute x11, waiting for transfers between devices, send(): return lax.ppermute(values, AXES, swap_pairs(counts, target))  6.82 us
    concatenate x1, other arithmetic, on_device(): jnp.concatenate([right_side.reshape(12, 8, 128), stiff_scale, nodal_mass]...  0.84 us
    unnamed x1, local copies, waits for them, and re-layouts  0.8 us
  transfers between devices with their start and end apart: 11, of which 9 were waited for; matrix products, arithmetic and copies ran while one was open for 3% of the time, Pallas kernels for 14%

profile of v5, /device:TPU:0, one launch (start us, length us, event | category | flops | bytes accessed | tf_op | source)
XLA Modules:
  0.0 33.5 jit_solution(7972121737115612993)
XLA Ops:
  0.0 0.8 %pad_maximum_fusion.main = f32[20,8,128]{2,1,0:T(8,128)S(1)} fusion(f32[4,8,128]{2,1,0:T(8,128)} %param.6, f32[4,8,128]{2,1,0:T(8,128)} %param.5, f32[12,8,128]{2,1,0:T(8,128)} %bitcast.17), kind=kLoop, calls=%fused_computation | loop fusion | flops 40960 | bytes 163840 | tf_op jit(solution)/shard_map/concatenate | solution.py:592
  0.8 0.1 shard_map.46
  0.9 0.5 %collective-permute-start = (f32[10,8,128]{2,1,0:T(8,128)S(1)}, f32[10,8,128]{2,1,0:T(8,128)S(1)}, u32[]{:S(2)}, u32[]{:S(2)}) collective-permute-start(f32[10,8,128]{2,1,0:T(8,128)S(1)} %get-tuple-element.31), channel_id=1, source_target_pairs={{0,1},{1,0},{2,3},{3,2},{4,5},{5,4},{6,7},{7,6},{8,16},{9,17},{10,... | collective-permute-start | bytes 122888 | tf_op jit(solution)/shard_map/ppermute | solution.py:556
  1.4 4.1 %collective-permute-start.1 = (f32[10,8,128]{2,1,0:T(8,128)S(1)}, f32[10,8,128]{2,1,0:T(8,128)S(1)}, u32[]{:S(2)}, u32[]{:S(2)}) collective-permute-start(f32[10,8,128]{2,1,0:T(8,128)S(1)} %get-tuple-element.32), channel_id=1, source_target_pairs={{0,8},{1,9},{2,10},{3,11},{4,12},{5,13},{6,14},{7,15},{8,0},{9,1},... | collective-permute-start | bytes 122888 | tf_op jit(solution)/shard_map/ppermute | solution.py:556
  5.6 0.8 %copy.5 = f32[27,3,3]{2,1,0:T(4,128)S(1)} copy(f32[27,3,3]{0,2,1:T(4,128)} %param.7) | data formatting | bytes 1944 | tf_op args[3]
  6.4 0.2 reshape.6.blocks
  6.6 0.0 collective-permute-done.got_b
  6.6 1.0 %collective-permute-done.1.got_a = f32[10,8,128]{2,1,0:T(8,128)S(1)} collective-permute-done((f32[10,8,128]{2,1,0:T(8,128)S(1)}, f32[10,8,128]{2,1,0:T(8,128)S(1)}, u32[]{:S(2)}, u32[]{:S(2)}) %collective-permute-start.1) | collective-permute-done | bytes 40992 | tf_op jit(solution)/shard_map/ppermute | solution.py:556
  7.6 0.1 shard_map.47
  7.7 2.5 %collective-permute-start.4 = (f32[20,8,256]{2,1,0:T(8,128)S(1)}, f32[20,8,256]{2,1,0:T(8,128)S(1)}, u32[]{:S(2)}, u32[]{:S(2)}) collective-permute-start(f32[20,8,256]{2,1,0:T(8,128)S(1)} %shard_map.47), channel_id=1, source_target_pairs={{0,6},{1,7},{2,4},{3,5},{4,2},{5,3},{6,0},{7,1},{8,14},{9,15},{10,... | collective-permute-start | bytes 491528 | tf_op jit(solution)/shard_map/ppermute | solution.py:556
  10.2 0.5 %collective-permute-start.3 = (f32[20,8,256]{2,1,0:T(8,128)S(1)}, f32[20,8,256]{2,1,0:T(8,128)S(1)}, u32[]{:S(2)}, u32[]{:S(2)}) collective-permute-start(f32[20,8,256]{2,1,0:T(8,128)S(1)} %shard_map.47), channel_id=1, source_target_pairs={{0,4},{1,5},{2,6},{3,7},{4,0},{5,1},{6,2},{7,3},{8,12},{9,13},{10,... | collective-permute-start | bytes 491528 | tf_op jit(solution)/shard_map/ppermute | solution.py:556
  10.7 0.5 %collective-permute-start.2 = (f32[20,8,256]{2,1,0:T(8,128)S(1)}, f32[20,8,256]{2,1,0:T(8,128)S(1)}, u32[]{:S(2)}, u32[]{:S(2)}) collective-permute-start(f32[20,8,256]{2,1,0:T(8,128)S(1)} %shard_map.47), channel_id=1, source_target_pairs={{0,2},{1,3},{2,0},{3,1},{4,6},{5,7},{6,4},{7,5},{8,10},{9,11},{10,... | collective-permute-start | bytes 491528 | tf_op jit(solution)/shard_map/ppermute | solution.py:556
  11.2 1.8 %shard_map.48 = (bf16[144,512]{1,0:T(8,128)(2,1)S(1)}, bf16[432,256]{1,0:T(8,128)(2,1)S(1)}, bf16[72,256]{1,0:T(8,128)(2,1)S(1)}, bf16[72,256]{1,0:T(8,128)(2,1)...) custom-call(f32[243]{0:T(256)S(1)} %reshape.6.blocks), custom_call_target="tpu_custom_call" | custom-call | flops 5000000000 | bytes 8000000 | tf_op jit(solution)/shard_map/pallas_call | solution.py:26
  13.1 0.1 collective-permute-start.5
  13.1 2.4 %collective-permute-done.4 = f32[20,8,256]{2,1,0:T(8,128)S(1)} collective-permute-done((f32[20,8,256]{2,1,0:T(8,128)S(1)}, f32[20,8,256]{2,1,0:T(8,128)S(1)}, u32[]{:S(2)}, u32[]{:S(2)}) %collective-permute-start.4) | collective-permute-done | bytes 163872 | tf_op jit(solution)/shard_map/ppermute | solution.py:556
  15.5 1.4 %collective-permute-done.3 = f32[20,8,256]{2,1,0:T(8,128)S(1)} collective-permute-done((f32[20,8,256]{2,1,0:T(8,128)S(1)}, f32[20,8,256]{2,1,0:T(8,128)S(1)}, u32[]{:S(2)}, u32[]{:S(2)}) %collective-permute-start.3) | collective-permute-done | bytes 163872 | tf_op jit(solution)/shard_map/ppermute | solution.py:556
  16.9 0.0 collective-permute-start.7
  16.9 0.1 collective-permute-done.2
  17.0 0.5 %collective-permute-start.6 = (f32[20,8,256]{2,1,0:T(8,128)S(1)}, f32[20,8,256]{2,1,0:T(8,128)S(1)}, u32[]{:S(2)}, u32[]{:S(2)}) collective-permute-start(f32[20,8,256]{2,1,0:T(8,128)S(1)} %collective-permute-done.2), channel_id=1, source_target_pairs={{0,1},{1,0},{2,3},{3,2},{4,5},{5,4},{6,7},{7,6},{8,9},{9,8},{10,11... | collective-permute-start | bytes 491528 | tf_op jit(solution)/shard_map/ppermute | solution.py:556
  17.4 0.1 collective-permute-start.8
  17.5 0.0 collective-permute-done.5
  17.5 0.8 %collective-permute-done.7 = f32[20,8,256]{2,1,0:T(8,128)S(1)} collective-permute-done((f32[20,8,256]{2,1,0:T(8,128)S(1)}, f32[20,8,256]{2,1,0:T(8,128)S(1)}, u32[]{:S(2)}, u32[]{:S(2)}) %collective-permute-start.7) | collective-permute-done | bytes 163872 | tf_op jit(solution)/shard_map/ppermute | solution.py:556
  18.3 0.2 collective-permute-done.6
  18.6 0.3 collective-permute-done.8
  18.8 1.8 %shard_map.49 = (f32[22,3,16,256]{3,2,1,0:T(8,128)S(1)}, f32[22,16,256]{2,1,0:T(8,128)S(1)}, f32[22,16,256]{2,1,0:T(8,128)S(1)}, f32[22,3,16,256]{3,2,1,0:T(8,12...) custom-call(f32[243]{0:T(256)S(1)} %reshape.6.blocks, ...), custom_call_target="tpu_custom_call" | custom-call | flops 1000000 | bytes 100000 | tf_op jit(solution)/shard_map/pallas_call | solution.py:26
  20.6 1.8 %collective-permute-start.9 = (f32[3,8,128]{2,1,0:T(8,128)S(1)}, f32[3,8,128]{2,1,0:T(8,128)S(1)}, u32[]{:S(2)}, u32[]{:S(2)}) collective-permute-start(f32[3,8,128]{2,1,0:T(8,128)S(1)} %get-tuple-element.41), channel_id=1, source_target_pairs={{0,9},{1,8},{2,11},{3,10},{4,13},{5,12},{6,15},{7,14},{8,1},{9,0},... | collective-permute-start | bytes 36872 | tf_op jit(solution)/shard_map/ppermute | solution.py:556
  22.4 1.0 %shard_map.50.power_1 = f32[22,3,16,256]{3,2,1,0:T(8,128)S(1)} custom-call(f32[22,16,256]{2,1,0:T(8,128)S(1)} %get-tuple-element.43.scale_w, f32[22,16,256]{2,1,0:T(8,128)S(1)} %get-tuple-element.44.mass_w, f32[22,3,16,256]{3,2,1,0:T(8,128)S(1)} %get-tuple-element.45.inverse_w, f32[22,3,16,256]{3,2,1,0:T(8,128)S(1)} %get-tuple-element.42.source_w, ...), custom_call_target="tpu_custom_call" | custom-call | flops 1000000000 | bytes 4000000 | tf_op jit(solution)/shard_map/pallas_call | solution.py:26
  23.4 0.4 %collective-permute-done.9 = f32[3,8,128]{2,1,0:T(8,128)S(1)} collective-permute-done((f32[3,8,128]{2,1,0:T(8,128)S(1)}, f32[3,8,128]{2,1,0:T(8,128)S(1)}, u32[]{:S(2)}, u32[]{:S(2)}) %collective-permute-start.9) | collective-permute-done | bytes 12320 | tf_op jit(solution)/shard_map/ppermute | solution.py:556
  23.8 1.8 %collective-permute-start.10 = (f32[3,8,128]{2,1,0:T(8,128)S(1)}, f32[3,8,128]{2,1,0:T(8,128)S(1)}, u32[]{:S(2)}, u32[]{:S(2)}) collective-permute-start(f32[3,8,128]{2,1,0:T(8,128)S(1)} %max.3.bounds_a), channel_id=1, source_target_pairs={{0,17},{1,16},{2,19},{3,18},{4,21},{5,20},{6,23},{7,22},{8,25},{9,... | collective-permute-start | bytes 36872 | tf_op jit(solution)/shard_map/ppermute | solution.py:556
  25.6 2.0 %shard_map.51.basis = f32[4,192,128]{2,1,0:T(8,128)S(1)} custom-call(f32[22,16,256]{2,1,0:T(8,128)S(1)} %get-tuple-element.43.scale_w, f32[22,16,256]{2,1,0:T(8,128)S(1)} %get-tuple-element.44.mass_w, f32[22,3,16,256]{3,2,1,0:T(8,128)S(1)} %get-tuple-element.45.inverse_w, f32[22,3,16,256]{3,2,1,0:T(8,128)S(1)} %get-tuple-element.42.source_w, ...), custom_call_target="tpu_custom_call" | custom-call | flops 2000000000 | bytes 8000000 | tf_op jit(solution)/shard_map/pallas_call | solution.py:26
  27.7 0.2 collective-permute-done.10.bounds_b
  27.8 5.7 %shard_map.52 = f32[3,4,8,128]{3,2,1,0:T(8,128)} custom-call(f32[3,8,128]{2,1,0:T(8,128)S(1)} %max.3.bounds_a, f32[3,8,128]{2,1,0:T(8,128)S(1)} %collective-permute-done.10.bounds_b, f32[22,3,16,256]{3,2,1,0:T(8,128)S(1)} %get-tuple-element.42.source_w, f32[22,16,256]{2,1,0:T(8,128)S(1)} %get-tuple-element.43.scale_w, ...), custom_call_target="tpu_custom_call" | custom-call | flops 1000000 | bytes 100000 | tf_op jit(solution)/shard_map/pallas_call | solution.py:26
  (1 shorter events, 0.0 us)
Async XLA Ops:
  0.9 5.6 %collective-permute-start = (f32[10,8,128]{2,1,0:T(8,128)S(1)}, f32[10,8,128]{2,1,0:T(8,128)S(1)}, u32[]{:S(2)}, u32[]{:S(2)}) collective-permute-start(f32[10,8,128]{2,1,0:T(8,128)S(1)} %get-tuple-element.31), channel_id=1, source_target_pairs={{0,1},{1,0},{2,3},{3,2},{4,5},{5,4},{6,7},{7,6},{8,16},{9,17},{10,... | collective-permute-start | bytes 122888 | tf_op jit(solution)/shard_map/ppermute | solution.py:556
  1.4 6.1 %collective-permute-start.1 = (f32[10,8,128]{2,1,0:T(8,128)S(1)}, f32[10,8,128]{2,1,0:T(8,128)S(1)}, u32[]{:S(2)}, u32[]{:S(2)}) collective-permute-start(f32[10,8,128]{2,1,0:T(8,128)S(1)} %get-tuple-element.32), channel_id=1, source_target_pairs={{0,8},{1,9},{2,10},{3,11},{4,12},{5,13},{6,14},{7,15},{8,0},{9,1},... | collective-permute-start | bytes 122888 | tf_op jit(solution)/shard_map/ppermute | solution.py:556
  7.7 7.9 %collective-permute-start.4 = (f32[20,8,256]{2,1,0:T(8,128)S(1)}, f32[20,8,256]{2,1,0:T(8,128)S(1)}, u32[]{:S(2)}, u32[]{:S(2)}) collective-permute-start(f32[20,8,256]{2,1,0:T(8,128)S(1)} %shard_map.47), channel_id=1, source_target_pairs={{0,6},{1,7},{2,4},{3,5},{4,2},{5,3},{6,0},{7,1},{8,14},{9,15},{10,... | collective-permute-start | bytes 491528 | tf_op jit(solution)/shard_map/ppermute | solution.py:556
  10.2 6.8 %collective-permute-start.3 = (f32[20,8,256]{2,1,0:T(8,128)S(1)}, f32[20,8,256]{2,1,0:T(8,128)S(1)}, u32[]{:S(2)}, u32[]{:S(2)}) collective-permute-start(f32[20,8,256]{2,1,0:T(8,128)S(1)} %shard_map.47), channel_id=1, source_target_pairs={{0,4},{1,5},{2,6},{3,7},{4,0},{5,1},{6,2},{7,3},{8,12},{9,13},{10,... | collective-permute-start | bytes 491528 | tf_op jit(solution)/shard_map/ppermute | solution.py:556
  10.7 6.3 %collective-permute-start.2 = (f32[20,8,256]{2,1,0:T(8,128)S(1)}, f32[20,8,256]{2,1,0:T(8,128)S(1)}, u32[]{:S(2)}, u32[]{:S(2)}) collective-permute-start(f32[20,8,256]{2,1,0:T(8,128)S(1)} %shard_map.47), channel_id=1, source_target_pairs={{0,2},{1,3},{2,0},{3,1},{4,6},{5,7},{6,4},{7,5},{8,10},{9,11},{10,... | collective-permute-start | bytes 491528 | tf_op jit(solution)/shard_map/ppermute | solution.py:556
  13.1 4.4 %collective-permute-start.5 = (f32[20,8,256]{2,1,0:T(8,128)S(1)}, f32[20,8,256]{2,1,0:T(8,128)S(1)}, u32[]{:S(2)}, u32[]{:S(2)}) collective-permute-start(f32[20,8,256]{2,1,0:T(8,128)S(1)} %shard_map.47), channel_id=1, source_target_pairs={{0,1},{1,0},{2,3},{3,2},{4,5},{5,4},{6,7},{7,6},{8,9},{9,8},{10,11... | collective-permute-start | bytes 491528 | tf_op jit(solution)/shard_map/ppermute | solution.py:556
  16.9 1.4 %collective-permute-start.7 = (f32[20,8,256]{2,1,0:T(8,128)S(1)}, f32[20,8,256]{2,1,0:T(8,128)S(1)}, u32[]{:S(2)}, u32[]{:S(2)}) collective-permute-start(f32[20,8,256]{2,1,0:T(8,128)S(1)} %collective-permute-done.3), channel_id=1, source_target_pairs={{0,1},{1,0},{2,3},{3,2},{4,5},{5,4},{6,7},{7,6},{8,9},{9,8},{10,11... | collective-permute-start | bytes 491528 | tf_op jit(solution)/shard_map/ppermute | solution.py:556
  17.0 1.6 %collective-permute-start.6 = (f32[20,8,256]{2,1,0:T(8,128)S(1)}, f32[20,8,256]{2,1,0:T(8,128)S(1)}, u32[]{:S(2)}, u32[]{:S(2)}) collective-permute-start(f32[20,8,256]{2,1,0:T(8,128)S(1)} %collective-permute-done.2), channel_id=1, source_target_pairs={{0,1},{1,0},{2,3},{3,2},{4,5},{5,4},{6,7},{7,6},{8,9},{9,8},{10,11... | collective-permute-start | bytes 491528 | tf_op jit(solution)/shard_map/ppermute | solution.py:556
  17.4 1.4 %collective-permute-start.8 = (f32[20,8,256]{2,1,0:T(8,128)S(1)}, f32[20,8,256]{2,1,0:T(8,128)S(1)}, u32[]{:S(2)}, u32[]{:S(2)}) collective-permute-start(f32[20,8,256]{2,1,0:T(8,128)S(1)} %collective-permute-done.4), channel_id=1, source_target_pairs={{0,1},{1,0},{2,3},{3,2},{4,5},{5,4},{6,7},{7,6},{8,9},{9,8},{10,11... | collective-permute-start | bytes 491528 | tf_op jit(solution)/shard_map/ppermute | solution.py:556
  20.6 3.2 %collective-permute-start.9 = (f32[3,8,128]{2,1,0:T(8,128)S(1)}, f32[3,8,128]{2,1,0:T(8,128)S(1)}, u32[]{:S(2)}, u32[]{:S(2)}) collective-permute-start(f32[3,8,128]{2,1,0:T(8,128)S(1)} %get-tuple-element.41), channel_id=1, source_target_pairs={{0,9},{1,8},{2,11},{3,10},{4,13},{5,12},{6,15},{7,14},{8,1},{9,0},... | collective-permute-start | bytes 36872 | tf_op jit(solution)/shard_map/ppermute | solution.py:556
  23.8 4.0 %collective-permute-start.10 = (f32[3,8,128]{2,1,0:T(8,128)S(1)}, f32[3,8,128]{2,1,0:T(8,128)S(1)}, u32[]{:S(2)}, u32[]{:S(2)}) collective-permute-start(f32[3,8,128]{2,1,0:T(8,128)S(1)} %max.3.bounds_a), channel_id=1, source_target_pairs={{0,17},{1,16},{2,19},{3,18},{4,21},{5,20},{6,23},{7,22},{8,25},{9,... | collective-permute-start | bytes 36872 | tf_op jit(solution)/shard_map/ppermute | solution.py:556

commit v6 on v5

--- a/solution.py
+++ b/solution.py
@@ -15,6 +15,7 @@
 VM = pl.BlockSpec(memory_space=pltpu.VMEM)
 SM = pl.BlockSpec(memory_space=pltpu.SMEM)
 LANES = 256
+LINE = 384
 PAD = 3
 
 
@@ -69,8 +70,8 @@
 
 
 def banded_planes(matrix, values, planes, step):
-    slab = values.shape[0] // planes
-    edge = jnp.zeros((slab, 128), F32)
+    slab, lanes = values.shape[0] // planes, values.shape[1]
+    edge = jnp.zeros((slab, lanes), F32)
     padded = jnp.concatenate([edge, values, edge], axis=0)
     beside = jnp.concatenate([padded[at * slab : (at + 3) * slab] for at in range(planes)], axis=1)
     high = beside.astype(BF16).astype(F32)
@@ -79,15 +80,15 @@
     outs = []
     for at in range(planes):
         below, here, above = (
-            product[part * slab : part * slab + slab, at * 128 : at * 128 + 128] for part in range(3)
+            product[part * slab : part * slab + slab, at * lanes : at * lanes + lanes] for part in range(3)
         )
-        outs.append(here + pltpu.roll(below, step, 1) + pltpu.roll(above, 128 - step, 1))
+        outs.append(here + pltpu.roll(below, step, 1) + pltpu.roll(above, lanes - step, 1))
     return jnp.concatenate(outs, axis=0)
 
 
 def paired_lanes(values):
     even = iota(values.shape, 1) % 2 == 0
-    return values + jnp.where(even, pltpu.roll(values, 127, 1), pltpu.roll(values, 1, 1))
+    return values + jnp.where(even, pltpu.roll(values, values.shape[1] - 1, 1), pltpu.roll(values, 1, 1))
 
 
 def shifted_sum(product, slabs, rows, lanes):
@@ -179,7 +180,7 @@
 
 def matrices_kernel(
     rows, planes, blocks, fine, fine_bound, mid, mid_bound, coarse, coarse_bound, coarse_diag,
-    gather_rows, spread_rows, squeeze, stretch,
+    gather_rows, spread_rows, squeeze, squeeze_line, stretch,
 ):
     def direct(offset, comp, other):
         return blocks[offset * 9 + comp * 3 + other]
@@ -247,32 +248,41 @@
     spread_rows[...] = ones_where(same_aggregate(iota(shape, 1) % (half * size), iota(shape, 0)))
     shape = (2 * LANES, 128)
     squeeze[...] = ones_where(iota(shape, 0) % LANES // 2 == iota(shape, 1))
+    shape = (2 * LINE, 256)
+    lane = iota(shape, 0) % LINE
+    squeeze_line[...] = ones_where(jnp.where(lane < 256, lane // 2, lane // 2 + 64) == iota(shape, 1))
     shape = (256, LANES)
     stretch[...] = ones_where(iota(shape, 0) % 128 == iota(shape, 1) // 2)
 
 
-def halves(planes, low):
-    first, second = planes[:10], pltpu.roll(planes[10:], 64, 2)
+def halves(planes):
+    count = planes.shape[0] // 2
+    low = iota((count, 8, 128), 2) < 64
+    first, second = planes[:count], pltpu.roll(planes[count:], 64, 2)
     return jnp.where(low, second, first), jnp.where(low, first, second)
 
 
 def pack_kernel(main, send_a, send_b):
-    high, low = halves(main[...], iota((10, 8, 128), 2) < 64)
+    high, low = halves(main[...])
+    more_high, more_low = halves(main[12:])
     even = lax.rem(lax.axis_index("gx"), 2) == 0
-    send_a[...] = jnp.where(even, high, low)
-    send_b[...] = jnp.where(even, low, high)
+    send_a[:10] = jnp.where(even, high, low)
+    send_a[10:] = jnp.where(even, more_low, more_high)
+    send_b[:10] = jnp.where(even, low, high)
+    send_b[10:] = jnp.zeros((4, 8, 128), F32)
 
 
 def widen_kernel(count, main, got_b, got_a, wide):
     index = lax.axis_index("gx")
     even = lax.rem(index, 2) == 0
-    first, second = got_a[...], got_b[...]
+    first, second, more = got_a[:10], got_b[:10], got_a[10:]
     above = jnp.where(index < count - 1, jnp.where(even, first, second), 0.0)
     below = jnp.where(index > 0, jnp.where(even, second, first), 0.0)
     low = iota((10, 8, 128), 2) < 64
-    wide[:, :, :128] = main[...]
-    wide[:10, :, 128:] = jnp.where(low, above, below)
-    wide[10:, :, 128:] = jnp.where(low, pltpu.roll(above, 64, 2), pltpu.roll(below, 64, 2))
+    wide[:20] = main[...]
+    wide[20:30] = jnp.where(low, above, below)
+    wide[30:40] = jnp.where(low, pltpu.roll(above, 64, 2), pltpu.roll(below, 64, 2))
+    wide[40:] = jnp.where(even, pltpu.roll(more, 64, 2), more)
 
 
 def inverse_diagonal(scale, mass, blocks, factor):
@@ -284,11 +294,10 @@
     return jnp.concatenate(parts, axis=1)
 
 
-def largest(ratio, lanes):
+def largest(ratio):
     width = ratio.shape[1]
     flat = jnp.max(ratio.reshape(-1, 8, width), axis=0)
-    own = jnp.where(iota((8, width), 1) < lanes, flat, -jnp.inf)
-    return functools.reduce(jnp.maximum, [own[:, at : at + 128] for at in range(0, width, 128)])
+    return functools.reduce(jnp.maximum, [flat[:, at : at + 128] for at in range(0, width, 128)])
 
 
 def paired_planes(values):
@@ -297,21 +306,25 @@
 
 
 def paired_rows(held, values):
-    for half in (0, 1):
-        held[half] = values[:, half * 128 : half * 128 + 128]
-    count = held.shape[1] // 2
+    parts, count = held.shape[0], held.shape[1] // 2
+    for part in range(parts):
+        held[part] = values[:, part * 128 : part * 128 + 128]
     return jnp.concatenate(
-        [held[half, pl.ds(0, count, stride=2)] + held[half, pl.ds(1, count, stride=2)] for half in (0, 1)], axis=1
+        [held[part, pl.ds(0, count, stride=2)] + held[part, pl.ds(1, count, stride=2)] for part in range(parts)], axis=1
     )
 
 
 def window_kernel(
     gys, ordered, blocks, *refs
 ):
-    (*blocks_in, fine_bound, mid_bound, coarse_bound, coarse_diag, gather_rows, squeeze,
-     source_w, scale_w, mass_w, inverse_w, spread_1w, weight_1w, inverse_1w, spread_2w, weight_2w, inverse_2w, bounds, held) = refs
+    (*blocks_in, fine_bound, mid_bound, coarse_bound, coarse_diag, gather_rows, squeeze_line, source_w, scale_w, mass_w, inverse_w,
+     spread_1w, weight_1w, inverse_1w, spread_2w, weight_2w, inverse_2w, bounds, scale_x, mass_x, held) = refs
     planes, rows = scale_w.shape[0] - 2 * PAD, scale_w.shape[1]
     gz, gy = lax.axis_index("gz"), lax.axis_index("gy")
+    even = lax.rem(lax.axis_index("gx"), 2) == 0
+    low = iota((4, 8, 128), 2) < 64
+    for at in (0, planes + 1):
+        scale_x[at] = jnp.zeros((rows, LINE), F32)
     for at in (0, planes + PAD):
         source_w[at : at + PAD] = jnp.zeros((PAD, 3, rows, LANES), F32)
         inverse_w[at : at + PAD] = jnp.zeros((PAD, 3, rows, LANES), F32)
@@ -327,53 +340,74 @@
                 place_y = lax.bitwise_xor(gy, number % 4 // 2)
             at_z = pl.ds(PAD + 4 * place_z, 4)
             at_y = pl.ds(pl.multiple_of(8 * place_y, 8), 8)
-            for comp in range(3):
-                source_w[at_z, comp, at_y, :] = ref[block, comp * 4 : comp * 4 + 4]
-            scale_w[at_z, at_y, :] = ref[block, 12:16]
-            mass_w[at_z, at_y, :] = ref[block, 16:20]
+            for half in (0, 1):
+                lanes = slice(half * 128, half * 128 + 128)
+                part = ref.at[block, half * 20 : half * 20 + 20]
+                for comp in range(3):
+                    source_w[at_z, comp, at_y, lanes] = part[comp * 4 : comp * 4 + 4]
+                scale_w[at_z, at_y, lanes] = part[12:16]
+                mass_w[at_z, at_y, lanes] = part[16:20]
+            here, more = ref.at[block], ref[block, 40:44]
+            turned_more = pltpu.roll(more, 64, 2)
+            for target, own, start, at_low, at_high in (
+                (scale_x, 12, 1, more, turned_more),
+                (mass_x, 16, 0, turned_more, more),
+            ):
+                at_x = pl.ds(start + 4 * place_z, 4)
+                halo = here[own + 20 : own + 24]
+                target[at_x, at_y, :128] = here[own : own + 4]
+                target[at_x, at_y, 128:256] = jnp.where(low, halo, jnp.where(even, at_high, 0.0))
+                target[at_x, at_y, 256:] = jnp.where(low, jnp.where(even, 0.0, at_low), halo)
             number += 1
 
-    scale, mass = scale_w[PAD : PAD + planes], mass_w[PAD : PAD + planes]
+    scale, mass = scale_x[1 : 1 + planes], mass_x[...]
     inverse = inverse_diagonal(scale, mass, blocks, 1.0)
-    inverse_w[PAD : PAD + planes] = inverse
+    inverse_w[PAD : PAD + planes, :, :, :128] = inverse[..., :128]
+    wide_low = iota(inverse.shape[:3] + (128,), 3) < 64
+    inverse_w[PAD : PAD + planes, :, :, 128:] = jnp.where(wide_low, inverse[..., 128:256], inverse[..., 256:])
     slab = 3 * rows
     outs = []
     at = 0
     for size in groups(planes, group_of(slab)):
-        near = scale_w[PAD - 1 + at : PAD + 1 + at + size].reshape((size + 2) * rows, LANES)
+        near = scale_x[at : at + size + 2].reshape((size + 2) * rows, LINE)
         if size < group_of(slab):
-            near = jnp.concatenate([near, jnp.zeros(((group_of(slab) - size) * rows, LANES), F32)], axis=0)
+            near = jnp.concatenate([near, jnp.zeros(((group_of(slab) - size) * rows, LINE), F32)], axis=0)
         depth = 3 * (group_of(slab) + 2) * rows
-        outs.append(shifted_sum(banded_stacked(fine_bound[: size * 3 * slab, :depth], near), size, slab, LANES))
+        outs.append(shifted_sum(banded_stacked(fine_bound[: size * 3 * slab, :depth], near), size, slab, LINE))
         at += size
-    total = jnp.concatenate(outs, axis=0).reshape(planes, 3, rows, LANES)
+    total = jnp.concatenate(outs, axis=0).reshape(planes, 3, rows, LINE)
     ratio = (scale[:, None] * total + mass[:, None]) * inverse
-    bounds[0] = largest(ratio.reshape(planes * slab, LANES), 128)
+    bounds[0] = largest(ratio.reshape(planes * slab, LINE))
 
     rows, planes = rows // 2, planes // 2
     slab = 3 * rows
     count = planes * rows
     pairs = [
-        paired_rows(held.at[at], paired_planes(values).reshape(2 * count, LANES))
+        paired_rows(held.at[at], paired_planes(values).reshape(2 * count, LINE))
         for at, values in enumerate((scale, mass))
     ]
-    middle = lanes_apply(jnp.concatenate(pairs, axis=0), squeeze[...])
-    scale_1 = (middle[:count] * 0.125).reshape(planes, rows, 128)
-    mass_1 = middle[count:].reshape(planes, rows, 128)
-    inverse_1 = inverse_diagonal(scale_1, mass_1, blocks, 2.0).reshape(planes * slab, 128)
-    spread_1 = jnp.broadcast_to(scale_1[:, None], (planes, 3, rows, 128)).reshape(planes * slab, 128)
-    weight_1 = jnp.broadcast_to(mass_1[:, None], (planes, 3, rows, 128)).reshape(planes * slab, 128)
+    middle = lanes_apply(jnp.concatenate(pairs, axis=0), squeeze_line[...])
+    scale_1 = (middle[:count] * 0.125).reshape(planes, rows, 256)
+    mass_1 = middle[count:].reshape(planes, rows, 256)
+    inverse_1 = inverse_diagonal(scale_1, mass_1, blocks, 2.0).reshape(planes * slab, 256)
+    spread_1 = jnp.broadcast_to(scale_1[:, None], (planes, 3, rows, 256)).reshape(planes * slab, 256)
+    weight_1 = jnp.broadcast_to(mass_1[:, None], (planes, 3, rows, 256)).reshape(planes * slab, 256)
     total = banded_planes(mid_bound, spread_1, planes, 1)
-    bounds[1] = largest((2.0 * spread_1 * total + weight_1) * inverse_1, 64)
-    spread_1w[...], weight_1w[...], inverse_1w[...] = spread_1, weight_1, inverse_1
+    bounds[1] = largest((2.0 * spread_1 * total + weight_1) * inverse_1)
+
+    def window(values):
+        return jnp.where(iota((values.shape[0], 128), 1) < 96, values[:, :128], values[:, 128:])
+
+    spread_1w[...], weight_1w[...], inverse_1w[...] = window(spread_1), window(weight_1), window(inverse_1)
 
     both = rows_apply(gather_rows[...], jnp.concatenate([spread_1, weight_1], axis=1))
-    spread_2 = paired_lanes(both[:, :128]) * 0.125
-    weight_2 = paired_lanes(both[:, 128:])
-    inverse_2 = jnp.where(spread_2 > 0.0, 1.0 / (4.0 * coarse_diag[...] * spread_2 * spread_2 + weight_2), 0.0)
+    spread_2 = paired_lanes(both[:, :256]) * 0.125
+    weight_2 = paired_lanes(both[:, 256:])
+    diag = jnp.concatenate([coarse_diag[...]] * 2, axis=1)
+    inverse_2 = jnp.where(spread_2 > 0.0, 1.0 / (4.0 * diag * spread_2 * spread_2 + weight_2), 0.0)
     total = banded_planes(coarse_bound, spread_2, planes // 2, 2)
-    bounds[2] = largest((4.0 * spread_2 * total + weight_2) * inverse_2, 64)
-    spread_2w[...], weight_2w[...], inverse_2w[...] = spread_2, weight_2, inverse_2
+    bounds[2] = largest((4.0 * spread_2 * total + weight_2) * inverse_2)
+    spread_2w[...], weight_2w[...], inverse_2w[...] = window(spread_2), window(weight_2), window(inverse_2)
 
 
 def inner_power(scale_w, mass_w, inverse_w, matrix, values, finish):
@@ -566,7 +600,8 @@
     size = coarse_slab(rows // 4)
     size_2 = planes // 4 * size
     (
-        fine, fine_bound, mid, mid_bound, coarse, coarse_bound, coarse_diag, gather_rows, spread_rows, squeeze, stretch,
+        fine, fine_bound, mid, mid_bound, coarse, coarse_bound, coarse_diag, gather_rows, spread_rows, squeeze,
+        squeeze_line, stretch,
     ) = call(
         functools.partial(matrices_kernel, rows, planes),
         [
@@ -580,6 +615,7 @@
             ((size_2, size_1), BF16),
             ((size_1, 2 * size_2), BF16),
             ((2 * LANES, 128), BF16),
+            ((2 * LINE, 256), BF16),
             ((256, LANES), BF16),
         ],
         specs=[SM],
@@ -588,12 +624,12 @@
         grant=grant,
     )(blocks)
 
-    half = ((10, 8, 128), F32)
+    half = ((14, 8, 128), F32)
     main = jnp.concatenate([right_side.reshape(12, 8, 128), stiff_scale, nodal_mass], axis=0)
     send_a, send_b = call(pack_kernel, [half, half], grant=8)(main)
     got_b = send(send_b, x_second)
     got_a = send(send_a, lambda x, y, z: (x ^ 1, y, z))
-    (wide,) = call(functools.partial(widen_kernel, gxs), [((20, 8, LANES), F32)], grant=8)(main, got_b, got_a)
+    (wide,) = call(functools.partial(widen_kernel, gxs), [((44, 8, 128), F32)], grant=8)(main, got_b, got_a)
     ordered = not (gys == 2 and gzs == 4)
     if ordered:
         gathered = [lax.all_gather(wide, ("gz", "gy"), tiled=False)]
@@ -613,16 +649,19 @@
         functools.partial(window_kernel, gys, ordered),
         [field, single, single, field] + [((size_1, 128), F32)] * 3 + [((size_2, 128), F32)] * 3 + [((3, 8, 128), F32)],
         specs=[SM] + [VM] * (len(gathered) + 6),
-        scratch=[pltpu.VMEM((2, 2, planes * rows // 2, 128), F32)],
+        scratch=[
+            pltpu.VMEM((planes + 2, rows, LINE), F32),
+            pltpu.VMEM((planes, rows, LINE), F32),
+            pltpu.VMEM((2, LINE // 128, planes * rows // 2, 128), F32),
+        ],
         grant=grant,
-    )(blocks, *gathered, fine_bound, mid_bound, coarse_bound, coarse_diag, gather_rows, squeeze)
-
-    step = 4
+    )(blocks, *gathered, fine_bound, mid_bound, coarse_bound, coarse_diag, gather_rows, squeeze_line)
+
+    step, other = 2, bounds
     while step < gxs:
-        bounds = jnp.maximum(bounds, send(bounds, lambda x, y, z: (x ^ step, y, z)))
+        bounds = jnp.maximum(bounds, other)
+        other = send(bounds, lambda x, y, z: (x ^ step, y, z ^ 1))
         step *= 2
-    bounds = jnp.maximum(bounds, send(bounds, lambda x, y, z: (x ^ 1, y, z ^ 1)))
-    other = send(bounds, lambda x, y, z: (x ^ 2, y, z ^ 1))
     (power_1,) = call(power_kernel, [field], flops=1000000000, size=4000000, grant=grant)(scale_w, mass_w, inverse_w, source_w, fine)
     (basis,) = call(
         restrict_kernel,

time: 33.8 us -> 32.9 us (0.973)
  starting transfers between devices: 12.4 us -> 10.7 us
  Pallas kernels: 12.4 us -> 13.6 us
    ppermute x11 -> x10, starting transfers between devices: 12.4 us -> 10.7 us  [send(): return lax.ppermute(values, AXES, swap_pairs(counts, target))]
    pallas_call x7, Pallas kernels: 12.4 us -> 13.6 us  [run(): pl.pallas_call(kernel, out_shape=outs, in_specs=specs or [VM] * len(args)...]
    ppermute x11 -> x10, waiting for transfers between devices: 6.82 us -> 6.51 us  [send(): return lax.ppermute(values, AXES, swap_pairs(counts, target))]
  transfers between devices with their start and end apart: 11 -> 10, of which waited for: 9 -> 7; matrix products, arithmetic and copies ran while one was open for 3% -> 3% of each run, Pallas kernels for 14% -> 16%
where the time goes in v6:
time: 32.9 us; the launch traced here: 32.7 us
  Pallas kernels  13.6 us (41%)
  starting transfers between devices  10.7 us (33%)
  waiting for transfers between devices  6.51 us (20%)
  local copies, waits for them, and re-layouts  0.97 us (3%)
  other arithmetic  0.84 us (3%)
    pallas_call x7, Pallas kernels, run(): pl.pallas_call(kernel, out_shape=outs, in_specs=specs or [VM] * len(args)...  13.6 us
    ppermute x10, starting transfers between devices, send(): return lax.ppermute(values, AXES, swap_pairs(counts, target))  10.7 us
    ppermute x10, waiting for transfers between devices, send(): return lax.ppermute(values, AXES, swap_pairs(counts, target))  6.51 us
    concatenate x1, other arithmetic, on_device(): jnp.concatenate([right_side.reshape(12, 8, 128), stiff_scale, nodal_mass]...  0.84 us
    unnamed x1, local copies, waits for them, and re-layouts  0.8 us
  transfers between devices with their start and end apart: 10, of which 7 were waited for; matrix products, arithmetic and copies ran while one was open for 3% of the time, Pallas kernels for 16%

profile of v6, /device:TPU:0, one launch (start us, length us, event | category | flops | bytes accessed | tf_op | source)
XLA Modules:
  0.0 32.7 jit_solution(2026451591533475114)
XLA Ops:
  0.0 0.8 %pad_maximum_fusion.main = f32[20,8,128]{2,1,0:T(8,128)S(1)} fusion(f32[4,8,128]{2,1,0:T(8,128)} %param.6, f32[4,8,128]{2,1,0:T(8,128)} %param.5, f32[12,8,128]{2,1,0:T(8,128)} %bitcast.17), kind=kLoop, calls=%fused_computation | loop fusion | flops 40960 | bytes 163840 | tf_op jit(solution)/shard_map/concatenate | solution.py:628
  0.8 0.1 shard_map.46
  0.9 0.5 %collective-permute-start = (f32[14,8,128]{2,1,0:T(8,128)S(1)}, f32[14,8,128]{2,1,0:T(8,128)S(1)}, u32[]{:S(2)}, u32[]{:S(2)}) collective-permute-start(f32[14,8,128]{2,1,0:T(8,128)S(1)} %get-tuple-element.32), channel_id=1, source_target_pairs={{0,1},{1,0},{2,3},{3,2},{4,5},{5,4},{6,7},{7,6},{8,16},{9,17},{10,... | collective-permute-start | bytes 172040 | tf_op jit(solution)/shard_map/ppermute | solution.py:590
  1.4 4.1 %collective-permute-start.1 = (f32[14,8,128]{2,1,0:T(8,128)S(1)}, f32[14,8,128]{2,1,0:T(8,128)S(1)}, u32[]{:S(2)}, u32[]{:S(2)}) collective-permute-start(f32[14,8,128]{2,1,0:T(8,128)S(1)} %get-tuple-element.33), channel_id=1, source_target_pairs={{0,8},{1,9},{2,10},{3,11},{4,12},{5,13},{6,14},{7,15},{8,0},{9,1},... | collective-permute-start | bytes 172040 | tf_op jit(solution)/shard_map/ppermute | solution.py:590
  5.6 0.8 %copy.5 = f32[27,3,3]{2,1,0:T(4,128)S(1)} copy(f32[27,3,3]{0,2,1:T(4,128)} %param.7) | data formatting | bytes 1944 | tf_op args[3]
  6.4 0.2 reshape.6.blocks
  6.6 0.0 collective-permute-done.got_b
  6.6 1.2 %collective-permute-done.1.got_a = f32[14,8,128]{2,1,0:T(8,128)S(1)} collective-permute-done((f32[14,8,128]{2,1,0:T(8,128)S(1)}, f32[14,8,128]{2,1,0:T(8,128)S(1)}, u32[]{:S(2)}, u32[]{:S(2)}) %collective-permute-start.1) | collective-permute-done | bytes 57376 | tf_op jit(solution)/shard_map/ppermute | solution.py:590
  7.7 0.1 shard_map.47
  7.9 2.5 %collective-permute-start.4 = (f32[44,8,128]{2,1,0:T(8,128)S(1)}, f32[44,8,128]{2,1,0:T(8,128)S(1)}, u32[]{:S(2)}, u32[]{:S(2)}) collective-permute-start(f32[44,8,128]{2,1,0:T(8,128)S(1)} %shard_map.47), channel_id=1, source_target_pairs={{0,6},{1,7},{2,4},{3,5},{4,2},{5,3},{6,0},{7,1},{8,14},{9,15},{10,... | collective-permute-start | bytes 540680 | tf_op jit(solution)/shard_map/ppermute | solution.py:590
  10.4 0.5 %collective-permute-start.3 = (f32[44,8,128]{2,1,0:T(8,128)S(1)}, f32[44,8,128]{2,1,0:T(8,128)S(1)}, u32[]{:S(2)}, u32[]{:S(2)}) collective-permute-start(f32[44,8,128]{2,1,0:T(8,128)S(1)} %shard_map.47), channel_id=1, source_target_pairs={{0,4},{1,5},{2,6},{3,7},{4,0},{5,1},{6,2},{7,3},{8,12},{9,13},{10,... | collective-permute-start | bytes 540680 | tf_op jit(solution)/shard_map/ppermute | solution.py:590
  10.9 0.5 %collective-permute-start.2 = (f32[44,8,128]{2,1,0:T(8,128)S(1)}, f32[44,8,128]{2,1,0:T(8,128)S(1)}, u32[]{:S(2)}, u32[]{:S(2)}) collective-permute-start(f32[44,8,128]{2,1,0:T(8,128)S(1)} %shard_map.47), channel_id=1, source_target_pairs={{0,2},{1,3},{2,0},{3,1},{4,6},{5,7},{6,4},{7,5},{8,10},{9,11},{10,... | collective-permute-start | bytes 540680 | tf_op jit(solution)/shard_map/ppermute | solution.py:590
  11.4 2.4 %shard_map.48 = (bf16[144,512]{1,0:T(8,128)(2,1)S(1)}, bf16[432,256]{1,0:T(8,128)(2,1)S(1)}, bf16[72,256]{1,0:T(8,128)(2,1)S(1)}, bf16[72,256]{1,0:T(8,128)(2,1)...) custom-call(f32[243]{0:T(256)S(1)} %reshape.6.blocks), custom_call_target="tpu_custom_call" | custom-call | flops 5000000000 | bytes 8000000 | tf_op jit(solution)/shard_map/pallas_call | solution.py:27
  13.8 0.1 collective-permute-start.5
  13.9 2.2 %collective-permute-done.4 = f32[44,8,128]{2,1,0:T(8,128)S(1)} collective-permute-done((f32[44,8,128]{2,1,0:T(8,128)S(1)}, f32[44,8,128]{2,1,0:T(8,128)S(1)}, u32[]{:S(2)}, u32[]{:S(2)}) %collective-permute-start.4) | collective-permute-done | bytes 180256 | tf_op jit(solution)/shard_map/ppermute | solution.py:590
  16.1 1.7 %collective-permute-done.3 = f32[44,8,128]{2,1,0:T(8,128)S(1)} collective-permute-done((f32[44,8,128]{2,1,0:T(8,128)S(1)}, f32[44,8,128]{2,1,0:T(8,128)S(1)}, u32[]{:S(2)}, u32[]{:S(2)}) %collective-permute-start.3) | collective-permute-done | bytes 180256 | tf_op jit(solution)/shard_map/ppermute | solution.py:590
  17.8 0.0 collective-permute-start.7
  17.8 0.1 collective-permute-done.2
  17.9 0.4 %collective-permute-start.6 = (f32[44,8,128]{2,1,0:T(8,128)S(1)}, f32[44,8,128]{2,1,0:T(8,128)S(1)}, u32[]{:S(2)}, u32[]{:S(2)}) collective-permute-start(f32[44,8,128]{2,1,0:T(8,128)S(1)} %collective-permute-done.2), channel_id=1, source_target_pairs={{0,1},{1,0},{2,3},{3,2},{4,5},{5,4},{6,7},{7,6},{8,9},{9,8},{10,11... | collective-permute-start | bytes 540680 | tf_op jit(solution)/shard_map/ppermute | solution.py:590
  18.3 0.1 collective-permute-start.8
  18.4 0.0 collective-permute-done.5
  18.4 0.8 %collective-permute-done.7 = f32[44,8,128]{2,1,0:T(8,128)S(1)} collective-permute-done((f32[44,8,128]{2,1,0:T(8,128)S(1)}, f32[44,8,128]{2,1,0:T(8,128)S(1)}, u32[]{:S(2)}, u32[]{:S(2)}) %collective-permute-start.7) | collective-permute-done | bytes 180256 | tf_op jit(solution)/shard_map/ppermute | solution.py:590
  19.2 0.3 collective-permute-done.6
  19.5 0.3 collective-permute-done.8
  19.8 2.4 %shard_map.49 = (f32[22,3,16,256]{3,2,1,0:T(8,128)S(1)}, f32[22,16,256]{2,1,0:T(8,128)S(1)}, f32[22,16,256]{2,1,0:T(8,128)S(1)}, f32[22,3,16,256]{3,2,1,0:T(8,12...) custom-call(f32[243]{0:T(256)S(1)} %reshape.6.blocks, ...), custom_call_target="tpu_custom_call" | custom-call | flops 1000000 | bytes 100000 | tf_op jit(solution)/shard_map/pallas_call | solution.py:27
  22.1 1.9 %collective-permute-start.9 = (f32[3,8,128]{2,1,0:T(8,128)S(1)}, f32[3,8,128]{2,1,0:T(8,128)S(1)}, u32[]{:S(2)}, u32[]{:S(2)}) collective-permute-start(f32[3,8,128]{2,1,0:T(8,128)S(1)} %get-tuple-element.42.bounds_a), channel_id=1, source_target_pairs={{0,17},{1,16},{2,19},{3,18},{4,21},{5,20},{6,23},{7,22},{8,25},{9,... | collective-permute-start | bytes 36872 | tf_op jit(solution)/shard_map/ppermute | solution.py:590
  24.0 0.9 %shard_map.50.power_1 = f32[22,3,16,256]{3,2,1,0:T(8,128)S(1)} custom-call(f32[22,16,256]{2,1,0:T(8,128)S(1)} %get-tuple-element.44.scale_w, f32[22,16,256]{2,1,0:T(8,128)S(1)} %get-tuple-element.45.mass_w, f32[22,3,16,256]{3,2,1,0:T(8,128)S(1)} %get-tuple-element.46.inverse_w, f32[22,3,16,256]{3,2,1,0:T(8,128)S(1)} %get-tuple-element.43.source_w, ...), custom_call_target="tpu_custom_call" | custom-call | flops 1000000000 | bytes 4000000 | tf_op jit(solution)/shard_map/pallas_call | solution.py:27
  25.0 2.0 %shard_map.51.basis = f32[4,192,128]{2,1,0:T(8,128)S(1)} custom-call(f32[22,16,256]{2,1,0:T(8,128)S(1)} %get-tuple-element.44.scale_w, f32[22,16,256]{2,1,0:T(8,128)S(1)} %get-tuple-element.45.mass_w, f32[22,3,16,256]{3,2,1,0:T(8,128)S(1)} %get-tuple-element.46.inverse_w, f32[22,3,16,256]{3,2,1,0:T(8,128)S(1)} %get-tuple-element.43.source_w, ...), custom_call_target="tpu_custom_call" | custom-call | flops 2000000000 | bytes 8000000 | tf_op jit(solution)/shard_map/pallas_call | solution.py:27
  27.0 0.0 collective-permute-done.9.bounds_b
  27.0 5.7 %shard_map.52 = f32[3,4,8,128]{3,2,1,0:T(8,128)} custom-call(f32[3,8,128]{2,1,0:T(8,128)S(1)} %get-tuple-element.42.bounds_a, f32[3,8,128]{2,1,0:T(8,128)S(1)} %collective-permute-done.9.bounds_b, f32[22,3,16,256]{3,2,1,0:T(8,128)S(1)} %get-tuple-element.43.source_w, f32[22,16,256]{2,1,0:T(8,128)S(1)} %get-tuple-element.44.scale_w, ...), custom_call_target="tpu_custom_call" | custom-call | flops 1000000 | bytes 100000 | tf_op jit(solution)/shard_map/pallas_call | solution.py:27
Async XLA Ops:
  0.9 5.6 %collective-permute-start = (f32[14,8,128]{2,1,0:T(8,128)S(1)}, f32[14,8,128]{2,1,0:T(8,128)S(1)}, u32[]{:S(2)}, u32[]{:S(2)}) collective-permute-start(f32[14,8,128]{2,1,0:T(8,128)S(1)} %get-tuple-element.32), channel_id=1, source_target_pairs={{0,1},{1,0},{2,3},{3,2},{4,5},{5,4},{6,7},{7,6},{8,16},{9,17},{10,... | collective-permute-start | bytes 172040 | tf_op jit(solution)/shard_map/ppermute | solution.py:590
  1.4 6.3 %collective-permute-start.1 = (f32[14,8,128]{2,1,0:T(8,128)S(1)}, f32[14,8,128]{2,1,0:T(8,128)S(1)}, u32[]{:S(2)}, u32[]{:S(2)}) collective-permute-start(f32[14,8,128]{2,1,0:T(8,128)S(1)} %get-tuple-element.33), channel_id=1, source_target_pairs={{0,8},{1,9},{2,10},{3,11},{4,12},{5,13},{6,14},{7,15},{8,0},{9,1},... | collective-permute-start | bytes 172040 | tf_op jit(solution)/shard_map/ppermute | solution.py:590
  7.9 8.2 %collective-permute-start.4 = (f32[44,8,128]{2,1,0:T(8,128)S(1)}, f32[44,8,128]{2,1,0:T(8,128)S(1)}, u32[]{:S(2)}, u32[]{:S(2)}) collective-permute-start(f32[44,8,128]{2,1,0:T(8,128)S(1)} %shard_map.47), channel_id=1, source_target_pairs={{0,6},{1,7},{2,4},{3,5},{4,2},{5,3},{6,0},{7,1},{8,14},{9,15},{10,... | collective-permute-start | bytes 540680 | tf_op jit(solution)/shard_map/ppermute | solution.py:590
  10.4 7.5 %collective-permute-start.3 = (f32[44,8,128]{2,1,0:T(8,128)S(1)}, f32[44,8,128]{2,1,0:T(8,128)S(1)}, u32[]{:S(2)}, u32[]{:S(2)}) collective-permute-start(f32[44,8,128]{2,1,0:T(8,128)S(1)} %shard_map.47), channel_id=1, source_target_pairs={{0,4},{1,5},{2,6},{3,7},{4,0},{5,1},{6,2},{7,3},{8,12},{9,13},{10,... | collective-permute-start | bytes 540680 | tf_op jit(solution)/shard_map/ppermute | solution.py:590
  10.9 7.0 %collective-permute-start.2 = (f32[44,8,128]{2,1,0:T(8,128)S(1)}, f32[44,8,128]{2,1,0:T(8,128)S(1)}, u32[]{:S(2)}, u32[]{:S(2)}) collective-permute-start(f32[44,8,128]{2,1,0:T(8,128)S(1)} %shard_map.47), channel_id=1, source_target_pairs={{0,2},{1,3},{2,0},{3,1},{4,6},{5,7},{6,4},{7,5},{8,10},{9,11},{10,... | collective-permute-start | bytes 540680 | tf_op jit(solution)/shard_map/ppermute | solution.py:590
  13.8 4.6 %collective-permute-start.5 = (f32[44,8,128]{2,1,0:T(8,128)S(1)}, f32[44,8,128]{2,1,0:T(8,128)S(1)}, u32[]{:S(2)}, u32[]{:S(2)}) collective-permute-start(f32[44,8,128]{2,1,0:T(8,128)S(1)} %shard_map.47), channel_id=1, source_target_pairs={{0,1},{1,0},{2,3},{3,2},{4,5},{5,4},{6,7},{7,6},{8,9},{9,8},{10,11... | collective-permute-start | bytes 540680 | tf_op jit(solution)/shard_map/ppermute | solution.py:590
  17.8 1.4 %collective-permute-start.7 = (f32[44,8,128]{2,1,0:T(8,128)S(1)}, f32[44,8,128]{2,1,0:T(8,128)S(1)}, u32[]{:S(2)}, u32[]{:S(2)}) collective-permute-start(f32[44,8,128]{2,1,0:T(8,128)S(1)} %collective-permute-done.3), channel_id=1, source_target_pairs={{0,1},{1,0},{2,3},{3,2},{4,5},{5,4},{6,7},{7,6},{8,9},{9,8},{10,11... | collective-permute-start | bytes 540680 | tf_op jit(solution)/shard_map/ppermute | solution.py:590
  17.9 1.6 %collective-permute-start.6 = (f32[44,8,128]{2,1,0:T(8,128)S(1)}, f32[44,8,128]{2,1,0:T(8,128)S(1)}, u32[]{:S(2)}, u32[]{:S(2)}) collective-permute-start(f32[44,8,128]{2,1,0:T(8,128)S(1)} %collective-permute-done.2), channel_id=1, source_target_pairs={{0,1},{1,0},{2,3},{3,2},{4,5},{5,4},{6,7},{7,6},{8,9},{9,8},{10,11... | collective-permute-start | bytes 540680 | tf_op jit(solution)/shard_map/ppermute | solution.py:590
  18.3 1.4 %collective-permute-start.8 = (f32[44,8,128]{2,1,0:T(8,128)S(1)}, f32[44,8,128]{2,1,0:T(8,128)S(1)}, u32[]{:S(2)}, u32[]{:S(2)}) collective-permute-start(f32[44,8,128]{2,1,0:T(8,128)S(1)} %collective-permute-done.4), channel_id=1, source_target_pairs={{0,1},{1,0},{2,3},{3,2},{4,5},{5,4},{6,7},{7,6},{8,9},{9,8},{10,11... | collective-permute-start | bytes 540680 | tf_op jit(solution)/shard_map/ppermute | solution.py:590
  22.1 4.9 %collective-permute-start.9 = (f32[3,8,128]{2,1,0:T(8,128)S(1)}, f32[3,8,128]{2,1,0:T(8,128)S(1)}, u32[]{:S(2)}, u32[]{:S(2)}) collective-permute-start(f32[3,8,128]{2,1,0:T(8,128)S(1)} %get-tuple-element.42.bounds_a), channel_id=1, source_target_pairs={{0,17},{1,16},{2,19},{3,18},{4,21},{5,20},{6,23},{7,22},{8,25},{9,... | collective-permute-start | bytes 36872 | tf_op jit(solution)/shard_map/ppermute | solution.py:590

commit v7 on v6

--- a/solution.py
+++ b/solution.py
@@ -105,12 +105,11 @@
 
 def groups(planes, most):
     sizes = []
-    while planes:
-        size = min(most, planes)
-        if most > 2 and planes == most + 1:
-            size = 2
-        sizes.append(size)
-        planes -= size
+    half = planes // 2
+    while half:
+        size = min(most, half)
+        sizes += [size, size]
+        half -= size
     return sizes
 
 
@@ -178,8 +177,16 @@
     return -(-3 * few // 16) * 16
 
 
+def own_rows(values, count):
+    index = lax.axis_index("gy")
+    found = values[..., :8, :]
+    for block in range(1, count):
+        found = jnp.where(index == block, values[..., block * 8 : block * 8 + 8, :], found)
+    return found
+
+
 def matrices_kernel(
-    rows, planes, blocks, fine, fine_bound, mid, mid_bound, coarse, coarse_bound, coarse_diag,
+    rows, planes, blocks, fine, fine_own, fine_bound, mid, mid_bound, coarse, coarse_bound, coarse_diag,
     gather_rows, spread_rows, squeeze, squeeze_line, stretch,
 ):
     def direct(offset, comp, other):
@@ -193,10 +200,12 @@
     group = group_of(slab)
     width = up128(3 * slab)
     found = panels(direct, 3, rows, width)
-    value = jnp.concatenate([found[step_x, comp] for step_x in range(3) for comp in range(3)], axis=0)
-    if fine.shape[1] > width:
-        value = jnp.concatenate([value, jnp.zeros((3 * slab, fine.shape[1] - width), F32)], axis=1)
-    fine[...] = stack3(value, 3 * slab)
+    every = [found[step_x, comp] for step_x in range(3) for comp in range(3)]
+    for target, parts in ((fine, every), (fine_own, [own_rows(part, rows // 8) for part in every])):
+        value = jnp.concatenate(parts, axis=0)
+        if target.shape[1] > width:
+            value = jnp.concatenate([value, jnp.zeros((value.shape[0], target.shape[1] - width), F32)], axis=1)
+        target[...] = stack3(value, 3 * slab)
     bound = panels(absolute, 1, rows, fine_bound.shape[1])
     for plane in range(group):
         for step_x in range(3):
@@ -294,10 +303,39 @@
     return jnp.concatenate(parts, axis=1)
 
 
-def largest(ratio):
+def line_lanes(shape, count, above, more_above, more_below, below, seam):
+    index = lax.axis_index("gx")
+    even = lax.rem(index, 2) == 0
+    odd = jnp.logical_not(even)
+    lane = iota(shape, 1)
+    end_above = more_above + (more_above - above) - jnp.where(index + 1 == count - 1, 0, seam)
+    start_below = more_below + jnp.where(index - 1 == 0, 0, seam)
+
+    def within(first, last, condition):
+        return jnp.logical_and(jnp.logical_and(lane >= first, lane < last), condition)
+
+    found = lane < above
+    for part in (
+        within(above, more_above - jnp.where(even, 0, seam), index < count - 1),
+        within(more_above, end_above, even),
+        within(start_below, below, odd),
+        within(below + jnp.where(even, seam, 0), shape[1], index > 0),
+    ):
+        found = jnp.logical_or(found, part)
+    return found
+
+
+def largest(ratio, *lanes):
     width = ratio.shape[1]
     flat = jnp.max(ratio.reshape(-1, 8, width), axis=0)
+    flat = jnp.where(line_lanes(flat.shape, *lanes), flat, -jnp.inf)
     return functools.reduce(jnp.maximum, [flat[:, at : at + 128] for at in range(0, width, 128)])
+
+
+def clear_pads(ref):
+    planes = ref.shape[0] - 2 * PAD
+    for at in (0, planes + PAD):
+        ref[at : at + PAD] = jnp.zeros((PAD,) + ref.shape[1:], F32)
 
 
 def paired_planes(values):
@@ -315,7 +353,7 @@
 
 
 def window_kernel(
-    gys, ordered, blocks, *refs
+    gxs, gys, ordered, blocks, *refs
 ):
     (*blocks_in, fine_bound, mid_bound, coarse_bound, coarse_diag, gather_rows, squeeze_line, source_w, scale_w, mass_w, inverse_w,
      spread_1w, weight_1w, inverse_1w, spread_2w, weight_2w, inverse_2w, bounds, scale_x, mass_x, held) = refs
@@ -325,11 +363,8 @@
     low = iota((4, 8, 128), 2) < 64
     for at in (0, planes + 1):
         scale_x[at] = jnp.zeros((rows, LINE), F32)
-    for at in (0, planes + PAD):
-        source_w[at : at + PAD] = jnp.zeros((PAD, 3, rows, LANES), F32)
-        inverse_w[at : at + PAD] = jnp.zeros((PAD, 3, rows, LANES), F32)
-        scale_w[at : at + PAD] = jnp.zeros((PAD, rows, LANES), F32)
-        mass_w[at : at + PAD] = jnp.zeros((PAD, rows, LANES), F32)
+    for ref in (source_w, inverse_w, scale_w, mass_w):
+        clear_pads(ref)
     number = 0
     for ref in blocks_in:
         for block in range(ref.shape[0]):
@@ -368,16 +403,20 @@
     slab = 3 * rows
     outs = []
     at = 0
-    for size in groups(planes, group_of(slab)):
-        near = scale_x[at : at + size + 2].reshape((size + 2) * rows, LINE)
-        if size < group_of(slab):
-            near = jnp.concatenate([near, jnp.zeros(((group_of(slab) - size) * rows, LINE), F32)], axis=0)
+    for size in groups(planes, group_of(slab))[::2]:
+        beside = []
+        for _ in range(2):
+            near = scale_x[at : at + size + 2].reshape((size + 2) * rows, LINE)
+            if size < group_of(slab):
+                near = jnp.concatenate([near, jnp.zeros(((group_of(slab) - size) * rows, LINE), F32)], axis=0)
+            beside.append(near)
+            at += size
         depth = 3 * (group_of(slab) + 2) * rows
-        outs.append(shifted_sum(banded_stacked(fine_bound[: size * 3 * slab, :depth], near), size, slab, LINE))
-        at += size
+        product = banded_stacked(fine_bound[: size * 3 * slab, :depth], jnp.concatenate(beside, axis=1))
+        outs += [shifted_sum(product[:, half * LINE : half * LINE + LINE], size, slab, LINE) for half in (0, 1)]
     total = jnp.concatenate(outs, axis=0).reshape(planes, 3, rows, LINE)
     ratio = (scale[:, None] * total + mass[:, None]) * inverse
-    bounds[0] = largest(ratio.reshape(planes * slab, LINE))
+    bounds[0] = largest(ratio.reshape(planes * slab, LINE), gxs, 128, 192, 256, 320, 1)
 
     rows, planes = rows // 2, planes // 2
     slab = 3 * rows
@@ -393,7 +432,7 @@
     spread_1 = jnp.broadcast_to(scale_1[:, None], (planes, 3, rows, 256)).reshape(planes * slab, 256)
     weight_1 = jnp.broadcast_to(mass_1[:, None], (planes, 3, rows, 256)).reshape(planes * slab, 256)
     total = banded_planes(mid_bound, spread_1, planes, 1)
-    bounds[1] = largest((2.0 * spread_1 * total + weight_1) * inverse_1)
+    bounds[1] = largest((2.0 * spread_1 * total + weight_1) * inverse_1, gxs, 64, 96, 192, 224, 1)
 
     def window(values):
         return jnp.where(iota((values.shape[0], 128), 1) < 96, values[:, :128], values[:, 128:])
@@ -406,7 +445,7 @@
     diag = jnp.concatenate([coarse_diag[...]] * 2, axis=1)
     inverse_2 = jnp.where(spread_2 > 0.0, 1.0 / (4.0 * diag * spread_2 * spread_2 + weight_2), 0.0)
     total = banded_planes(coarse_bound, spread_2, planes // 2, 2)
-    bounds[2] = largest((4.0 * spread_2 * total + weight_2) * inverse_2)
+    bounds[2] = largest((4.0 * spread_2 * total + weight_2) * inverse_2, gxs, 64, 96, 192, 224, 2)
     spread_2w[...], weight_2w[...], inverse_2w[...] = window(spread_2), window(weight_2), window(inverse_2)
 
 
@@ -424,28 +463,25 @@
     )
 
 
-def power_kernel(scale_w, mass_w, inverse_w, source_w, fine, power):
-    planes, shape = scale_w.shape[0] - 2 * PAD, power.shape[1:]
-    power[:PAD] = jnp.zeros((PAD,) + shape, F32)
-    power[PAD + planes :] = jnp.zeros((PAD,) + shape, F32)
-
-    def finish(at, values):
-        power[PAD + at] = values
-
-    inner_power(scale_w, mass_w, inverse_w, fine, source_w, finish)
-
-
-def restrict_kernel(scale_w, mass_w, inverse_w, source_w, power_1, fine, squeeze, basis, power_2, held):
+def powers_kernel(scale_w, mass_w, inverse_w, source_w, fine, squeeze, power_1, basis, power_2, held):
     planes, rows = scale_w.shape[0] - 2 * PAD, scale_w.shape[1]
-    power_kernel(scale_w, mass_w, inverse_w, power_1, fine, power_2)
     third = []
+    for source, target in ((source_w, power_1), (power_1, power_2)):
+        clear_pads(target)
+
+        def finish(at, values, target=target):
+            target[PAD + at] = values
+
+        inner_power(scale_w, mass_w, inverse_w, fine, source, finish)
     inner_power(scale_w, mass_w, inverse_w, fine, power_2, lambda at, values: third.append(values))
-    third = jnp.stack(third, axis=0)
     inner = slice(PAD, PAD + planes)
     size = planes // 2 * 3 * rows
-    for at, values in enumerate((source_w[inner], power_1[inner], power_2[inner], third)):
-        pairs = paired_rows(held.at[at], paired_planes(values).reshape(size, LANES))
-        basis[at] = lanes_apply(pairs, squeeze[...])
+    pairs = []
+    for at, values in enumerate((source_w[inner], power_1[inner], power_2[inner], jnp.stack(third, axis=0))):
+        pairs.append(paired_rows(held.at[at], paired_planes(values).reshape(size, LANES)))
+    restricted = lanes_apply(jnp.concatenate(pairs, axis=0), squeeze[...])
+    for at in range(4):
+        basis[at] = restricted[at * size // 2 : (at + 1) * size // 2]
 
 
 def chebyshev_constants(ratio, degree):
@@ -483,12 +519,12 @@
 def final_kernel(
     bounds_a, bounds_b, source_w, scale_w, mass_w, inverse_w, power_1, basis,
     spread_1w, weight_1w, inverse_1w, spread_2w, weight_2w, inverse_2w,
-    fine, mid, coarse, gather_rows, spread_rows, stretch, result, lifted_w, doubled_w, answer_w,
+    fine, fine_own, mid, coarse, gather_rows, spread_rows, stretch, result, lifted_w, doubled_w,
 ):
     rows = scale_w.shape[1] // 2
     planes = (scale_w.shape[0] - 2 * PAD) // 2
     slab = 3 * rows
-    gz, gy = lax.axis_index("gz"), lax.axis_index("gy")
+    gz = lax.axis_index("gz")
     worst = jnp.maximum(bounds_a[...], bounds_b[...])
     inverse_bounds = [1.0 / jnp.full((8, 128), jnp.max(worst[level]), F32) for level in range(3)]
     over_0 = inverse_bounds[0]
@@ -562,11 +598,20 @@
     iterate = inverse * (before - omega * image) + error[1:9]
     residue = source[1:7] - apply(iterate, 2)
     direction = first * (inverse[1:7] * residue)
-    last = residue[1:5] - apply(direction, 1)
-    answer = iterate[2:6] + (1.0 + hold) * direction[1:5] + push * (inverse[2:6] * last)
-    answer_w[...] = answer[:, :, :, :128]
-    for comp in range(3):
-        result[comp] = answer_w[:, comp, pl.ds(pl.multiple_of(8 * gy, 8), 8), :]
+
+    def own(values):
+        return own_rows(values, 2 * rows // 8)
+
+    for plane in range(4):
+        near = [split((scale[plane + 2 + i][None] * direction[plane + i]).reshape(6 * rows, LANES)) for i in range(3)]
+        stacked = jnp.concatenate([part[0] for part in near] * 2 + [part[1] for part in near], axis=0)
+        product = dot(fine_own[:, : 18 * slab], stacked)
+        total = shifted_sum(product, 1, 24, LANES).reshape(3, 8, LANES)[..., :128]
+        here = own(direction[plane + 1])[..., :128]
+        image = own(scale[plane + 3])[None, :, :128] * total + own(mass[plane + 2])[None, :, :128] * here
+        last = own(residue[plane + 1])[..., :128] - image
+        answer = own(iterate[plane + 2])[..., :128] + (1.0 + hold) * here
+        result[:, plane] = answer + push * (own(inverse[plane + 2])[..., :128] * last)
 
 
 def swap_pairs(counts, target):
@@ -600,12 +645,13 @@
     size = coarse_slab(rows // 4)
     size_2 = planes // 4 * size
     (
-        fine, fine_bound, mid, mid_bound, coarse, coarse_bound, coarse_diag, gather_rows, spread_rows, squeeze,
+        fine, fine_own, fine_bound, mid, mid_bound, coarse, coarse_bound, coarse_diag, gather_rows, spread_rows, squeeze,
         squeeze_line, stretch,
     ) = call(
         functools.partial(matrices_kernel, rows, planes),
         [
             ((3 * slab, up128(9 * slab)), BF16),
+            ((72, up128(9 * slab)), BF16),
             ((group * 3 * slab, up128(3 * (group + 2) * rows)), BF16),
             ((3 * slab // 2, up128(9 * slab // 2)), BF16),
             ((3 * slab // 2, up128(9 * slab // 2)), BF16),
@@ -646,7 +692,7 @@
     field = ((planes + 2 * PAD, 3, rows, LANES), F32)
     single = ((planes + 2 * PAD, rows, LANES), F32)
     source_w, scale_w, mass_w, inverse_w, *levels, bounds = call(
-        functools.partial(window_kernel, gys, ordered),
+        functools.partial(window_kernel, gxs, gys, ordered),
         [field, single, single, field] + [((size_1, 128), F32)] * 3 + [((size_2, 128), F32)] * 3 + [((3, 8, 128), F32)],
         specs=[SM] + [VM] * (len(gathered) + 6),
         scratch=[
@@ -662,27 +708,25 @@
         bounds = jnp.maximum(bounds, other)
         other = send(bounds, lambda x, y, z: (x ^ step, y, z ^ 1))
         step *= 2
-    (power_1,) = call(power_kernel, [field], flops=1000000000, size=4000000, grant=grant)(scale_w, mass_w, inverse_w, source_w, fine)
-    (basis,) = call(
-        restrict_kernel,
-        [((4, size_1, 128), F32)],
+    power_1, basis = call(
+        powers_kernel,
+        [field, ((4, size_1, 128), F32)],
         scratch=[pltpu.VMEM(*field), pltpu.VMEM((4, 2, 2 * size_1, 128), F32)],
-        flops=2000000000,
-        size=8000000,
+        flops=3000000000,
+        size=12000000,
         grant=grant,
-    )(scale_w, mass_w, inverse_w, source_w, power_1, fine, squeeze)
+    )(scale_w, mass_w, inverse_w, source_w, fine, squeeze)
     (result,) = call(
         final_kernel,
         [(right_side.shape, F32)],
         scratch=[
             pltpu.VMEM((planes // 2 + 4, slab // 2, 128), F32),
             pltpu.VMEM((2, 6 * slab, 128), F32),
-            pltpu.VMEM((4, 3, rows, 128), F32),
         ],
         grant=grant,
     )(
         bounds, other, source_w, scale_w, mass_w, inverse_w, power_1, basis, *levels,
-        fine, mid, coarse, gather_rows, spread_rows, stretch,
+        fine, fine_own, mid, coarse, gather_rows, spread_rows, stretch,
     )
     return result
 

time: 32.9 us -> 32.6 us (level)
  Pallas kernels: 13.6 us -> 13.2 us
    pallas_call x7 -> x6, Pallas kernels: 13.6 us -> 13.2 us  [run(): pl.pallas_call(kernel, out_shape=outs, in_specs=specs or [VM] * len(args)...]
where the time goes in v7:
time: 32.6 us; the launch traced here: 32.3 us
  Pallas kernels  13.2 us (40%)
  starting transfers between devices  10.7 us (33%)
  waiting for transfers between devices  6.53 us (20%)
  local copies, waits for them, and re-layouts  0.97 us (3%)
  other arithmetic  0.84 us (3%)
    pallas_call x6, Pallas kernels, run(): pl.pallas_call(kernel, out_shape=outs, in_specs=specs or [VM] * len(args)...  13.2 us
    ppermute x10, starting transfers between devices, send(): return lax.ppermute(values, AXES, swap_pairs(counts, target))  10.7 us
    ppermute x10, waiting for transfers between devices, send(): return lax.ppermute(values, AXES, swap_pairs(counts, target))  6.53 us
    concatenate x1, other arithmetic, on_device(): jnp.concatenate([right_side.reshape(12, 8, 128), stiff_scale, nodal_mass]...  0.84 us
    unnamed x1, local copies, waits for them, and re-layouts  0.8 us
  transfers between devices with their start and end apart: 10, of which 7 were waited for; matrix products, arithmetic and copies ran while one was open for 3% of the time, Pallas kernels for 16%

profile of v7, /device:TPU:0, one launch (start us, length us, event | category | flops | bytes accessed | tf_op | source)
XLA Modules:
  0.0 32.3 jit_solution(9470156031142707923)
XLA Ops:
  0.0 0.8 %pad_maximum_fusion.main = f32[20,8,128]{2,1,0:T(8,128)S(1)} fusion(f32[4,8,128]{2,1,0:T(8,128)} %param.6, f32[4,8,128]{2,1,0:T(8,128)} %param.5, f32[12,8,128]{2,1,0:T(8,128)} %bitcast.17), kind=kLoop, calls=%fused_computation | loop fusion | flops 40960 | bytes 163840 | tf_op jit(solution)/shard_map/concatenate | solution.py:674
  0.8 0.1 shard_map.46
  0.9 0.5 %collective-permute-start = (f32[14,8,128]{2,1,0:T(8,128)S(1)}, f32[14,8,128]{2,1,0:T(8,128)S(1)}, u32[]{:S(2)}, u32[]{:S(2)}) collective-permute-start(f32[14,8,128]{2,1,0:T(8,128)S(1)} %get-tuple-element.35), channel_id=1, source_target_pairs={{0,1},{1,0},{2,3},{3,2},{4,5},{5,4},{6,7},{7,6},{8,16},{9,17},{10,... | collective-permute-start | bytes 172040 | tf_op jit(solution)/shard_map/ppermute | solution.py:635
  1.4 4.1 %collective-permute-start.1 = (f32[14,8,128]{2,1,0:T(8,128)S(1)}, f32[14,8,128]{2,1,0:T(8,128)S(1)}, u32[]{:S(2)}, u32[]{:S(2)}) collective-permute-start(f32[14,8,128]{2,1,0:T(8,128)S(1)} %get-tuple-element.36), channel_id=1, source_target_pairs={{0,8},{1,9},{2,10},{3,11},{4,12},{5,13},{6,14},{7,15},{8,0},{9,1},... | collective-permute-start | bytes 172040 | tf_op jit(solution)/shard_map/ppermute | solution.py:635
  5.6 0.8 %copy.5 = f32[27,3,3]{2,1,0:T(4,128)S(1)} copy(f32[27,3,3]{0,2,1:T(4,128)} %param.7) | data formatting | bytes 1944 | tf_op args[3]
  6.4 0.2 reshape.6.blocks
  6.6 0.0 collective-permute-done.got_b
  6.6 1.2 %collective-permute-done.1.got_a = f32[14,8,128]{2,1,0:T(8,128)S(1)} collective-permute-done((f32[14,8,128]{2,1,0:T(8,128)S(1)}, f32[14,8,128]{2,1,0:T(8,128)S(1)}, u32[]{:S(2)}, u32[]{:S(2)}) %collective-permute-start.1) | collective-permute-done | bytes 57376 | tf_op jit(solution)/shard_map/ppermute | solution.py:635
  7.7 0.1 shard_map.47
  7.9 2.5 %collective-permute-start.4 = (f32[44,8,128]{2,1,0:T(8,128)S(1)}, f32[44,8,128]{2,1,0:T(8,128)S(1)}, u32[]{:S(2)}, u32[]{:S(2)}) collective-permute-start(f32[44,8,128]{2,1,0:T(8,128)S(1)} %shard_map.47), channel_id=1, source_target_pairs={{0,6},{1,7},{2,4},{3,5},{4,2},{5,3},{6,0},{7,1},{8,14},{9,15},{10,... | collective-permute-start | bytes 540680 | tf_op jit(solution)/shard_map/ppermute | solution.py:635
  10.4 0.5 %collective-permute-start.3 = (f32[44,8,128]{2,1,0:T(8,128)S(1)}, f32[44,8,128]{2,1,0:T(8,128)S(1)}, u32[]{:S(2)}, u32[]{:S(2)}) collective-permute-start(f32[44,8,128]{2,1,0:T(8,128)S(1)} %shard_map.47), channel_id=1, source_target_pairs={{0,4},{1,5},{2,6},{3,7},{4,0},{5,1},{6,2},{7,3},{8,12},{9,13},{10,... | collective-permute-start | bytes 540680 | tf_op jit(solution)/shard_map/ppermute | solution.py:635
  10.9 0.5 %collective-permute-start.2 = (f32[44,8,128]{2,1,0:T(8,128)S(1)}, f32[44,8,128]{2,1,0:T(8,128)S(1)}, u32[]{:S(2)}, u32[]{:S(2)}) collective-permute-start(f32[44,8,128]{2,1,0:T(8,128)S(1)} %shard_map.47), channel_id=1, source_target_pairs={{0,2},{1,3},{2,0},{3,1},{4,6},{5,7},{6,4},{7,5},{8,10},{9,11},{10,... | collective-permute-start | bytes 540680 | tf_op jit(solution)/shard_map/ppermute | solution.py:635
  11.4 2.4 %shard_map.48 = (bf16[144,512]{1,0:T(8,128)(2,1)S(1)}, bf16[72,512]{1,0:T(8,128)(2,1)S(1)}, bf16[432,256]{1,0:T(8,128)(2,1)S(1)}, bf16[72,256]{1,0:T(8,128)(2,1)...) custom-call(f32[243]{0:T(256)S(1)} %reshape.6.blocks), custom_call_target="tpu_custom_call" | custom-call | flops 5000000000 | bytes 8000000 | tf_op jit(solution)/shard_map/pallas_call | solution.py:27
  13.8 0.1 collective-permute-start.5
  13.9 2.2 %collective-permute-done.4 = f32[44,8,128]{2,1,0:T(8,128)S(1)} collective-permute-done((f32[44,8,128]{2,1,0:T(8,128)S(1)}, f32[44,8,128]{2,1,0:T(8,128)S(1)}, u32[]{:S(2)}, u32[]{:S(2)}) %collective-permute-start.4) | collective-permute-done | bytes 180256 | tf_op jit(solution)/shard_map/ppermute | solution.py:635
  16.1 1.7 %collective-permute-done.3 = f32[44,8,128]{2,1,0:T(8,128)S(1)} collective-permute-done((f32[44,8,128]{2,1,0:T(8,128)S(1)}, f32[44,8,128]{2,1,0:T(8,128)S(1)}, u32[]{:S(2)}, u32[]{:S(2)}) %collective-permute-start.3) | collective-permute-done | bytes 180256 | tf_op jit(solution)/shard_map/ppermute | solution.py:635
  17.8 0.0 collective-permute-start.7
  17.8 0.1 collective-permute-done.2
  17.9 0.4 %collective-permute-start.6 = (f32[44,8,128]{2,1,0:T(8,128)S(1)}, f32[44,8,128]{2,1,0:T(8,128)S(1)}, u32[]{:S(2)}, u32[]{:S(2)}) collective-permute-start(f32[44,8,128]{2,1,0:T(8,128)S(1)} %collective-permute-done.2), channel_id=1, source_target_pairs={{0,1},{1,0},{2,3},{3,2},{4,5},{5,4},{6,7},{7,6},{8,9},{9,8},{10,11... | collective-permute-start | bytes 540680 | tf_op jit(solution)/shard_map/ppermute | solution.py:635
  18.3 0.1 collective-permute-start.8
  18.4 0.0 collective-permute-done.5
  18.4 0.8 %collective-permute-done.7 = f32[44,8,128]{2,1,0:T(8,128)S(1)} collective-permute-done((f32[44,8,128]{2,1,0:T(8,128)S(1)}, f32[44,8,128]{2,1,0:T(8,128)S(1)}, u32[]{:S(2)}, u32[]{:S(2)}) %collective-permute-start.7) | collective-permute-done | bytes 180256 | tf_op jit(solution)/shard_map/ppermute | solution.py:635
  19.2 0.3 collective-permute-done.6
  19.5 0.3 collective-permute-done.8
  19.8 2.4 %shard_map.49 = (f32[22,3,16,256]{3,2,1,0:T(8,128)S(1)}, f32[22,16,256]{2,1,0:T(8,128)S(1)}, f32[22,16,256]{2,1,0:T(8,128)S(1)}, f32[22,3,16,256]{3,2,1,0:T(8,12...) custom-call(f32[243]{0:T(256)S(1)} %reshape.6.blocks, ...), custom_call_target="tpu_custom_call" | custom-call | flops 1000000 | bytes 100000 | tf_op jit(solution)/shard_map/pallas_call | solution.py:27
  22.1 1.9 %collective-permute-start.9 = (f32[3,8,128]{2,1,0:T(8,128)S(1)}, f32[3,8,128]{2,1,0:T(8,128)S(1)}, u32[]{:S(2)}, u32[]{:S(2)}) collective-permute-start(f32[3,8,128]{2,1,0:T(8,128)S(1)} %get-tuple-element.45.bounds_a), channel_id=1, source_target_pairs={{0,17},{1,16},{2,19},{3,18},{4,21},{5,20},{6,23},{7,22},{8,25},{9,... | collective-permute-start | bytes 36872 | tf_op jit(solution)/shard_map/ppermute | solution.py:635
  24.0 2.7 %shard_map.50 = (f32[22,3,16,256]{3,2,1,0:T(8,128)S(1)}, f32[4,192,128]{2,1,0:T(8,128)S(1)}) custom-call(f32[22,16,256]{2,1,0:T(8,128)S(1)} %get-tuple-element.47.scale_w, f32[22,16,256]{2,1,0:T(8,128)S(1)} %get-tuple-element.48.mass_w, f32[22,3,16,256]{3,2,1,0:T(8,128)S(1)} %get-tuple-element.49.inverse_w, ...), custom_call_target="tpu_custom_call" | custom-call | flops 3000000000 | bytes 12000000 | tf_op jit(solution)/shard_map/pallas_call | solution.py:27
  26.7 0.0 collective-permute-done.9.bounds_b
  26.7 5.6 %shard_map.51 = f32[3,4,8,128]{3,2,1,0:T(8,128)} custom-call(f32[3,8,128]{2,1,0:T(8,128)S(1)} %get-tuple-element.45.bounds_a, f32[3,8,128]{2,1,0:T(8,128)S(1)} %collective-permute-done.9.bounds_b, f32[22,3,16,256]{3,2,1,0:T(8,128)S(1)} %get-tuple-element.46.source_w, f32[22,16,256]{2,1,0:T(8,128)S(1)} %get-tuple-element.47.scale_w, ...), custom_call_target="tpu_custom_call" | custom-call | flops 1000000 | bytes 100000 | tf_op jit(solution)/shard_map/pallas_call | solution.py:27
Async XLA Ops:
  0.9 5.6 %collective-permute-start = (f32[14,8,128]{2,1,0:T(8,128)S(1)}, f32[14,8,128]{2,1,0:T(8,128)S(1)}, u32[]{:S(2)}, u32[]{:S(2)}) collective-permute-start(f32[14,8,128]{2,1,0:T(8,128)S(1)} %get-tuple-element.35), channel_id=1, source_target_pairs={{0,1},{1,0},{2,3},{3,2},{4,5},{5,4},{6,7},{7,6},{8,16},{9,17},{10,... | collective-permute-start | bytes 172040 | tf_op jit(solution)/shard_map/ppermute | solution.py:635
  1.4 6.3 %collective-permute-start.1 = (f32[14,8,128]{2,1,0:T(8,128)S(1)}, f32[14,8,128]{2,1,0:T(8,128)S(1)}, u32[]{:S(2)}, u32[]{:S(2)}) collective-permute-start(f32[14,8,128]{2,1,0:T(8,128)S(1)} %get-tuple-element.36), channel_id=1, source_target_pairs={{0,8},{1,9},{2,10},{3,11},{4,12},{5,13},{6,14},{7,15},{8,0},{9,1},... | collective-permute-start | bytes 172040 | tf_op jit(solution)/shard_map/ppermute | solution.py:635
  7.9 8.2 %collective-permute-start.4 = (f32[44,8,128]{2,1,0:T(8,128)S(1)}, f32[44,8,128]{2,1,0:T(8,128)S(1)}, u32[]{:S(2)}, u32[]{:S(2)}) collective-permute-start(f32[44,8,128]{2,1,0:T(8,128)S(1)} %shard_map.47), channel_id=1, source_target_pairs={{0,6},{1,7},{2,4},{3,5},{4,2},{5,3},{6,0},{7,1},{8,14},{9,15},{10,... | collective-permute-start | bytes 540680 | tf_op jit(solution)/shard_map/ppermute | solution.py:635
  10.4 7.5 %collective-permute-start.3 = (f32[44,8,128]{2,1,0:T(8,128)S(1)}, f32[44,8,128]{2,1,0:T(8,128)S(1)}, u32[]{:S(2)}, u32[]{:S(2)}) collective-permute-start(f32[44,8,128]{2,1,0:T(8,128)S(1)} %shard_map.47), channel_id=1, source_target_pairs={{0,4},{1,5},{2,6},{3,7},{4,0},{5,1},{6,2},{7,3},{8,12},{9,13},{10,... | collective-permute-start | bytes 540680 | tf_op jit(solution)/shard_map/ppermute | solution.py:635
  10.9 7.0 %collective-permute-start.2 = (f32[44,8,128]{2,1,0:T(8,128)S(1)}, f32[44,8,128]{2,1,0:T(8,128)S(1)}, u32[]{:S(2)}, u32[]{:S(2)}) collective-permute-start(f32[44,8,128]{2,1,0:T(8,128)S(1)} %shard_map.47), channel_id=1, source_target_pairs={{0,2},{1,3},{2,0},{3,1},{4,6},{5,7},{6,4},{7,5},{8,10},{9,11},{10,... | collective-permute-start | bytes 540680 | tf_op jit(solution)/shard_map/ppermute | solution.py:635
  13.8 4.6 %collective-permute-start.5 = (f32[44,8,128]{2,1,0:T(8,128)S(1)}, f32[44,8,128]{2,1,0:T(8,128)S(1)}, u32[]{:S(2)}, u32[]{:S(2)}) collective-permute-start(f32[44,8,128]{2,1,0:T(8,128)S(1)} %shard_map.47), channel_id=1, source_target_pairs={{0,1},{1,0},{2,3},{3,2},{4,5},{5,4},{6,7},{7,6},{8,9},{9,8},{10,11... | collective-permute-start | bytes 540680 | tf_op jit(solution)/shard_map/ppermute | solution.py:635
  17.8 1.4 %collective-permute-start.7 = (f32[44,8,128]{2,1,0:T(8,128)S(1)}, f32[44,8,128]{2,1,0:T(8,128)S(1)}, u32[]{:S(2)}, u32[]{:S(2)}) collective-permute-start(f32[44,8,128]{2,1,0:T(8,128)S(1)} %collective-permute-done.3), channel_id=1, source_target_pairs={{0,1},{1,0},{2,3},{3,2},{4,5},{5,4},{6,7},{7,6},{8,9},{9,8},{10,11... | collective-permute-start | bytes 540680 | tf_op jit(solution)/shard_map/ppermute | solution.py:635
  17.9 1.6 %collective-permute-start.6 = (f32[44,8,128]{2,1,0:T(8,128)S(1)}, f32[44,8,128]{2,1,0:T(8,128)S(1)}, u32[]{:S(2)}, u32[]{:S(2)}) collective-permute-start(f32[44,8,128]{2,1,0:T(8,128)S(1)} %collective-permute-done.2), channel_id=1, source_target_pairs={{0,1},{1,0},{2,3},{3,2},{4,5},{5,4},{6,7},{7,6},{8,9},{9,8},{10,11... | collective-permute-start | bytes 540680 | tf_op jit(solution)/shard_map/ppermute | solution.py:635
  18.3 1.4 %collective-permute-start.8 = (f32[44,8,128]{2,1,0:T(8,128)S(1)}, f32[44,8,128]{2,1,0:T(8,128)S(1)}, u32[]{:S(2)}, u32[]{:S(2)}) collective-permute-start(f32[44,8,128]{2,1,0:T(8,128)S(1)} %collective-permute-done.4), channel_id=1, source_target_pairs={{0,1},{1,0},{2,3},{3,2},{4,5},{5,4},{6,7},{7,6},{8,9},{9,8},{10,11... | collective-permute-start | bytes 540680 | tf_op jit(solution)/shard_map/ppermute | solution.py:635
  22.1 4.6 %collective-permute-start.9 = (f32[3,8,128]{2,1,0:T(8,128)S(1)}, f32[3,8,128]{2,1,0:T(8,128)S(1)}, u32[]{:S(2)}, u32[]{:S(2)}) collective-permute-start(f32[3,8,128]{2,1,0:T(8,128)S(1)} %get-tuple-element.45.bounds_a), channel_id=1, source_target_pairs={{0,17},{1,16},{2,19},{3,18},{4,21},{5,20},{6,23},{7,22},{8,25},{9,... | collective-permute-start | bytes 36872 | tf_op jit(solution)/shard_map/ppermute | solution.py:635

commit v8 on v7

--- a/solution.py
+++ b/solution.py
@@ -16,6 +16,7 @@
 SM = pl.BlockSpec(memory_space=pltpu.SMEM)
 LANES = 256
 LINE = 384
+FREE, PIECES = 52, (0, 25, 79, 104)
 PAD = 3
 
 
@@ -289,9 +290,17 @@
     below = jnp.where(index > 0, jnp.where(even, second, first), 0.0)
     low = iota((10, 8, 128), 2) < 64
     wide[:20] = main[...]
-    wide[20:30] = jnp.where(low, above, below)
-    wide[30:40] = jnp.where(low, pltpu.roll(above, 64, 2), pltpu.roll(below, 64, 2))
-    wide[40:] = jnp.where(even, pltpu.roll(more, 64, 2), more)
+    halo = jnp.concatenate(
+        [jnp.where(low, above, below), jnp.where(low, pltpu.roll(above, 64, 2), pltpu.roll(below, 64, 2))], axis=0
+    )
+    lane = iota((8, 128), 1)
+    free = jnp.logical_and(lane >= FREE, lane < FREE + 25)
+    for guest in range(2):
+        for piece, start in enumerate(PIECES):
+            moved = pltpu.roll(halo[8 + guest], (FREE - start) % 128, 1)
+            wide[20 + guest * 4 + piece] = jnp.where(free, moved, halo[guest * 4 + piece])
+    wide[28:38] = halo[10:]
+    wide[38:] = jnp.where(even, pltpu.roll(more, 64, 2), more)
 
 
 def inverse_diagonal(scale, mass, blocks, factor):
@@ -361,6 +370,7 @@
     gz, gy = lax.axis_index("gz"), lax.axis_index("gy")
     even = lax.rem(lax.axis_index("gx"), 2) == 0
     low = iota((4, 8, 128), 2) < 64
+    lane = iota((8, 128), 1)
     for at in (0, planes + 1):
         scale_x[at] = jnp.zeros((rows, LINE), F32)
     for ref in (source_w, inverse_w, scale_w, mass_w):
@@ -375,21 +385,27 @@
                 place_y = lax.bitwise_xor(gy, number % 4 // 2)
             at_z = pl.ds(PAD + 4 * place_z, 4)
             at_y = pl.ds(pl.multiple_of(8 * place_y, 8), 8)
-            for half in (0, 1):
-                lanes = slice(half * 128, half * 128 + 128)
-                part = ref.at[block, half * 20 : half * 20 + 20]
-                for comp in range(3):
-                    source_w[at_z, comp, at_y, lanes] = part[comp * 4 : comp * 4 + 4]
-                scale_w[at_z, at_y, lanes] = part[12:16]
-                mass_w[at_z, at_y, lanes] = part[16:20]
-            here, more = ref.at[block], ref[block, 40:44]
+            here, more = ref.at[block], ref[block, 38:42]
+            for comp in range(3):
+                source_w[at_z, comp, at_y, :128] = here[comp * 4 : comp * 4 + 4]
+            for comp in range(2):
+                source_w[at_z, comp, at_y, 128:] = here[20 + comp * 4 : 24 + comp * 4]
+            source_w[pl.ds(PAD + 4 * place_z + 2, 2), 2, at_y, 128:] = here[28:30]
+            for guest in range(2):
+                found = here[20 + guest * 4]
+                for piece, start in enumerate(PIECES):
+                    back = pltpu.roll(here[20 + guest * 4 + piece], (start - FREE) % 128, 1)
+                    found = jnp.where(lane >= (0, 25, 64, 104)[piece], back, found)
+                source_w[PAD + 4 * place_z + guest, 2, at_y, 128:] = found
+            scale_w[at_z, at_y, :128], scale_w[at_z, at_y, 128:] = here[12:16], here[30:34]
+            mass_w[at_z, at_y, :128], mass_w[at_z, at_y, 128:] = here[16:20], here[34:38]
             turned_more = pltpu.roll(more, 64, 2)
             for target, own, start, at_low, at_high in (
                 (scale_x, 12, 1, more, turned_more),
                 (mass_x, 16, 0, turned_more, more),
             ):
                 at_x = pl.ds(start + 4 * place_z, 4)
-                halo = here[own + 20 : own + 24]
+                halo = here[own + 18 : own + 22]
                 target[at_x, at_y, :128] = here[own : own + 4]
                 target[at_x, at_y, 128:256] = jnp.where(low, halo, jnp.where(even, at_high, 0.0))
                 target[at_x, at_y, 256:] = jnp.where(low, jnp.where(even, 0.0, at_low), halo)
@@ -675,7 +691,7 @@
     send_a, send_b = call(pack_kernel, [half, half], grant=8)(main)
     got_b = send(send_b, x_second)
     got_a = send(send_a, lambda x, y, z: (x ^ 1, y, z))
-    (wide,) = call(functools.partial(widen_kernel, gxs), [((44, 8, 128), F32)], grant=8)(main, got_b, got_a)
+    (wide,) = call(functools.partial(widen_kernel, gxs), [((42, 8, 128), F32)], grant=8)(main, got_b, got_a)
     ordered = not (gys == 2 and gzs == 4)
     if ordered:
         gathered = [lax.all_gather(wide, ("gz", "gy"), tiled=False)]

time: 32.6 us -> 32.2 us (0.988)
  waiting for transfers between devices: 6.53 us -> 6.17 us
    ppermute x10, waiting for transfers between devices: 6.53 us -> 6.17 us  [send(): return lax.ppermute(values, AXES, swap_pairs(counts, target))]
where the time goes in v8:
time: 32.2 us; the launch traced here: 31.9 us
  Pallas kernels  13.2 us (41%)
  starting transfers between devices  10.7 us (33%)
  waiting for transfers between devices  6.17 us (19%)
  local copies, waits for them, and re-layouts  0.97 us (3%)
  other arithmetic  0.84 us (3%)
    pallas_call x6, Pallas kernels, run(): pl.pallas_call(kernel, out_shape=outs, in_specs=specs or [VM] * len(args)...  13.2 us
    ppermute x10, starting transfers between devices, send(): return lax.ppermute(values, AXES, swap_pairs(counts, target))  10.7 us
    ppermute x10, waiting for transfers between devices, send(): return lax.ppermute(values, AXES, swap_pairs(counts, target))  6.17 us
    concatenate x1, other arithmetic, on_device(): jnp.concatenate([right_side.reshape(12, 8, 128), stiff_scale, nodal_mass]...  0.84 us
    unnamed x1, local copies, waits for them, and re-layouts  0.8 us
  transfers between devices with their start and end apart: 10, of which 7 were waited for; matrix products, arithmetic and copies ran while one was open for 3% of the time, Pallas kernels for 16%

profile of v8, /device:TPU:0, one launch (start us, length us, event | category | flops | bytes accessed | tf_op | source)
XLA Modules:
  0.0 31.9 jit_solution(1319195104321471264)
XLA Ops:
  0.0 0.8 %pad_maximum_fusion.main = f32[20,8,128]{2,1,0:T(8,128)S(1)} fusion(f32[4,8,128]{2,1,0:T(8,128)} %param.6, f32[4,8,128]{2,1,0:T(8,128)} %param.5, f32[12,8,128]{2,1,0:T(8,128)} %bitcast.17), kind=kLoop, calls=%fused_computation | loop fusion | flops 40960 | bytes 163840 | tf_op jit(solution)/shard_map/concatenate | solution.py:690
  0.8 0.1 shard_map.46
  0.9 0.5 %collective-permute-start = (f32[14,8,128]{2,1,0:T(8,128)S(1)}, f32[14,8,128]{2,1,0:T(8,128)S(1)}, u32[]{:S(2)}, u32[]{:S(2)}) collective-permute-start(f32[14,8,128]{2,1,0:T(8,128)S(1)} %get-tuple-element.35), channel_id=1, source_target_pairs={{0,1},{1,0},{2,3},{3,2},{4,5},{5,4},{6,7},{7,6},{8,16},{9,17},{10,... | collective-permute-start | bytes 172040 | tf_op jit(solution)/shard_map/ppermute | solution.py:651
  1.4 4.1 %collective-permute-start.1 = (f32[14,8,128]{2,1,0:T(8,128)S(1)}, f32[14,8,128]{2,1,0:T(8,128)S(1)}, u32[]{:S(2)}, u32[]{:S(2)}) collective-permute-start(f32[14,8,128]{2,1,0:T(8,128)S(1)} %get-tuple-element.36), channel_id=1, source_target_pairs={{0,8},{1,9},{2,10},{3,11},{4,12},{5,13},{6,14},{7,15},{8,0},{9,1},... | collective-permute-start | bytes 172040 | tf_op jit(solution)/shard_map/ppermute | solution.py:651
  5.6 0.8 %copy.5 = f32[27,3,3]{2,1,0:T(4,128)S(1)} copy(f32[27,3,3]{0,2,1:T(4,128)} %param.7) | data formatting | bytes 1944 | tf_op args[3]
  6.4 0.2 reshape.6.blocks
  6.6 0.0 collective-permute-done.got_b
  6.6 1.2 %collective-permute-done.1.got_a = f32[14,8,128]{2,1,0:T(8,128)S(1)} collective-permute-done((f32[14,8,128]{2,1,0:T(8,128)S(1)}, f32[14,8,128]{2,1,0:T(8,128)S(1)}, u32[]{:S(2)}, u32[]{:S(2)}) %collective-permute-start.1) | collective-permute-done | bytes 57376 | tf_op jit(solution)/shard_map/ppermute | solution.py:651
  7.7 0.1 shard_map.47
  7.9 2.5 %collective-permute-start.4 = (f32[42,8,128]{2,1,0:T(8,128)S(1)}, f32[42,8,128]{2,1,0:T(8,128)S(1)}, u32[]{:S(2)}, u32[]{:S(2)}) collective-permute-start(f32[42,8,128]{2,1,0:T(8,128)S(1)} %shard_map.47), channel_id=1, source_target_pairs={{0,6},{1,7},{2,4},{3,5},{4,2},{5,3},{6,0},{7,1},{8,14},{9,15},{10,... | collective-permute-start | bytes 516104 | tf_op jit(solution)/shard_map/ppermute | solution.py:651
  10.4 0.5 %collective-permute-start.3 = (f32[42,8,128]{2,1,0:T(8,128)S(1)}, f32[42,8,128]{2,1,0:T(8,128)S(1)}, u32[]{:S(2)}, u32[]{:S(2)}) collective-permute-start(f32[42,8,128]{2,1,0:T(8,128)S(1)} %shard_map.47), channel_id=1, source_target_pairs={{0,4},{1,5},{2,6},{3,7},{4,0},{5,1},{6,2},{7,3},{8,12},{9,13},{10,... | collective-permute-start | bytes 516104 | tf_op jit(solution)/shard_map/ppermute | solution.py:651
  10.9 0.5 %collective-permute-start.2 = (f32[42,8,128]{2,1,0:T(8,128)S(1)}, f32[42,8,128]{2,1,0:T(8,128)S(1)}, u32[]{:S(2)}, u32[]{:S(2)}) collective-permute-start(f32[42,8,128]{2,1,0:T(8,128)S(1)} %shard_map.47), channel_id=1, source_target_pairs={{0,2},{1,3},{2,0},{3,1},{4,6},{5,7},{6,4},{7,5},{8,10},{9,11},{10,... | collective-permute-start | bytes 516104 | tf_op jit(solution)/shard_map/ppermute | solution.py:651
  11.4 2.4 %shard_map.48 = (bf16[144,512]{1,0:T(8,128)(2,1)S(1)}, bf16[72,512]{1,0:T(8,128)(2,1)S(1)}, bf16[432,256]{1,0:T(8,128)(2,1)S(1)}, bf16[72,256]{1,0:T(8,128)(2,1)...) custom-call(f32[243]{0:T(256)S(1)} %reshape.6.blocks), custom_call_target="tpu_custom_call" | custom-call | flops 5000000000 | bytes 8000000 | tf_op jit(solution)/shard_map/pallas_call | solution.py:28
  13.8 0.1 collective-permute-start.5
  13.9 2.0 %collective-permute-done.4 = f32[42,8,128]{2,1,0:T(8,128)S(1)} collective-permute-done((f32[42,8,128]{2,1,0:T(8,128)S(1)}, f32[42,8,128]{2,1,0:T(8,128)S(1)}, u32[]{:S(2)}, u32[]{:S(2)}) %collective-permute-start.4) | collective-permute-done | bytes 172064 | tf_op jit(solution)/shard_map/ppermute | solution.py:651
  15.9 1.6 %collective-permute-done.3 = f32[42,8,128]{2,1,0:T(8,128)S(1)} collective-permute-done((f32[42,8,128]{2,1,0:T(8,128)S(1)}, f32[42,8,128]{2,1,0:T(8,128)S(1)}, u32[]{:S(2)}, u32[]{:S(2)}) %collective-permute-start.3) | collective-permute-done | bytes 172064 | tf_op jit(solution)/shard_map/ppermute | solution.py:651
  17.5 0.0 collective-permute-start.7
  17.5 0.1 collective-permute-done.2
  17.5 0.4 %collective-permute-start.6 = (f32[42,8,128]{2,1,0:T(8,128)S(1)}, f32[42,8,128]{2,1,0:T(8,128)S(1)}, u32[]{:S(2)}, u32[]{:S(2)}) collective-permute-start(f32[42,8,128]{2,1,0:T(8,128)S(1)} %collective-permute-done.2), channel_id=1, source_target_pairs={{0,1},{1,0},{2,3},{3,2},{4,5},{5,4},{6,7},{7,6},{8,9},{9,8},{10,11... | collective-permute-start | bytes 516104 | tf_op jit(solution)/shard_map/ppermute | solution.py:651
  18.0 0.1 collective-permute-start.8
  18.1 0.0 collective-permute-done.5
  18.1 0.8 %collective-permute-done.7 = f32[42,8,128]{2,1,0:T(8,128)S(1)} collective-permute-done((f32[42,8,128]{2,1,0:T(8,128)S(1)}, f32[42,8,128]{2,1,0:T(8,128)S(1)}, u32[]{:S(2)}, u32[]{:S(2)}) %collective-permute-start.7) | collective-permute-done | bytes 172064 | tf_op jit(solution)/shard_map/ppermute | solution.py:651
  18.9 0.2 collective-permute-done.6
  19.1 0.3 collective-permute-done.8
  19.4 2.3 %shard_map.49 = (f32[22,3,16,256]{3,2,1,0:T(8,128)S(1)}, f32[22,16,256]{2,1,0:T(8,128)S(1)}, f32[22,16,256]{2,1,0:T(8,128)S(1)}, f32[22,3,16,256]{3,2,1,0:T(8,12...) custom-call(f32[243]{0:T(256)S(1)} %reshape.6.blocks, ...), custom_call_target="tpu_custom_call" | custom-call | flops 1000000 | bytes 100000 | tf_op jit(solution)/shard_map/pallas_call | solution.py:28
  21.7 1.9 %collective-permute-start.9 = (f32[3,8,128]{2,1,0:T(8,128)S(1)}, f32[3,8,128]{2,1,0:T(8,128)S(1)}, u32[]{:S(2)}, u32[]{:S(2)}) collective-permute-start(f32[3,8,128]{2,1,0:T(8,128)S(1)} %get-tuple-element.45.bounds_a), channel_id=1, source_target_pairs={{0,17},{1,16},{2,19},{3,18},{4,21},{5,20},{6,23},{7,22},{8,25},{9,... | collective-permute-start | bytes 36872 | tf_op jit(solution)/shard_map/ppermute | solution.py:651
  23.6 2.7 %shard_map.50 = (f32[22,3,16,256]{3,2,1,0:T(8,128)S(1)}, f32[4,192,128]{2,1,0:T(8,128)S(1)}) custom-call(f32[22,16,256]{2,1,0:T(8,128)S(1)} %get-tuple-element.47.scale_w, f32[22,16,256]{2,1,0:T(8,128)S(1)} %get-tuple-element.48.mass_w, f32[22,3,16,256]{3,2,1,0:T(8,128)S(1)} %get-tuple-element.49.inverse_w, ...), custom_call_target="tpu_custom_call" | custom-call | flops 3000000000 | bytes 12000000 | tf_op jit(solution)/shard_map/pallas_call | solution.py:28
  26.3 0.0 collective-permute-done.9.bounds_b
  26.3 5.6 %shard_map.51 = f32[3,4,8,128]{3,2,1,0:T(8,128)} custom-call(f32[3,8,128]{2,1,0:T(8,128)S(1)} %get-tuple-element.45.bounds_a, f32[3,8,128]{2,1,0:T(8,128)S(1)} %collective-permute-done.9.bounds_b, f32[22,3,16,256]{3,2,1,0:T(8,128)S(1)} %get-tuple-element.46.source_w, f32[22,16,256]{2,1,0:T(8,128)S(1)} %get-tuple-element.47.scale_w, ...), custom_call_target="tpu_custom_call" | custom-call | flops 1000000 | bytes 100000 | tf_op jit(solution)/shard_map/pallas_call | solution.py:28
Async XLA Ops:
  0.9 5.6 %collective-permute-start = (f32[14,8,128]{2,1,0:T(8,128)S(1)}, f32[14,8,128]{2,1,0:T(8,128)S(1)}, u32[]{:S(2)}, u32[]{:S(2)}) collective-permute-start(f32[14,8,128]{2,1,0:T(8,128)S(1)} %get-tuple-element.35), channel_id=1, source_target_pairs={{0,1},{1,0},{2,3},{3,2},{4,5},{5,4},{6,7},{7,6},{8,16},{9,17},{10,... | collective-permute-start | bytes 172040 | tf_op jit(solution)/shard_map/ppermute | solution.py:651
  1.4 6.3 %collective-permute-start.1 = (f32[14,8,128]{2,1,0:T(8,128)S(1)}, f32[14,8,128]{2,1,0:T(8,128)S(1)}, u32[]{:S(2)}, u32[]{:S(2)}) collective-permute-start(f32[14,8,128]{2,1,0:T(8,128)S(1)} %get-tuple-element.36), channel_id=1, source_target_pairs={{0,8},{1,9},{2,10},{3,11},{4,12},{5,13},{6,14},{7,15},{8,0},{9,1},... | collective-permute-start | bytes 172040 | tf_op jit(solution)/shard_map/ppermute | solution.py:651
  7.9 8.0 %collective-permute-start.4 = (f32[42,8,128]{2,1,0:T(8,128)S(1)}, f32[42,8,128]{2,1,0:T(8,128)S(1)}, u32[]{:S(2)}, u32[]{:S(2)}) collective-permute-start(f32[42,8,128]{2,1,0:T(8,128)S(1)} %shard_map.47), channel_id=1, source_target_pairs={{0,6},{1,7},{2,4},{3,5},{4,2},{5,3},{6,0},{7,1},{8,14},{9,15},{10,... | collective-permute-start | bytes 516104 | tf_op jit(solution)/shard_map/ppermute | solution.py:651
  10.4 7.1 %collective-permute-start.3 = (f32[42,8,128]{2,1,0:T(8,128)S(1)}, f32[42,8,128]{2,1,0:T(8,128)S(1)}, u32[]{:S(2)}, u32[]{:S(2)}) collective-permute-start(f32[42,8,128]{2,1,0:T(8,128)S(1)} %shard_map.47), channel_id=1, source_target_pairs={{0,4},{1,5},{2,6},{3,7},{4,0},{5,1},{6,2},{7,3},{8,12},{9,13},{10,... | collective-permute-start | bytes 516104 | tf_op jit(solution)/shard_map/ppermute | solution.py:651
  10.9 6.7 %collective-permute-start.2 = (f32[42,8,128]{2,1,0:T(8,128)S(1)}, f32[42,8,128]{2,1,0:T(8,128)S(1)}, u32[]{:S(2)}, u32[]{:S(2)}) collective-permute-start(f32[42,8,128]{2,1,0:T(8,128)S(1)} %shard_map.47), channel_id=1, source_target_pairs={{0,2},{1,3},{2,0},{3,1},{4,6},{5,7},{6,4},{7,5},{8,10},{9,11},{10,... | collective-permute-start | bytes 516104 | tf_op jit(solution)/shard_map/ppermute | solution.py:651
  13.8 4.2 %collective-permute-start.5 = (f32[42,8,128]{2,1,0:T(8,128)S(1)}, f32[42,8,128]{2,1,0:T(8,128)S(1)}, u32[]{:S(2)}, u32[]{:S(2)}) collective-permute-start(f32[42,8,128]{2,1,0:T(8,128)S(1)} %shard_map.47), channel_id=1, source_target_pairs={{0,1},{1,0},{2,3},{3,2},{4,5},{5,4},{6,7},{7,6},{8,9},{9,8},{10,11... | collective-permute-start | bytes 516104 | tf_op jit(solution)/shard_map/ppermute | solution.py:651
  17.5 1.4 %collective-permute-start.7 = (f32[42,8,128]{2,1,0:T(8,128)S(1)}, f32[42,8,128]{2,1,0:T(8,128)S(1)}, u32[]{:S(2)}, u32[]{:S(2)}) collective-permute-start(f32[42,8,128]{2,1,0:T(8,128)S(1)} %collective-permute-done.3), channel_id=1, source_target_pairs={{0,1},{1,0},{2,3},{3,2},{4,5},{5,4},{6,7},{7,6},{8,9},{9,8},{10,11... | collective-permute-start | bytes 516104 | tf_op jit(solution)/shard_map/ppermute | solution.py:651
  17.5 1.6 %collective-permute-start.6 = (f32[42,8,128]{2,1,0:T(8,128)S(1)}, f32[42,8,128]{2,1,0:T(8,128)S(1)}, u32[]{:S(2)}, u32[]{:S(2)}) collective-permute-start(f32[42,8,128]{2,1,0:T(8,128)S(1)} %collective-permute-done.2), channel_id=1, source_target_pairs={{0,1},{1,0},{2,3},{3,2},{4,5},{5,4},{6,7},{7,6},{8,9},{9,8},{10,11... | collective-permute-start | bytes 516104 | tf_op jit(solution)/shard_map/ppermute | solution.py:651
  18.0 1.4 %collective-permute-start.8 = (f32[42,8,128]{2,1,0:T(8,128)S(1)}, f32[42,8,128]{2,1,0:T(8,128)S(1)}, u32[]{:S(2)}, u32[]{:S(2)}) collective-permute-start(f32[42,8,128]{2,1,0:T(8,128)S(1)} %collective-permute-done.4), channel_id=1, source_target_pairs={{0,1},{1,0},{2,3},{3,2},{4,5},{5,4},{6,7},{7,6},{8,9},{9,8},{10,11... | collective-permute-start | bytes 516104 | tf_op jit(solution)/shard_map/ppermute | solution.py:651
  21.7 4.5 %collective-permute-start.9 = (f32[3,8,128]{2,1,0:T(8,128)S(1)}, f32[3,8,128]{2,1,0:T(8,128)S(1)}, u32[]{:S(2)}, u32[]{:S(2)}) collective-permute-start(f32[3,8,128]{2,1,0:T(8,128)S(1)} %get-tuple-element.45.bounds_a), channel_id=1, source_target_pairs={{0,17},{1,16},{2,19},{3,18},{4,21},{5,20},{6,23},{7,22},{8,25},{9,... | collective-permute-start | bytes 36872 | tf_op jit(solution)/shard_map/ppermute | solution.py:651

commit v9 on v8

--- a/solution.py
+++ b/solution.py
@@ -75,8 +75,12 @@
     edge = jnp.zeros((slab, lanes), F32)
     padded = jnp.concatenate([edge, values, edge], axis=0)
     beside = jnp.concatenate([padded[at * slab : (at + 3) * slab] for at in range(planes)], axis=1)
-    high = beside.astype(BF16).astype(F32)
-    stacked = jnp.concatenate([high, high, beside - high], axis=0).astype(BF16)
+    if slab % 16 == 0:
+        high, low = split(beside)
+        stacked = jnp.concatenate([high, high, low], axis=0)
+    else:
+        high = beside.astype(BF16).astype(F32)
+        stacked = jnp.concatenate([high, high, beside - high], axis=0).astype(BF16)
     product = dot(matrix[:, : 9 * slab], stacked)
     outs = []
     for at in range(planes):

time: 32.2 us -> 32.2 us (level)
  no operation moved by 1% of the time
where the time goes in v9:
time: 32.2 us; the launch traced here: 31.9 us
  Pallas kernels  13.2 us (41%)
  starting transfers between devices  10.7 us (33%)
  waiting for transfers between devices  6.17 us (19%)
  local copies, waits for them, and re-layouts  0.97 us (3%)
  other arithmetic  0.84 us (3%)
    pallas_call x6, Pallas kernels, run(): pl.pallas_call(kernel, out_shape=outs, in_specs=specs or [VM] * len(args)...  13.2 us
    ppermute x10, starting transfers between devices, send(): return lax.ppermute(values, AXES, swap_pairs(counts, target))  10.7 us
    ppermute x10, waiting for transfers between devices, send(): return lax.ppermute(values, AXES, swap_pairs(counts, target))  6.17 us
    concatenate x1, other arithmetic, on_device(): jnp.concatenate([right_side.reshape(12, 8, 128), stiff_scale, nodal_mass]...  0.84 us
    unnamed x1, local copies, waits for them, and re-layouts  0.8 us
  transfers between devices with their start and end apart: 10, of which 7 were waited for; matrix products, arithmetic and copies ran while one was open for 3% of the time, Pallas kernels for 16%

profile of v9, /device:TPU:0, one launch (start us, length us, event | category | flops | bytes accessed | tf_op | source)
XLA Modules:
  0.0 31.9 jit_solution(1319195104321471264)
XLA Ops:
  0.0 0.8 %pad_maximum_fusion.main = f32[20,8,128]{2,1,0:T(8,128)S(1)} fusion(f32[4,8,128]{2,1,0:T(8,128)} %param.6, f32[4,8,128]{2,1,0:T(8,128)} %param.5, f32[12,8,128]{2,1,0:T(8,128)} %bitcast.17), kind=kLoop, calls=%fused_computation | loop fusion | flops 40960 | bytes 163840 | tf_op jit(solution)/shard_map/concatenate | solution.py:694
  0.8 0.1 shard_map.46
  0.9 0.5 %collective-permute-start = (f32[14,8,128]{2,1,0:T(8,128)S(1)}, f32[14,8,128]{2,1,0:T(8,128)S(1)}, u32[]{:S(2)}, u32[]{:S(2)}) collective-permute-start(f32[14,8,128]{2,1,0:T(8,128)S(1)} %get-tuple-element.35), channel_id=1, source_target_pairs={{0,1},{1,0},{2,3},{3,2},{4,5},{5,4},{6,7},{7,6},{8,16},{9,17},{10,... | collective-permute-start | bytes 172040 | tf_op jit(solution)/shard_map/ppermute | solution.py:655
  1.4 4.1 %collective-permute-start.1 = (f32[14,8,128]{2,1,0:T(8,128)S(1)}, f32[14,8,128]{2,1,0:T(8,128)S(1)}, u32[]{:S(2)}, u32[]{:S(2)}) collective-permute-start(f32[14,8,128]{2,1,0:T(8,128)S(1)} %get-tuple-element.36), channel_id=1, source_target_pairs={{0,8},{1,9},{2,10},{3,11},{4,12},{5,13},{6,14},{7,15},{8,0},{9,1},... | collective-permute-start | bytes 172040 | tf_op jit(solution)/shard_map/ppermute | solution.py:655
  5.6 0.8 %copy.5 = f32[27,3,3]{2,1,0:T(4,128)S(1)} copy(f32[27,3,3]{0,2,1:T(4,128)} %param.7) | data formatting | bytes 1944 | tf_op args[3]
  6.4 0.2 reshape.6.blocks
  6.6 0.0 collective-permute-done.got_b
  6.6 1.2 %collective-permute-done.1.got_a = f32[14,8,128]{2,1,0:T(8,128)S(1)} collective-permute-done((f32[14,8,128]{2,1,0:T(8,128)S(1)}, f32[14,8,128]{2,1,0:T(8,128)S(1)}, u32[]{:S(2)}, u32[]{:S(2)}) %collective-permute-start.1) | collective-permute-done | bytes 57376 | tf_op jit(solution)/shard_map/ppermute | solution.py:655
  7.7 0.1 shard_map.47
  7.9 2.5 %collective-permute-start.4 = (f32[42,8,128]{2,1,0:T(8,128)S(1)}, f32[42,8,128]{2,1,0:T(8,128)S(1)}, u32[]{:S(2)}, u32[]{:S(2)}) collective-permute-start(f32[42,8,128]{2,1,0:T(8,128)S(1)} %shard_map.47), channel_id=1, source_target_pairs={{0,6},{1,7},{2,4},{3,5},{4,2},{5,3},{6,0},{7,1},{8,14},{9,15},{10,... | collective-permute-start | bytes 516104 | tf_op jit(solution)/shard_map/ppermute | solution.py:655
  10.4 0.5 %collective-permute-start.3 = (f32[42,8,128]{2,1,0:T(8,128)S(1)}, f32[42,8,128]{2,1,0:T(8,128)S(1)}, u32[]{:S(2)}, u32[]{:S(2)}) collective-permute-start(f32[42,8,128]{2,1,0:T(8,128)S(1)} %shard_map.47), channel_id=1, source_target_pairs={{0,4},{1,5},{2,6},{3,7},{4,0},{5,1},{6,2},{7,3},{8,12},{9,13},{10,... | collective-permute-start | bytes 516104 | tf_op jit(solution)/shard_map/ppermute | solution.py:655
  10.9 0.5 %collective-permute-start.2 = (f32[42,8,128]{2,1,0:T(8,128)S(1)}, f32[42,8,128]{2,1,0:T(8,128)S(1)}, u32[]{:S(2)}, u32[]{:S(2)}) collective-permute-start(f32[42,8,128]{2,1,0:T(8,128)S(1)} %shard_map.47), channel_id=1, source_target_pairs={{0,2},{1,3},{2,0},{3,1},{4,6},{5,7},{6,4},{7,5},{8,10},{9,11},{10,... | collective-permute-start | bytes 516104 | tf_op jit(solution)/shard_map/ppermute | solution.py:655
  11.4 2.4 %shard_map.48 = (bf16[144,512]{1,0:T(8,128)(2,1)S(1)}, bf16[72,512]{1,0:T(8,128)(2,1)S(1)}, bf16[432,256]{1,0:T(8,128)(2,1)S(1)}, bf16[72,256]{1,0:T(8,128)(2,1)...) custom-call(f32[243]{0:T(256)S(1)} %reshape.6.blocks), custom_call_target="tpu_custom_call" | custom-call | flops 5000000000 | bytes 8000000 | tf_op jit(solution)/shard_map/pallas_call | solution.py:28
  13.8 0.1 collective-permute-start.5
  13.9 2.0 %collective-permute-done.4 = f32[42,8,128]{2,1,0:T(8,128)S(1)} collective-permute-done((f32[42,8,128]{2,1,0:T(8,128)S(1)}, f32[42,8,128]{2,1,0:T(8,128)S(1)}, u32[]{:S(2)}, u32[]{:S(2)}) %collective-permute-start.4) | collective-permute-done | bytes 172064 | tf_op jit(solution)/shard_map/ppermute | solution.py:655
  15.9 1.6 %collective-permute-done.3 = f32[42,8,128]{2,1,0:T(8,128)S(1)} collective-permute-done((f32[42,8,128]{2,1,0:T(8,128)S(1)}, f32[42,8,128]{2,1,0:T(8,128)S(1)}, u32[]{:S(2)}, u32[]{:S(2)}) %collective-permute-start.3) | collective-permute-done | bytes 172064 | tf_op jit(solution)/shard_map/ppermute | solution.py:655
  17.5 0.0 collective-permute-start.7
  17.5 0.1 collective-permute-done.2
  17.5 0.4 %collective-permute-start.6 = (f32[42,8,128]{2,1,0:T(8,128)S(1)}, f32[42,8,128]{2,1,0:T(8,128)S(1)}, u32[]{:S(2)}, u32[]{:S(2)}) collective-permute-start(f32[42,8,128]{2,1,0:T(8,128)S(1)} %collective-permute-done.2), channel_id=1, source_target_pairs={{0,1},{1,0},{2,3},{3,2},{4,5},{5,4},{6,7},{7,6},{8,9},{9,8},{10,11... | collective-permute-start | bytes 516104 | tf_op jit(solution)/shard_map/ppermute | solution.py:655
  18.0 0.1 collective-permute-start.8
  18.1 0.0 collective-permute-done.5
  18.1 0.8 %collective-permute-done.7 = f32[42,8,128]{2,1,0:T(8,128)S(1)} collective-permute-done((f32[42,8,128]{2,1,0:T(8,128)S(1)}, f32[42,8,128]{2,1,0:T(8,128)S(1)}, u32[]{:S(2)}, u32[]{:S(2)}) %collective-permute-start.7) | collective-permute-done | bytes 172064 | tf_op jit(solution)/shard_map/ppermute | solution.py:655
  18.9 0.2 collective-permute-done.6
  19.1 0.3 collective-permute-done.8
  19.4 2.3 %shard_map.49 = (f32[22,3,16,256]{3,2,1,0:T(8,128)S(1)}, f32[22,16,256]{2,1,0:T(8,128)S(1)}, f32[22,16,256]{2,1,0:T(8,128)S(1)}, f32[22,3,16,256]{3,2,1,0:T(8,12...) custom-call(f32[243]{0:T(256)S(1)} %reshape.6.blocks, ...), custom_call_target="tpu_custom_call" | custom-call | flops 1000000 | bytes 100000 | tf_op jit(solution)/shard_map/pallas_call | solution.py:28
  21.7 1.9 %collective-permute-start.9 = (f32[3,8,128]{2,1,0:T(8,128)S(1)}, f32[3,8,128]{2,1,0:T(8,128)S(1)}, u32[]{:S(2)}, u32[]{:S(2)}) collective-permute-start(f32[3,8,128]{2,1,0:T(8,128)S(1)} %get-tuple-element.45.bounds_a), channel_id=1, source_target_pairs={{0,17},{1,16},{2,19},{3,18},{4,21},{5,20},{6,23},{7,22},{8,25},{9,... | collective-permute-start | bytes 36872 | tf_op jit(solution)/shard_map/ppermute | solution.py:655
  23.6 2.7 %shard_map.50 = (f32[22,3,16,256]{3,2,1,0:T(8,128)S(1)}, f32[4,192,128]{2,1,0:T(8,128)S(1)}) custom-call(f32[22,16,256]{2,1,0:T(8,128)S(1)} %get-tuple-element.47.scale_w, f32[22,16,256]{2,1,0:T(8,128)S(1)} %get-tuple-element.48.mass_w, f32[22,3,16,256]{3,2,1,0:T(8,128)S(1)} %get-tuple-element.49.inverse_w, ...), custom_call_target="tpu_custom_call" | custom-call | flops 3000000000 | bytes 12000000 | tf_op jit(solution)/shard_map/pallas_call | solution.py:28
  26.3 0.0 collective-permute-done.9.bounds_b
  26.3 5.6 %shard_map.51 = f32[3,4,8,128]{3,2,1,0:T(8,128)} custom-call(f32[3,8,128]{2,1,0:T(8,128)S(1)} %get-tuple-element.45.bounds_a, f32[3,8,128]{2,1,0:T(8,128)S(1)} %collective-permute-done.9.bounds_b, f32[22,3,16,256]{3,2,1,0:T(8,128)S(1)} %get-tuple-element.46.source_w, f32[22,16,256]{2,1,0:T(8,128)S(1)} %get-tuple-element.47.scale_w, ...), custom_call_target="tpu_custom_call" | custom-call | flops 1000000 | bytes 100000 | tf_op jit(solution)/shard_map/pallas_call | solution.py:28
Async XLA Ops:
  0.9 5.6 %collective-permute-start = (f32[14,8,128]{2,1,0:T(8,128)S(1)}, f32[14,8,128]{2,1,0:T(8,128)S(1)}, u32[]{:S(2)}, u32[]{:S(2)}) collective-permute-start(f32[14,8,128]{2,1,0:T(8,128)S(1)} %get-tuple-element.35), channel_id=1, source_target_pairs={{0,1},{1,0},{2,3},{3,2},{4,5},{5,4},{6,7},{7,6},{8,16},{9,17},{10,... | collective-permute-start | bytes 172040 | tf_op jit(solution)/shard_map/ppermute | solution.py:655
  1.4 6.3 %collective-permute-start.1 = (f32[14,8,128]{2,1,0:T(8,128)S(1)}, f32[14,8,128]{2,1,0:T(8,128)S(1)}, u32[]{:S(2)}, u32[]{:S(2)}) collective-permute-start(f32[14,8,128]{2,1,0:T(8,128)S(1)} %get-tuple-element.36), channel_id=1, source_target_pairs={{0,8},{1,9},{2,10},{3,11},{4,12},{5,13},{6,14},{7,15},{8,0},{9,1},... | collective-permute-start | bytes 172040 | tf_op jit(solution)/shard_map/ppermute | solution.py:655
  7.9 8.0 %collective-permute-start.4 = (f32[42,8,128]{2,1,0:T(8,128)S(1)}, f32[42,8,128]{2,1,0:T(8,128)S(1)}, u32[]{:S(2)}, u32[]{:S(2)}) collective-permute-start(f32[42,8,128]{2,1,0:T(8,128)S(1)} %shard_map.47), channel_id=1, source_target_pairs={{0,6},{1,7},{2,4},{3,5},{4,2},{5,3},{6,0},{7,1},{8,14},{9,15},{10,... | collective-permute-start | bytes 516104 | tf_op jit(solution)/shard_map/ppermute | solution.py:655
  10.4 7.1 %collective-permute-start.3 = (f32[42,8,128]{2,1,0:T(8,128)S(1)}, f32[42,8,128]{2,1,0:T(8,128)S(1)}, u32[]{:S(2)}, u32[]{:S(2)}) collective-permute-start(f32[42,8,128]{2,1,0:T(8,128)S(1)} %shard_map.47), channel_id=1, source_target_pairs={{0,4},{1,5},{2,6},{3,7},{4,0},{5,1},{6,2},{7,3},{8,12},{9,13},{10,... | collective-permute-start | bytes 516104 | tf_op jit(solution)/shard_map/ppermute | solution.py:655
  10.9 6.7 %collective-permute-start.2 = (f32[42,8,128]{2,1,0:T(8,128)S(1)}, f32[42,8,128]{2,1,0:T(8,128)S(1)}, u32[]{:S(2)}, u32[]{:S(2)}) collective-permute-start(f32[42,8,128]{2,1,0:T(8,128)S(1)} %shard_map.47), channel_id=1, source_target_pairs={{0,2},{1,3},{2,0},{3,1},{4,6},{5,7},{6,4},{7,5},{8,10},{9,11},{10,... | collective-permute-start | bytes 516104 | tf_op jit(solution)/shard_map/ppermute | solution.py:655
  13.8 4.2 %collective-permute-start.5 = (f32[42,8,128]{2,1,0:T(8,128)S(1)}, f32[42,8,128]{2,1,0:T(8,128)S(1)}, u32[]{:S(2)}, u32[]{:S(2)}) collective-permute-start(f32[42,8,128]{2,1,0:T(8,128)S(1)} %shard_map.47), channel_id=1, source_target_pairs={{0,1},{1,0},{2,3},{3,2},{4,5},{5,4},{6,7},{7,6},{8,9},{9,8},{10,11... | collective-permute-start | bytes 516104 | tf_op jit(solution)/shard_map/ppermute | solution.py:655
  17.5 1.4 %collective-permute-start.7 = (f32[42,8,128]{2,1,0:T(8,128)S(1)}, f32[42,8,128]{2,1,0:T(8,128)S(1)}, u32[]{:S(2)}, u32[]{:S(2)}) collective-permute-start(f32[42,8,128]{2,1,0:T(8,128)S(1)} %collective-permute-done.3), channel_id=1, source_target_pairs={{0,1},{1,0},{2,3},{3,2},{4,5},{5,4},{6,7},{7,6},{8,9},{9,8},{10,11... | collective-permute-start | bytes 516104 | tf_op jit(solution)/shard_map/ppermute | solution.py:655
  17.5 1.6 %collective-permute-start.6 = (f32[42,8,128]{2,1,0:T(8,128)S(1)}, f32[42,8,128]{2,1,0:T(8,128)S(1)}, u32[]{:S(2)}, u32[]{:S(2)}) collective-permute-start(f32[42,8,128]{2,1,0:T(8,128)S(1)} %collective-permute-done.2), channel_id=1, source_target_pairs={{0,1},{1,0},{2,3},{3,2},{4,5},{5,4},{6,7},{7,6},{8,9},{9,8},{10,11... | collective-permute-start | bytes 516104 | tf_op jit(solution)/shard_map/ppermute | solution.py:655
  18.0 1.4 %collective-permute-start.8 = (f32[42,8,128]{2,1,0:T(8,128)S(1)}, f32[42,8,128]{2,1,0:T(8,128)S(1)}, u32[]{:S(2)}, u32[]{:S(2)}) collective-permute-start(f32[42,8,128]{2,1,0:T(8,128)S(1)} %collective-permute-done.4), channel_id=1, source_target_pairs={{0,1},{1,0},{2,3},{3,2},{4,5},{5,4},{6,7},{7,6},{8,9},{9,8},{10,11... | collective-permute-start | bytes 516104 | tf_op jit(solution)/shard_map/ppermute | solution.py:655
  21.7 4.5 %collective-permute-start.9 = (f32[3,8,128]{2,1,0:T(8,128)S(1)}, f32[3,8,128]{2,1,0:T(8,128)S(1)}, u32[]{:S(2)}, u32[]{:S(2)}) collective-permute-start(f32[3,8,128]{2,1,0:T(8,128)S(1)} %get-tuple-element.45.bounds_a), channel_id=1, source_target_pairs={{0,17},{1,16},{2,19},{3,18},{4,21},{5,20},{6,23},{7,22},{8,25},{9,... | collective-permute-start | bytes 36872 | tf_op jit(solution)/shard_map/ppermute | solution.py:655
